TPU v7x, 32 devices: a whole 2x2x4 slice. The times are simulated.
32 devices in a mesh: replica: 2 (over x), fsdp: 16 (over z, y, core).
Axes of the slice: x: 2, y: 2, z: 4, core: 2. Of those that a mesh axis runs over, the one named last changes fastest.
Arguments:
- master: float32 [2, 8192, 512], P('replica', 'fsdp'), may hold values from -0.0625 to 0.0625
- momentum: float32 [2, 8192, 512], P('replica', 'fsdp'), may hold values from -0.03125 to 0.03125
- working: bfloat16 [2, 8192, 512], P('replica', 'fsdp'), may hold values from -0.0625 to 0.0625
- tokens: bfloat16 [2, 3072, 8192], P('replica', 'fsdp'), may hold values from -6 to 6
- partners: int32 [2, 4], replicated, may hold values from 0 to 1, as said below
- mix_weights: int32 [2, 5], replicated, may hold values from 1 to 3
Outputs:
- new_master: float32 [2, 8192, 512], P('replica', 'fsdp')
- new_momentum: float32 [2, 8192, 512], P('replica', 'fsdp')
- keys: bfloat16 [2, 3072, 512], P('replica', 'fsdp')
Inputs may be any that keep to these rules, and one draw needn't show every extreme that they name: partners[g, 0] is a perfect matching of the groups (never g itself, and symmetric); partners[g, 1..3] are any groups, g itself included, repeats allowed.
All inputs are finite; a program needn't handle non-finite values.
Results may differ from a plain program's by a relative error of at most 0.0049.
Values may be sent and summed in bfloat16 or wider, within the bound.
No kernel may reach another device: no remote copies, remote signals or barrier semaphores. Data moves between devices by JAX's collectives and lax.ppermute only.
A program may use at most 64 MiB of HBM per device.

v0:
```python
import jax
import jax.numpy as jnp
from jax import lax
from jax.sharding import PartitionSpec as P

outer_rate = 0.7
momentum_decay = 0.9


def shards(master, momentum, working, tokens, partners, mix_weights):
    groups = lax.axis_size("replica")
    own_group = lax.axis_index("replica")
    group_ids = jnp.arange(groups, dtype=jnp.int32)
    weights_f = mix_weights.astype(jnp.float32)
    total = jnp.sum(weights_f[own_group])
    delta = master - working.astype(jnp.float32)
    own_partners = partners[own_group]
    own_weights = weights_f[own_group]
    row_coef = own_weights[0] * (group_ids == own_group).astype(jnp.float32)
    for slot in range(4):
        row_coef = row_coef + own_weights[slot + 1] * (group_ids == own_partners[slot]).astype(
            jnp.float32
        )
    summed = jnp.sum(
        row_coef[:, None, None] * lax.all_gather(delta, "replica", axis=0, tiled=True),
        axis=0,
        keepdims=True,
    )
    mixed = summed / total
    new_momentum = momentum_decay * momentum + mixed
    new_master = master - outer_rate * (mixed + momentum_decay * new_momentum)
    fresh = new_master.astype(jnp.bfloat16)
    inputs = tokens[0]
    summed_keys = jnp.dot(
        inputs,
        lax.all_gather(fresh, "fsdp", axis=1, tiled=True)[0],
        preferred_element_type=jnp.float32,
    )
    keys = summed_keys.astype(jnp.bfloat16)[None]
    return (new_master, new_momentum, keys)


def solution(mesh):
    return jax.shard_map(
        shards,
        mesh=mesh,
        in_specs=(
            P("replica", "fsdp", None),
            P("replica", "fsdp", None),
            P("replica", "fsdp", None),
            P("replica", "fsdp", None),
            P(),
            P(),
        ),
        out_specs=(
            P("replica", "fsdp", None),
            P("replica", "fsdp", None),
            P("replica", "fsdp", None),
        ),
        check_vma=False,
    )
```

profile of v0, /device:TPU:0, one launch (start us, length us, event | category | flops | bytes accessed | tf_op | source)
XLA Modules:
  0.0 138.6 jit_solution(16320607994123544726)
XLA Ops:
  7.2 0.0 copy-start
  7.2 0.0 copy-start.3
  7.2 0.0 copy-start.4
  7.2 0.0 all-gather.3.cloned.1.call-start
  7.2 2.6 %convert_subtract_fusion = f32[1,512,512]{2,1,0:T(8,128)} fusion(f32[1,512,512]{2,1,0:T(8,128)} %param.6, bf16[1,512,512]{2,1,0:T(8,128)(2,1)} %param.8), kind=kLoop, calls=%fused_computation.10 | loop fusion | flops 524288 | bytes 2621440 | tf_op jit(solution)/shard_map/sub | solution.py:16
  9.9 0.0 all-gather.3.cloned.1.call-update
  9.9 0.0 all-gather.5.cloned.1.call-start
  10.0 0.0 copy-done.3
  10.0 0.0 copy-done.4
  10.0 0.6 fusion.21
  10.6 0.6 fusion.23
  11.2 0.7 fusion.22
  11.9 5.6 %fusion.18 = f32[2]{0:T(128)S(1)} fusion(f32[]{:T(128)} %bitcast.8, s32[]{:T(128)} %bitcast.7, f32[]{:T(128)} %bitcast.6, s32[]{:T(128)} %bitcast.5, f32[]{:T(128)} %bitcast.4, s32[]{:T(128)} %bitcast.3, f32[]{:T(128)} %bitcast.2, s32[]{:T(128)} %bitcast.1, f32[]{:T(128)} %bitcast, s32[]{:T(128)S(6)} %axis_index.15), kind=kLoop, calls=%fused_computation.20 | loop fusion | flops 28 | bytes 48 | tf_op jit(solution)/shard_map/add | solution.py:21
  17.5 28.5 %all-gather.3.cloned.1.call-done = f32[2,512,512]{2,1,0:T(8,128)} async-done(((f32[1,512,512]{2,1,0:T(8,128)}), f32[2,512,512]{2,1,0:T(8,128)}) %all-gather.3.cloned.1.call-update) | async-done | bytes 2097168 | tf_op jit(solution)/shard_map/all_gather | solution.py:25
  46.0 0.0 copy-start.1
  46.0 0.0 copy-start.2
  46.0 2.2 %multiply_reduce_fusion = f32[512,512]{1,0:T(8,128)S(1)} fusion(f32[2,512,512]{2,1,0:T(8,128)} %all-gather.3.cloned.1.call-done, f32[2]{0:T(128)S(1)} %fusion.18), kind=kLoop, calls=%fused_computation.3 | loop fusion | flops 786432 | bytes 3145736 | tf_op jit(solution)/shard_map/reduce_sum | solution.py:24
  48.2 0.0 copy-done.1
  48.2 0.0 copy-done.2
  48.2 2.6 %fusion.19 = (bf16[1,512,512]{2,1,0:T(8,128)(2,1)}, f32[1,512,512]{2,1,0:T(8,128)}, f32[1,512,512]{2,1,0:T(8,128)}) fusion(f32[1,512,512]{2,1,0:T(8,128)S(1)} %copy-done.1, f32[512,512]{1,0:T(8,128)S(1)} %multiply_reduce_fusion, f32[]{:T(128)} %get-tuple-element.6, f32[1,512,512]{2,1,0:T(8,128)S(1)} %copy-done.2), kind=kLoop, calls=%fused_computation.23 | loop fusion | flops 2097152 | bytes 5767172 | tf_op jit(solution)/shard_map/convert_element_type | solution.py:32
  50.8 0.0 all-gather.5.cloned.1.call-update
  50.8 75.1 %all-gather.5.cloned.1.call-done = bf16[1,8192,512]{2,1,0:T(8,128)(2,1)} async-done(((bf16[1,512,512]{2,1,0:T(8,128)(2,1)}), bf16[1,8192,512]{2,1,0:T(8,128)(2,1)}) %all-gather.5.cloned.1.call-update) | async-done | bytes 8388624 | tf_op jit(solution)/shard_map/all_gather | solution.py:36
  125.9 0.0 copy-done
  125.9 5.8 %fusion.8 = bf16[1,192,512]{2,1,0:T(8,128)(2,1)} fusion(bf16[1,8192,512]{2,1,0:T(8,128)(2,1)} %all-gather.5.cloned.1.call-done, bf16[1,192,8192]{2,1,0:T(8,128)(2,1)S(1)} %copy-done), kind=kOutput, calls=%fused_computation.5 | convolution fusion | flops 1610711040 | bytes 11730944 | tf_op jit(solution)/shard_map/dot_general | solution.py:34
  (2 shorter events, 0.0 us)
Async XLA Ops:
  7.2 118.7 %copy-start = (bf16[1,192,8192]{2,1,0:T(8,128)(2,1)S(1)}, bf16[1,192,8192]{2,1,0:T(8,128)(2,1)}, u32[]{:S(2)}) copy-start(bf16[1,192,8192]{2,1,0:T(8,128)(2,1)} %param.9) | copy-start | bytes 9437188
  7.2 2.8 %copy-start.3 = (s32[2,5]{1,0:T(2,128)S(1)}, s32[2,5]{1,0:T(2,128)}, u32[]{:S(2)}) copy-start(s32[2,5]{1,0:T(2,128)} %param.11) | copy-start | bytes 124
  7.2 2.8 %copy-start.4 = (s32[2,4]{1,0:T(2,128)S(1)}, s32[2,4]{1,0:T(2,128)}, u32[]{:S(2)}) copy-start(s32[2,4]{1,0:T(2,128)} %param.10) | copy-start | bytes 100
  7.2 38.8 %all-gather.3.cloned.1.call-start = ((), (), s32[]{:S(2)}) async-start(), calls=%async_computation | async-start | bytes 3145728 | tf_op jit(solution)/shard_map/all_gather | solution.py:25
  9.9 116.0 %all-gather.5.cloned.1.call-start = ((), (), s32[]{:S(2)}) async-start(), calls=%async_computation.1 | async-start | bytes 8912896 | tf_op jit(solution)/shard_map/all_gather | solution.py:36
  46.0 2.2 %copy-start.1 = (f32[1,512,512]{2,1,0:T(8,128)S(1)}, f32[1,512,512]{2,1,0:T(8,128)}, u32[]{:S(2)}) copy-start(f32[1,512,512]{2,1,0:T(8,128)} %param.6) | copy-start | bytes 3145732
  46.0 2.2 %copy-start.2 = (f32[1,512,512]{2,1,0:T(8,128)S(1)}, f32[1,512,512]{2,1,0:T(8,128)}, u32[]{:S(2)}) copy-start(f32[1,512,512]{2,1,0:T(8,128)} %param.7) | copy-start | bytes 3145732
Sparse Core Ops, SparseCore 0:
  10.2 35.7 all-gather.2
  51.0 74.8 all-gather.4
where the time goes:
time: 139 us
  waiting for transfers between devices  104 us (75%)
  between operations  14.1 us (10%)
  other arithmetic  13.6 us (10%)
  matrix products  5.85 us (4%)
    all_gather x1, waiting for transfers between devices, shards(): lax.all_gather(fresh, 'fsdp', axis=1, tiled=True)[0]  75.1 us
    all_gather x1, waiting for transfers between devices, shards(): lax.all_gather(delta, 'replica', axis=0, tiled=True)  28.5 us
    dot_general x1, matrix products, shards(): jnp.dot(inputs, lax.all_gather(fresh, 'fsdp', axis=1, tiled=True)[0], pre...  5.85 us
    add x1, other arithmetic, shards(): row_coef + own_weights[slot + 1] * (group_ids == own_partners[slot]).asty...  5.58 us
  transfers between devices with their start and end apart: 2, of which 2 were waited for; matrix products, arithmetic and copies ran while one was open for 5% of the time, Pallas kernels for 0%

commit v1 on v0

v1 whole, which is shorter than its diff:
```python
import jax
import jax.numpy as jnp
from jax import lax
from jax.experimental import pallas as pl
from jax.experimental.pallas import tpu as pltpu
from jax.sharding import PartitionSpec as P

outer_rate = 0.7
momentum_decay = 0.9
PLANE = 4
CHUNKS = 2


def plane_pairs(size, bit):
    return [(i, i ^ bit) for i in range(size)]


def line_pairs(size, to):
    return [(i, to[i // PLANE] * PLANE + i % PLANE) for i in range(size)]


def arrange_body(order, *refs):
    for source, target in zip(refs[:PLANE], refs[PLANE:]):
        target[...] = source[...]


def arrange_tokens(tokens, order, width):
    rows, blocks = tokens.shape[0], order.shape[0] // PLANE

    def column(distance):
        return lambda k, order: (0, order[k * PLANE + distance])

    return pl.pallas_call(
        arrange_body,
        grid_spec=pltpu.PrefetchScalarGridSpec(
            num_scalar_prefetch=1,
            grid=(blocks,),
            in_specs=[pl.BlockSpec((rows, width), column(d)) for d in range(PLANE)],
            out_specs=[pl.BlockSpec((rows, width), lambda k, order: (0, k))] * PLANE,
        ),
        out_shape=[jax.ShapeDtypeStruct((rows, blocks * width), tokens.dtype)] * PLANE,
        name="arrange_tokens",
    )(order, *([tokens] * PLANE))


def product(tokens, weights):
    return jnp.dot(tokens, weights, preferred_element_type=jnp.float32)


def shards(master, momentum, working, tokens, partners, mix_weights):
    groups = lax.axis_size("replica")
    size = lax.axis_size("fsdp")
    line = size // PLANE
    own_group = lax.axis_index("replica")
    place = lax.axis_index("fsdp")
    master, momentum, working, tokens = master[0], momentum[0], working[0], tokens[0]
    rows = master.shape[0]
    chunks = CHUNKS if rows % (CHUNKS * 16) == 0 else 1
    step = rows // chunks
    cut = [slice(i * step, (i + 1) * step) for i in range(chunks)]

    group_ids = jnp.arange(groups, dtype=jnp.int32)
    weights_f = mix_weights.astype(jnp.float32)
    own_partners = partners[own_group]
    own_weights = weights_f[own_group]
    total = jnp.sum(own_weights)
    row_coef = own_weights[0] * (group_ids == own_group).astype(jnp.float32)
    for slot in range(4):
        row_coef = row_coef + own_weights[slot + 1] * (group_ids == own_partners[slot]).astype(
            jnp.float32
        )
    row_coef = row_coef / total

    def others(s):
        delta = (master[s] - working[s].astype(jnp.float32)).astype(jnp.bfloat16)
        if groups == 2:
            return [lax.ppermute(delta, "replica", [(0, 1), (1, 0)])]
        every = lax.all_gather(delta, "replica", axis=0)
        return [every[g] for g in range(groups)]

    def update(master, momentum, working, received):
        delta = master - working.astype(jnp.float32)
        mixed = row_coef[own_group] * delta
        if groups == 2:
            mixed = mixed + row_coef[1 - own_group] * received[0].astype(jnp.float32)
        else:
            for g in range(groups):
                coef = jnp.where(own_group == g, 0.0, row_coef[g])
                mixed = mixed + coef * received[g].astype(jnp.float32)
        new_momentum = momentum_decay * momentum + mixed
        new_master = master - outer_rate * (mixed + momentum_decay * new_momentum)
        return new_master, new_momentum

    received = [others(s) for s in cut]

    if line == 4:
        order = [0, 1, 3, 2]
        order = jnp.stack([place ^ (k * PLANE + d) for k in order for d in range(PLANE)])
    else:
        order = jnp.stack([((place % PLANE) ^ d) + k * PLANE for k in range(line) for d in range(PLANE)])
    own, for_core, for_y, for_both = arrange_tokens(tokens, order.astype(jnp.int32), rows)
    from_y = lax.ppermute(for_y, "fsdp", plane_pairs(size, 2))
    at_core = lax.ppermute(for_both, "fsdp", plane_pairs(size, 1))
    from_core = lax.ppermute(for_core, "fsdp", plane_pairs(size, 1))
    from_both = lax.ppermute(at_core, "fsdp", plane_pairs(size, 2))
    inputs = [own, from_core, from_y, from_both]

    fresh = [
        update(master[s], momentum[s], working[s], r)[0].astype(jnp.bfloat16)
        for s, r in zip(cut, received)
    ]
    if line == 4:
        z = place // PLANE
        middle = (z == 1) | (z == 2)
        near, far, last = [], [], []
        for f in fresh:
            far.append(lax.ppermute(f, "fsdp", line_pairs(size, [3, 2, 1, 0])))
            near.append(lax.ppermute(f, "fsdp", line_pairs(size, [1, 0, 3, 2])))
        for f, g in zip(fresh, far):
            last.append(lax.ppermute(jnp.where(middle, g, f), "fsdp", line_pairs(size, [2, 0, 3, 1])))
        arrivals = [fresh, near, far, last]
    else:
        lines = [[k * PLANE + p for k in range(line)] for p in range(PLANE)]
        every = [lax.all_gather(f, "fsdp", axis=0, axis_index_groups=lines) for f in fresh]
        arrivals = [[e[k] for e in every] for k in range(line)]

    def partial_keys(t):
        return sum(
            product(t[:, k * rows + s.start : k * rows + s.stop], w)
            for k, block in enumerate(arrivals)
            for s, w in zip(cut, block)
        )

    own, from_core, from_y, from_both = [partial_keys(t) for t in inputs]
    back = lax.ppermute(jnp.concatenate([from_core, from_both]), "fsdp", plane_pairs(size, 1))
    count = own.shape[0]
    own = own + back[:count]
    to_y = (from_y + back[count:]).astype(jnp.bfloat16)
    keys = own + lax.ppermute(to_y, "fsdp", plane_pairs(size, 2)).astype(jnp.float32)

    full = [jnp.concatenate(list(r)) for r in zip(*received)]
    new_master, new_momentum = update(master, momentum, working, full)
    return new_master[None], new_momentum[None], keys.astype(jnp.bfloat16)[None]


def solution(mesh):
    return jax.shard_map(
        shards,
        mesh=mesh,
        in_specs=(
            P("replica", "fsdp", None),
            P("replica", "fsdp", None),
            P("replica", "fsdp", None),
            P("replica", "fsdp", None),
            P(),
            P(),
        ),
        out_specs=(
            P("replica", "fsdp", None),
            P("replica", "fsdp", None),
            P("replica", "fsdp", None),
        ),
        check_vma=False,
    )
```

time: 139 us -> 109 us (0.78)
  waiting for transfers between devices: 104 us -> 31.8 us
  starting transfers between devices: 0.08 us -> 31.5 us
  matrix products: 5.85 us -> 22 us
  between operations: 14.1 us -> 0.92 us
  Pallas kernels: 0 us -> 5.23 us
    all_gather x2 -> x0, waiting for transfers between devices: 104 us -> none  [the longest x1 75.1 us: shards(): lax.all_gather(fresh, 'fsdp', axis=1, tiled=True)[0]]
    ppermute x0 -> x14, waiting for transfers between devices: none -> 31.8 us  [the longest x1 13.7 us: shards(): from_both = lax.ppermute(at_core, 'fsdp', plane_pairs(size, 2))]
    ppermute x0 -> x14, starting transfers between devices: none -> 31.5 us  [the longest x2 15.1 us: shards(): near.append(lax.ppermute(f, 'fsdp', line_pairs(size, [1, 0, 3, 2])))]
    dot_general x1 -> x32, matrix products: 5.85 us -> 22 us  [product(): return jnp.dot(tokens, weights, preferred_element_type=jnp.float32)]
    div x0 -> x1, other arithmetic: none -> 6.24 us  [shards(): row_coef = row_coef / total]
    add x1 -> x0, other arithmetic: 5.58 us -> none  [shards(): row_coef + own_weights[slot + 1] * (group_ids == own_partners[slot]).asty...]
    pallas_call x0 -> x1, Pallas kernels: none -> 5.23 us  [arrange_tokens(): pl.pallas_call(arrange_body, grid_spec=pltpu.PrefetchScalarGridSpec(num_s...]
    reduce_sum x2 -> x1, other arithmetic: 2.78 us -> 0.6 us  [shards(): total = jnp.sum(own_weights)]
  transfers between devices with their start and end apart: 2 -> 14, of which waited for: 2 -> 4; matrix products, arithmetic and copies ran while one was open for 5% -> 30% of each run, Pallas kernels for 0% -> 5%
where the time goes in v1:
time: 109 us; the launch traced here: 108 us
  waiting for transfers between devices  31.8 us (29%)
  starting transfers between devices  31.5 us (29%)
  matrix products  22 us (20%)
  other arithmetic  13.8 us (13%)
  Pallas kernels  5.23 us (5%)
  local copies, waits for them, and re-layouts  2.5 us (2%)
    dot_general x32, matrix products, product(): return jnp.dot(tokens, weights, preferred_element_type=jnp.float32)  22 us
    ppermute x2, starting transfers between devices, shards(): near.append(lax.ppermute(f, 'fsdp', line_pairs(size, [1, 0, 3, 2])))  15.1 us
    ppermute x1, waiting for transfers between devices, shards(): from_both = lax.ppermute(at_core, 'fsdp', plane_pairs(size, 2))  13.7 us
    ppermute x2, waiting for transfers between devices, shards(): lax.ppermute(jnp.where(middle, g, f), 'fsdp', line_pairs(size, [2, 0, 3,...  7.65 us
    ppermute x1, waiting for transfers between devices, shards(): lax.ppermute(to_y, 'fsdp', plane_pairs(size, 2)).astype(jnp.float32)  6.59 us
    div x1, other arithmetic, shards(): row_coef = row_coef / total  6.24 us
    ppermute x2, starting transfers between devices, shards(): lax.ppermute(jnp.where(middle, g, f), 'fsdp', line_pairs(size, [2, 0, 3,...  5.76 us
    pallas_call x1, Pallas kernels, arrange_tokens(): pl.pallas_call(arrange_body, grid_spec=pltpu.PrefetchScalarGridSpec(num_s...  5.23 us
  transfers between devices with their start and end apart: 14, of which 4 were waited for; matrix products, arithmetic and copies ran while one was open for 30% of the time, Pallas kernels for 5%

profile of v1, /device:TPU:0, one launch (start us, length us, event | category | flops | bytes accessed | tf_op | source)
XLA Modules:
  0.0 107.7 jit_solution(13105524953728503007)
XLA Ops:
  0.6 0.0 copy-start
  0.6 2.2 %fusion.39 = (bf16[256,512]{1,0:T(8,128)(2,1)}, bf16[256,512]{1,0:T(8,128)(2,1)S(1)}) fusion(f32[1,512,512]{2,1,0:T(8,128)} %param.6, bf16[1,512,512]{2,1,0:T(8,128)(2,1)} %param.8), kind=kLoop, calls=%fused_computation.53 | loop fusion | flops 786432 | bytes 2097152 | tf_op jit(solution)/shard_map/convert_element_type | solution.py:75
  2.9 2.9 %collective-permute-start = (bf16[256,512]{1,0:T(8,128)(2,1)}, bf16[256,512]{1,0:T(8,128)(2,1)S(1)}, u32[]{:S(2)}, u32[]{:S(2)}) collective-permute-start(bf16[256,512]{1,0:T(8,128)(2,1)} %get-tuple-element.17), channel_id=1, source_target_pairs={{0,16},{16,0},{1,17},{17,1},{2,18},{18,2},{3,19},{19,3},{4,20},{20... | collective-permute-start | bytes 786440 | tf_op jit(solution)/shard_map/ppermute | solution.py:77
  5.8 0.0 collective-permute-start.1
  5.8 0.6 stack.67.order
  6.4 5.2 %arrange_tokens.1 = (bf16[192,2048]{1,0:T(8,128)(2,1)}, bf16[192,2048]{1,0:T(8,128)(2,1)}, bf16[192,2048]{1,0:T(8,128)(2,1)}, bf16[192,2048]{1,0:T(8,128)(2,1)}) custom-call(s32[16]{0:T(128)} %stack.67.order, bf16[192,8192]{1,0:T(8,128)(2,1)} %bitcast.110, bf16[192,8192]{1,0:T(8,128)(2,1)} %bitcast.111, bf16[192,8192]{1,0:T(8,128)(2,1)} %bitcast.112, ...), custom_call_target="tpu_custom_call" | custom-call | tf_op jit(solution)/shard_map/arrange_tokens/pallas_call | solution.py:33
  11.7 0.5 collective-permute-start.9
  12.2 2.0 %collective-permute-start.12 = (bf16[192,2048]{1,0:T(8,128)(2,1)}, bf16[192,2048]{1,0:T(8,128)(2,1)}, u32[]{:S(2)}, u32[]{:S(2)}) collective-permute-start(bf16[192,2048]{1,0:T(8,128)(2,1)} %get-tuple-element.10), channel_id=1, source_target_pairs={{0,2},{1,3},{2,0},{3,1},{4,6},{5,7},{6,4},{7,5},{8,10},{9,11},{10,... | collective-permute-start | bytes 2359304 | tf_op jit(solution)/shard_map/ppermute | solution.py:102
  14.2 0.6 fusion.108
  14.8 0.6 fusion.105
  15.4 0.7 fusion.107
  16.1 6.2 %fusion.104 = f32[2]{0:T(128)S(1)} fusion(f32[]{:T(128)} %get-tuple-element.13, f32[]{:T(128)} %bitcast.8, s32[]{:T(128)} %bitcast.7, f32[]{:T(128)} %bitcast.6, s32[]{:T(128)} %bitcast.5, f32[]{:T(128)} %bitcast.4, s32[]{:T(128)} %bitcast.3, f32[]{:T(128)} %bitcast.2, s32[]{:T(128)} %bitcast.1, f32[]{:T(128)} %bitcast, s32[]{:T(128)S(6)} %axis_index.23), kind=kLoop, calls=%fused_computation.125 | loop fusion | flops 30 | bytes 52 | tf_op jit(solution)/shard_map/div | solution.py:72
  22.3 0.6 fusion.106
  23.0 1.7 %fusion.38 = (bf16[256,512]{1,0:T(8,128)(2,1)S(1)}, bf16[256,512]{1,0:T(8,128)(2,1)S(1)}) fusion(f32[1,512,512]{2,1,0:T(8,128)S(1)} %copy-done.3, bf16[256,512]{1,0:T(8,128)(2,1)S(1)} %collective-permute-done, f32[1,512,512]{2,1,0:T(8,128)S(1)} %copy-done.1, f32[]{:T(128)} %bitcast.10, f32[]{:T(128)} %bitcast.9, bf16[1,512,512]{2,1,0:T(8,128)(2,1)S(1)} %copy-done.2, ...), kind=kLoop, calls=%fused_computation.52 | loop fusion | flops 3407872 | bytes 3670024 | tf_op jit(solution)/shard_map/convert_element_type | solution.py:109
  24.6 3.7 %collective-permute-start.4 = (bf16[256,512]{1,0:T(8,128)(2,1)S(1)}, bf16[256,512]{1,0:T(8,128)(2,1)S(1)}, u32[]{:S(2)}, u32[]{:S(2)}) collective-permute-start(bf16[256,512]{1,0:T(8,128)(2,1)S(1)} %get-tuple-element.15), channel_id=1, source_target_pairs={{0,12},{1,13},{2,14},{3,15},{4,8},{5,9},{6,10},{7,11},{8,4},{9,5},... | collective-permute-start | bytes 786440 | tf_op jit(solution)/shard_map/ppermute | solution.py:117
  28.3 0.2 collective-permute-start.5
  28.5 3.0 %multiply_subtract_fusion = (f32[1,512,512]{2,1,0:T(8,128)}, f32[1,512,512]{2,1,0:T(8,128)}) fusion(f32[1,512,512]{2,1,0:T(8,128)S(1)} %copy-done.1, bf16[1,512,512]{2,1,0:T(8,128)(2,1)S(1)} %copy-done.2, f32[]{:T(128)} %bitcast.10, f32[]{:T(128)} %bitcast.9, bf16[1,256,512]{2,1,0:T(8,128)(2,1)S(1)} %bitcast.115, bf16[1,256,512]{2,1,0:T(8,128)(2,1)S(1)} %bitcast.114, ...), kind=kLoop, calls=%fused_computation.34 | loop fusion | flops 3932160 | bytes 5242888 | tf_op jit(solution)/shard_map/sub | solution.py:91
  31.5 0.2 fusion.98
  31.7 0.2 convolution_add_fusion.4
  31.9 3.8 %collective-permute-done.4 = bf16[256,512]{1,0:T(8,128)(2,1)S(1)} collective-permute-done((bf16[256,512]{1,0:T(8,128)(2,1)S(1)}, bf16[256,512]{1,0:T(8,128)(2,1)S(1)}, u32[]{:S(2)}, u32[]{:S(2)}) %collective-permute-start.4) | collective-permute-done | bytes 262176 | tf_op jit(solution)/shard_map/ppermute | solution.py:117
  35.8 10.7 %collective-permute-start.3 = (bf16[256,512]{1,0:T(8,128)(2,1)S(1)}, bf16[256,512]{1,0:T(8,128)(2,1)S(1)}, u32[]{:S(2)}, u32[]{:S(2)}) collective-permute-start(bf16[256,512]{1,0:T(8,128)(2,1)S(1)} %get-tuple-element.16), channel_id=1, source_target_pairs={{0,4},{1,5},{2,6},{3,7},{4,0},{5,1},{6,2},{7,3},{8,12},{9,13},{10,... | collective-permute-start | bytes 786440 | tf_op jit(solution)/shard_map/ppermute | solution.py:118
  46.5 0.2 fusion.92
  46.7 0.0 collective-permute-done.5
  46.7 4.4 %collective-permute-start.2 = (bf16[256,512]{1,0:T(8,128)(2,1)S(1)}, bf16[256,512]{1,0:T(8,128)(2,1)S(1)}, u32[]{:S(2)}, u32[]{:S(2)}) collective-permute-start(bf16[256,512]{1,0:T(8,128)(2,1)S(1)} %get-tuple-element.15), channel_id=1, source_target_pairs={{0,4},{1,5},{2,6},{3,7},{4,0},{5,1},{6,2},{7,3},{8,12},{9,13},{10,... | collective-permute-start | bytes 786440 | tf_op jit(solution)/shard_map/ppermute | solution.py:118
  51.1 0.2 fusion.90
  51.3 0.0 collective-permute-done.3
  51.4 3.1 %collective-permute-start.6 = (bf16[256,512]{1,0:T(8,128)(2,1)S(1)}, bf16[256,512]{1,0:T(8,128)(2,1)S(1)}, u32[]{:S(2)}, u32[]{:S(2)}) collective-permute-start(bf16[256,512]{1,0:T(8,128)(2,1)S(1)} %broadcast_select_fusion.1), channel_id=1, source_target_pairs={{0,8},{1,9},{2,10},{3,11},{4,0},{5,1},{6,2},{7,3},{8,12},{9,13},{1... | collective-permute-start | bytes 786440 | tf_op jit(solution)/shard_map/ppermute | solution.py:120
  54.5 0.2 fusion.94
  54.7 7.6 %collective-permute-done.6 = bf16[256,512]{1,0:T(8,128)(2,1)S(1)} collective-permute-done((bf16[256,512]{1,0:T(8,128)(2,1)S(1)}, bf16[256,512]{1,0:T(8,128)(2,1)S(1)}, u32[]{:S(2)}, u32[]{:S(2)}) %collective-permute-start.6) | collective-permute-done | bytes 262176 | tf_op jit(solution)/shard_map/ppermute | solution.py:120
  62.4 2.6 %collective-permute-start.7 = (bf16[256,512]{1,0:T(8,128)(2,1)S(1)}, bf16[256,512]{1,0:T(8,128)(2,1)S(1)}, u32[]{:S(2)}, u32[]{:S(2)}) collective-permute-start(bf16[256,512]{1,0:T(8,128)(2,1)S(1)} %broadcast_select_fusion), channel_id=1, source_target_pairs={{0,8},{1,9},{2,10},{3,11},{4,0},{5,1},{6,2},{7,3},{8,12},{9,13},{1... | collective-permute-start | bytes 786440 | tf_op jit(solution)/shard_map/ppermute | solution.py:120
  65.0 0.2 fusion.88
  65.2 1.1 %fusion.73 = f32[192,512]{1,0:T(8,128)S(1)} fusion(bf16[256,512]{1,0:T(8,128)(2,1)S(1)} %collective-permute-done.6, bf16[192,2048]{1,0:T(8,128)(2,1)} %collective-permute-done.8), kind=kOutput, calls=%fused_computation.89 | convolution fusion | flops 50331648 | bytes 753664 | tf_op jit(solution)/shard_map/dot_general | solution.py:47
  66.3 1.1 %fusion.75 = f32[192,512]{1,0:T(8,128)S(1)} fusion(bf16[256,512]{1,0:T(8,128)(2,1)S(1)} %collective-permute-done.5, bf16[192,2048]{1,0:T(8,128)(2,1)} %collective-permute-done.8), kind=kOutput, calls=%fused_computation.91 | convolution fusion | flops 50331648 | bytes 753664 | tf_op jit(solution)/shard_map/dot_general | solution.py:47
  67.4 1.1 %fusion.77 = f32[192,512]{1,0:T(8,128)S(1)} fusion(bf16[256,512]{1,0:T(8,128)(2,1)S(1)} %collective-permute-done.4, bf16[192,2048]{1,0:T(8,128)(2,1)} %collective-permute-done.8), kind=kOutput, calls=%fused_computation.93 | convolution fusion | flops 50331648 | bytes 753664 | tf_op jit(solution)/shard_map/dot_general | solution.py:47
  68.5 1.1 %fusion.79 = f32[192,512]{1,0:T(8,128)S(1)} fusion(bf16[256,512]{1,0:T(8,128)(2,1)S(1)} %collective-permute-done.3, bf16[192,2048]{1,0:T(8,128)(2,1)} %collective-permute-done.8), kind=kOutput, calls=%fused_computation.95 | convolution fusion | flops 50331648 | bytes 753664 | tf_op jit(solution)/shard_map/dot_general | solution.py:47
  69.6 1.1 %fusion.83 = f32[192,512]{1,0:T(8,128)S(1)} fusion(bf16[256,512]{1,0:T(8,128)(2,1)S(1)} %get-tuple-element.16, bf16[192,2048]{1,0:T(8,128)(2,1)} %collective-permute-done.8), kind=kOutput, calls=%fused_computation.99 | convolution fusion | flops 50331648 | bytes 753664 | tf_op jit(solution)/shard_map/dot_general | solution.py:47
  70.8 1.1 %fusion.71 = f32[192,512]{1,0:T(8,128)S(1)} fusion(bf16[256,512]{1,0:T(8,128)(2,1)S(1)} %collective-permute-done.7, bf16[192,2048]{1,0:T(8,128)(2,1)} %collective-permute-done.8), kind=kOutput, calls=%fused_computation.87 | convolution fusion | flops 50331648 | bytes 753664 | tf_op jit(solution)/shard_map/dot_general | solution.py:47
  71.8 0.0 collective-permute-done.12
  71.9 1.1 %fusion.43 = f32[192,512]{1,0:T(8,128)S(1)} fusion(bf16[256,512]{1,0:T(8,128)(2,1)S(1)} %collective-permute-done.6, bf16[192,2048]{1,0:T(8,128)(2,1)} %collective-permute-done.12), kind=kOutput, calls=%fused_computation.59 | convolution fusion | flops 50331648 | bytes 753664 | tf_op jit(solution)/shard_map/dot_general | solution.py:47
  73.0 1.1 %fusion.41 = f32[192,512]{1,0:T(8,128)S(1)} fusion(bf16[256,512]{1,0:T(8,128)(2,1)S(1)} %collective-permute-done.7, bf16[192,2048]{1,0:T(8,128)(2,1)} %collective-permute-done.12), kind=kOutput, calls=%fused_computation.57 | convolution fusion | flops 50331648 | bytes 753664 | tf_op jit(solution)/shard_map/dot_general | solution.py:47
  74.1 0.6 collective-permute-start.10
  74.6 1.1 %fusion.45 = f32[192,512]{1,0:T(8,128)S(1)} fusion(bf16[256,512]{1,0:T(8,128)(2,1)S(1)} %collective-permute-done.5, bf16[192,2048]{1,0:T(8,128)(2,1)} %collective-permute-done.12), kind=kOutput, calls=%fused_computation.61 | convolution fusion | flops 50331648 | bytes 753664 | tf_op jit(solution)/shard_map/dot_general | solution.py:47
  75.8 1.1 %fusion.81 = f32[192,512]{1,0:T(8,128)S(1)} fusion(bf16[256,512]{1,0:T(8,128)(2,1)S(1)} %collective-permute-done.2, bf16[192,2048]{1,0:T(8,128)(2,1)} %collective-permute-done.8), kind=kOutput, calls=%fused_computation.97 | convolution fusion | flops 50331648 | bytes 753664 | tf_op jit(solution)/shard_map/dot_general | solution.py:47
  76.9 1.2 %fusion.19 = f32[192,512]{1,0:T(8,128)S(1)} fusion(f32[192,512]{1,0:T(8,128)S(1)} %fusion.71, f32[192,512]{1,0:T(8,128)S(1)} %fusion.73, f32[192,512]{1,0:T(8,128)S(1)} %fusion.75, f32[192,512]{1,0:T(8,128)S(1)} %fusion.77, f32[192,512]{1,0:T(8,128)S(1)} %fusion.79, f32[192,512]{1,0:T(8,128)S(1)} %fusion.81, f32[192,512]{1,0:T(8,128)S(1)} %fusion.83, ...), kind=kOutput, calls=%fused_computation.24 | convolution fusion | flops 51019776 | bytes 3506176 | tf_op jit(solution)/shard_map/dot_general | solution.py:47
  78.1 13.7 %collective-permute-done.10 = bf16[192,2048]{1,0:T(8,128)(2,1)S(1)} collective-permute-done((bf16[192,2048]{1,0:T(8,128)(2,1)}, bf16[192,2048]{1,0:T(8,128)(2,1)S(1)}, u32[]{:S(2)}, u32[]{:S(2)}) %collective-permute-start.10) | collective-permute-done | bytes 786464 | tf_op jit(solution)/shard_map/ppermute | solution.py:105
  91.7 0.2 fusion.58
  91.9 0.2 fusion.56
  92.2 0.2 fusion.60
  92.4 0.2 fusion.62
  92.6 0.2 fusion.64
  92.8 0.2 fusion.66
  93.0 0.2 fusion.68
  93.2 0.3 fusion.14
  93.5 0.1 pad_maximum_fusion
  93.6 0.1 collective-permute-start.11
  93.7 1.1 %fusion.47 = f32[192,512]{1,0:T(8,128)S(1)} fusion(bf16[256,512]{1,0:T(8,128)(2,1)S(1)} %collective-permute-done.4, bf16[192,2048]{1,0:T(8,128)(2,1)} %collective-permute-done.12), kind=kOutput, calls=%fused_computation.63 | convolution fusion | flops 50331648 | bytes 753664 | tf_op jit(solution)/shard_map/dot_general | solution.py:47
  94.8 1.1 %fusion.49 = f32[192,512]{1,0:T(8,128)S(1)} fusion(bf16[256,512]{1,0:T(8,128)(2,1)S(1)} %collective-permute-done.3, bf16[192,2048]{1,0:T(8,128)(2,1)} %collective-permute-done.12), kind=kOutput, calls=%fused_computation.65 | convolution fusion | flops 50331648 | bytes 753664 | tf_op jit(solution)/shard_map/dot_general | solution.py:47
  95.9 1.1 %fusion.51 = f32[192,512]{1,0:T(8,128)S(1)} fusion(bf16[256,512]{1,0:T(8,128)(2,1)S(1)} %collective-permute-done.2, bf16[192,2048]{1,0:T(8,128)(2,1)} %collective-permute-done.12), kind=kOutput, calls=%fused_computation.67 | convolution fusion | flops 50331648 | bytes 753664 | tf_op jit(solution)/shard_map/dot_general | solution.py:47
  97.0 1.1 %fusion.53 = f32[192,512]{1,0:T(8,128)S(1)} fusion(bf16[256,512]{1,0:T(8,128)(2,1)S(1)} %get-tuple-element.16, bf16[192,2048]{1,0:T(8,128)(2,1)} %collective-permute-done.12), kind=kOutput, calls=%fused_computation.69 | convolution fusion | flops 50331648 | bytes 753664 | tf_op jit(solution)/shard_map/dot_general | solution.py:47
  98.1 1.2 %fusion.27 = bf16[192,512]{1,0:T(8,128)(2,1)S(1)} fusion(f32[192,512]{1,0:T(8,128)S(1)} %fusion.41, f32[192,512]{1,0:T(8,128)S(1)} %fusion.43, f32[192,512]{1,0:T(8,128)S(1)} %fusion.45, f32[192,512]{1,0:T(8,128)S(1)} %fusion.47, f32[192,512]{1,0:T(8,128)S(1)} %fusion.49, f32[192,512]{1,0:T(8,128)S(1)} %fusion.51, f32[192,512]{1,0:T(8,128)S(1)} %fusion.53, ...), kind=kOutput, calls=%fused_computation.32 | convolution fusion | flops 51216384 | bytes 3702784 | tf_op jit(solution)/shard_map/dot_general | solution.py:47
  99.3 0.6 collective-permute-start.13
  99.9 0.2 fusion.86
  100.1 6.6 %collective-permute-done.13 = bf16[192,512]{1,0:T(8,128)(2,1)S(1)} collective-permute-done((bf16[192,512]{1,0:T(8,128)(2,1)S(1)}, bf16[192,512]{1,0:T(8,128)(2,1)S(1)}, u32[]{:S(2)}, u32[]{:S(2)}) %collective-permute-start.13) | collective-permute-done | bytes 196640 | tf_op jit(solution)/shard_map/ppermute | solution.py:139
  106.7 1.0 fusion.28
  (23 shorter events, 0.1 us)
Async XLA Ops:
  0.6 13.6 %copy-start = (s32[2,4]{1,0:T(2,128)S(1)}, s32[2,4]{1,0:T(2,128)}, u32[]{:S(2)}) copy-start(s32[2,4]{1,0:T(2,128)} %param.10) | copy-start | bytes 100
  2.9 20.1 %collective-permute-start = (bf16[256,512]{1,0:T(8,128)(2,1)}, bf16[256,512]{1,0:T(8,128)(2,1)S(1)}, u32[]{:S(2)}, u32[]{:S(2)}) collective-permute-start(bf16[256,512]{1,0:T(8,128)(2,1)} %get-tuple-element.17), channel_id=1, source_target_pairs={{0,16},{16,0},{1,17},{17,1},{2,18},{18,2},{3,19},{19,3},{4,20},{20... | collective-permute-start | bytes 786440 | tf_op jit(solution)/shard_map/ppermute | solution.py:77
  5.8 17.2 %collective-permute-start.1 = (bf16[256,512]{1,0:T(8,128)(2,1)S(1)}, bf16[256,512]{1,0:T(8,128)(2,1)S(1)}, u32[]{:S(2)}, u32[]{:S(2)}) collective-permute-start(bf16[256,512]{1,0:T(8,128)(2,1)S(1)} %get-tuple-element.18), channel_id=1, source_target_pairs={{0,16},{16,0},{1,17},{17,1},{2,18},{18,2},{3,19},{19,3},{4,20},{20... | collective-permute-start | bytes 786440 | tf_op jit(solution)/shard_map/ppermute | solution.py:77
  6.4 7.8 %copy-start.5 = (s32[2,5]{1,0:T(2,128)S(1)}, s32[2,5]{1,0:T(2,128)}, u32[]{:S(2)}) copy-start(s32[2,5]{1,0:T(2,128)} %param.11) | copy-start | bytes 124
  6.4 16.5 %copy-start.1 = (f32[1,512,512]{2,1,0:T(8,128)S(1)}, f32[1,512,512]{2,1,0:T(8,128)}, u32[]{:S(2)}) copy-start(f32[1,512,512]{2,1,0:T(8,128)} %param.6) | copy-start | bytes 3145732
  6.4 16.5 %copy-start.2 = (bf16[1,512,512]{2,1,0:T(8,128)(2,1)S(1)}, bf16[1,512,512]{2,1,0:T(8,128)(2,1)}, u32[]{:S(2)}) copy-start(bf16[1,512,512]{2,1,0:T(8,128)(2,1)} %param.8) | copy-start | bytes 1572868
  6.4 16.6 %copy-start.3 = (f32[1,512,512]{2,1,0:T(8,128)S(1)}, f32[1,512,512]{2,1,0:T(8,128)}, u32[]{:S(2)}) copy-start(f32[1,512,512]{2,1,0:T(8,128)} %param.7) | copy-start | bytes 3145732
  11.6 53.6 %collective-permute-start.8 = (bf16[192,2048]{1,0:T(8,128)(2,1)}, bf16[192,2048]{1,0:T(8,128)(2,1)}, u32[]{:S(2)}, u32[]{:S(2)}) collective-permute-start(bf16[192,2048]{1,0:T(8,128)(2,1)} %get-tuple-element.8), channel_id=1, source_target_pairs={{0,1},{1,0},{2,3},{3,2},{4,5},{5,4},{6,7},{7,6},{8,9},{9,8},{10,11... | collective-permute-start | bytes 2359304 | tf_op jit(solution)/shard_map/ppermute | solution.py:104
  11.7 62.4 %collective-permute-start.9 = (bf16[192,2048]{1,0:T(8,128)(2,1)}, bf16[192,2048]{1,0:T(8,128)(2,1)}, u32[]{:S(2)}, u32[]{:S(2)}) collective-permute-start(bf16[192,2048]{1,0:T(8,128)(2,1)} %get-tuple-element.9), channel_id=1, source_target_pairs={{0,1},{1,0},{2,3},{3,2},{4,5},{5,4},{6,7},{7,6},{8,9},{9,8},{10,11... | collective-permute-start | bytes 2359304 | tf_op jit(solution)/shard_map/ppermute | solution.py:103
  12.2 59.7 %collective-permute-start.12 = (bf16[192,2048]{1,0:T(8,128)(2,1)}, bf16[192,2048]{1,0:T(8,128)(2,1)}, u32[]{:S(2)}, u32[]{:S(2)}) collective-permute-start(bf16[192,2048]{1,0:T(8,128)(2,1)} %get-tuple-element.10), channel_id=1, source_target_pairs={{0,2},{1,3},{2,0},{3,1},{4,6},{5,7},{6,4},{7,5},{8,10},{9,11},{10,... | collective-permute-start | bytes 2359304 | tf_op jit(solution)/shard_map/ppermute | solution.py:102
  24.6 6.9 %copy-start.4 = (bf16[192,2048]{1,0:T(8,128)(2,1)S(1)}, bf16[192,2048]{1,0:T(8,128)(2,1)}, u32[]{:S(2)}) copy-start(bf16[192,2048]{1,0:T(8,128)(2,1)} %get-tuple-element.7) | copy-start | bytes 2359300
  24.6 11.1 %collective-permute-start.4 = (bf16[256,512]{1,0:T(8,128)(2,1)S(1)}, bf16[256,512]{1,0:T(8,128)(2,1)S(1)}, u32[]{:S(2)}, u32[]{:S(2)}) collective-permute-start(bf16[256,512]{1,0:T(8,128)(2,1)S(1)} %get-tuple-element.15), channel_id=1, source_target_pairs={{0,12},{1,13},{2,14},{3,15},{4,8},{5,9},{6,10},{7,11},{8,4},{9,5},... | collective-permute-start | bytes 786440 | tf_op jit(solution)/shard_map/ppermute | solution.py:117
  28.3 18.4 %collective-permute-start.5 = (bf16[256,512]{1,0:T(8,128)(2,1)S(1)}, bf16[256,512]{1,0:T(8,128)(2,1)S(1)}, u32[]{:S(2)}, u32[]{:S(2)}) collective-permute-start(bf16[256,512]{1,0:T(8,128)(2,1)S(1)} %get-tuple-element.16), channel_id=1, source_target_pairs={{0,12},{1,13},{2,14},{3,15},{4,8},{5,9},{6,10},{7,11},{8,4},{9,5},... | collective-permute-start | bytes 786440 | tf_op jit(solution)/shard_map/ppermute | solution.py:117
  35.8 15.6 %collective-permute-start.3 = (bf16[256,512]{1,0:T(8,128)(2,1)S(1)}, bf16[256,512]{1,0:T(8,128)(2,1)S(1)}, u32[]{:S(2)}, u32[]{:S(2)}) collective-permute-start(bf16[256,512]{1,0:T(8,128)(2,1)S(1)} %get-tuple-element.16), channel_id=1, source_target_pairs={{0,4},{1,5},{2,6},{3,7},{4,0},{5,1},{6,2},{7,3},{8,12},{9,13},{10,... | collective-permute-start | bytes 786440 | tf_op jit(solution)/shard_map/ppermute | solution.py:118
  46.7 29.0 %collective-permute-start.2 = (bf16[256,512]{1,0:T(8,128)(2,1)S(1)}, bf16[256,512]{1,0:T(8,128)(2,1)S(1)}, u32[]{:S(2)}, u32[]{:S(2)}) collective-permute-start(bf16[256,512]{1,0:T(8,128)(2,1)S(1)} %get-tuple-element.15), channel_id=1, source_target_pairs={{0,4},{1,5},{2,6},{3,7},{4,0},{5,1},{6,2},{7,3},{8,12},{9,13},{10,... | collective-permute-start | bytes 786440 | tf_op jit(solution)/shard_map/ppermute | solution.py:118
  51.4 11.0 %collective-permute-start.6 = (bf16[256,512]{1,0:T(8,128)(2,1)S(1)}, bf16[256,512]{1,0:T(8,128)(2,1)S(1)}, u32[]{:S(2)}, u32[]{:S(2)}) collective-permute-start(bf16[256,512]{1,0:T(8,128)(2,1)S(1)} %broadcast_select_fusion.1), channel_id=1, source_target_pairs={{0,8},{1,9},{2,10},{3,11},{4,0},{5,1},{6,2},{7,3},{8,12},{9,13},{1... | collective-permute-start | bytes 786440 | tf_op jit(solution)/shard_map/ppermute | solution.py:120
  62.4 8.4 %collective-permute-start.7 = (bf16[256,512]{1,0:T(8,128)(2,1)S(1)}, bf16[256,512]{1,0:T(8,128)(2,1)S(1)}, u32[]{:S(2)}, u32[]{:S(2)}) collective-permute-start(bf16[256,512]{1,0:T(8,128)(2,1)S(1)} %broadcast_select_fusion), channel_id=1, source_target_pairs={{0,8},{1,9},{2,10},{3,11},{4,0},{5,1},{6,2},{7,3},{8,12},{9,13},{1... | collective-permute-start | bytes 786440 | tf_op jit(solution)/shard_map/ppermute | solution.py:120
  74.1 17.7 %collective-permute-start.10 = (bf16[192,2048]{1,0:T(8,128)(2,1)}, bf16[192,2048]{1,0:T(8,128)(2,1)S(1)}, u32[]{:S(2)}, u32[]{:S(2)}) collective-permute-start(bf16[192,2048]{1,0:T(8,128)(2,1)} %collective-permute-done.9), channel_id=1, source_target_pairs={{0,2},{1,3},{2,0},{3,1},{4,6},{5,7},{6,4},{7,5},{8,10},{9,11},{10,... | collective-permute-start | bytes 2359304 | tf_op jit(solution)/shard_map/ppermute | solution.py:105
  93.6 4.5 %collective-permute-start.11 = (f32[384,512]{1,0:T(8,128)S(1)}, f32[384,512]{1,0:T(8,128)S(1)}, u32[]{:S(2)}, u32[]{:S(2)}) collective-permute-start(f32[384,512]{1,0:T(8,128)S(1)} %pad_maximum_fusion), channel_id=1, source_target_pairs={{0,1},{1,0},{2,3},{3,2},{4,5},{5,4},{6,7},{7,6},{8,9},{9,8},{10,11... | collective-permute-start | bytes 2359304 | tf_op jit(solution)/shard_map/ppermute | solution.py:135
  99.3 7.4 %collective-permute-start.13 = (bf16[192,512]{1,0:T(8,128)(2,1)S(1)}, bf16[192,512]{1,0:T(8,128)(2,1)S(1)}, u32[]{:S(2)}, u32[]{:S(2)}) collective-permute-start(bf16[192,512]{1,0:T(8,128)(2,1)S(1)} %fusion.27), channel_id=1, source_target_pairs={{0,2},{1,3},{2,0},{3,1},{4,6},{5,7},{6,4},{7,5},{8,10},{9,11},{10,... | collective-permute-start | bytes 589832 | tf_op jit(solution)/shard_map/ppermute | solution.py:139

commit v2 on v1

v2 whole, which is shorter than its diff:
```python
import functools

import jax
import jax.numpy as jnp
from jax import lax
from jax.experimental import pallas as pl
from jax.experimental.pallas import tpu as pltpu
from jax.sharding import PartitionSpec as P

outer_rate = 0.7
momentum_decay = 0.9
PLANE = 4
CHUNKS = 2
SMEM = pl.BlockSpec(memory_space=pltpu.SMEM)
SMALL = pltpu.CompilerParams(vmem_limit_bytes=16 * 2**20)
LITTLE = pl.CostEstimate(flops=0, bytes_accessed=0, transcendentals=0)


def plane_pairs(size, bit):
    return [(i, i ^ bit) for i in range(size)]


def line_pairs(size, to):
    return [(i, to[i // PLANE] * PLANE + i % PLANE) for i in range(size)]


def whole(array):
    return pl.BlockSpec(array.shape, lambda *_: (0,) * array.ndim)


def arrange_body(order, *refs):
    for source, target in zip(refs[:PLANE], refs[PLANE:]):
        target[...] = source[...]


def arrange_tokens(tokens, order, width):
    rows, blocks = tokens.shape[0], order.shape[0] // PLANE

    def column(distance):
        return lambda k, order: (0, order[k * PLANE + distance])

    return pl.pallas_call(
        arrange_body,
        grid_spec=pltpu.PrefetchScalarGridSpec(
            num_scalar_prefetch=1,
            grid=(blocks,),
            in_specs=[pl.BlockSpec((rows, width), column(d)) for d in range(PLANE)],
            out_specs=[pl.BlockSpec((rows, width), lambda k, order: (0, k))] * PLANE,
        ),
        out_shape=[jax.ShapeDtypeStruct((rows, blocks * width), tokens.dtype)] * PLANE,
        cost_estimate=LITTLE,
        compiler_params=SMALL,
        name="arrange_tokens",
    )(order, *([tokens] * PLANE))


def delta_body(master, working, delta):
    delta[...] = (master[...] - working[...].astype(jnp.float32)).astype(delta.dtype)


def pseudo_gradient(master, working, chunk, rows):
    block = pl.BlockSpec((rows, master.shape[1]), lambda *_: (chunk, 0))
    shape = (rows, master.shape[1])
    return pl.pallas_call(
        delta_body,
        grid=(1,),
        in_specs=[block, block],
        out_specs=pl.BlockSpec(shape, lambda *_: (0, 0)),
        out_shape=jax.ShapeDtypeStruct(shape, jnp.bfloat16),
        cost_estimate=LITTLE,
        compiler_params=SMALL,
        name="pseudo_gradient",
    )(master, working)


def update_body(groups, own_group, partners, mix_weights, master, momentum, working, *refs):
    received, outs = refs[: max(groups - 1, 1) if groups == 2 else groups], refs[-2:]
    me = own_group[0]
    numerators = [mix_weights[me, j].astype(jnp.float32) for j in range(5)]
    total = sum(numerators)

    def coefficient(group):
        found = jnp.where(group == me, numerators[0], 0.0)
        for j in range(4):
            found = found + jnp.where(partners[me, j] == group, numerators[j + 1], 0.0)
        return found

    mixed = coefficient(me) * (master[...] - working[...].astype(jnp.float32))
    if groups == 2:
        mixed = mixed + coefficient(1 - me) * received[0][...].astype(jnp.float32)
    else:
        for g in range(groups):
            away = jnp.where(g == me, 0.0, coefficient(g))
            mixed = mixed + away * received[g][...].astype(jnp.float32)
    mixed = mixed / total
    new_momentum = momentum_decay * momentum[...] + mixed
    new_master = master[...] - outer_rate * (mixed + momentum_decay * new_momentum)
    if len(refs) == len(received) + 1:
        refs[-1][...] = new_master.astype(jnp.bfloat16)
    else:
        outs[0][...] = new_master
        outs[1][...] = new_momentum


def next_working(scalars, groups, master, momentum, working, received, chunk, rows):
    width = master.shape[1]
    block = pl.BlockSpec((rows, width), lambda *_: (chunk, 0))
    return pl.pallas_call(
        functools.partial(update_body, groups),
        grid=(1,),
        in_specs=[SMEM] * 3 + [block] * 3 + [whole(r) for r in received],
        out_specs=pl.BlockSpec((rows, width), lambda *_: (0, 0)),
        out_shape=jax.ShapeDtypeStruct((rows, width), jnp.bfloat16),
        cost_estimate=LITTLE,
        compiler_params=SMALL,
        name="next_working",
    )(*scalars, master, momentum, working, *received)


def outer_step_body(groups, chunks, own_group, partners, mix_weights, master, momentum, working, *refs):
    received, outs = refs[:-2], refs[-2:]
    step = master.shape[0] // chunks
    each = len(received) // chunks
    for i in range(chunks):
        part = pl.ds(i * step, step)
        update_body(
            groups, own_group, partners, mix_weights, master.at[part], momentum.at[part], working.at[part],
            *received[i * each : (i + 1) * each], *[o.at[part] for o in outs],
        )


def outer_step(scalars, groups, master, momentum, working, received):
    received = [r for chunk in received for r in chunk]
    chunks = len(received) // (1 if groups == 2 else groups)
    shape = jax.ShapeDtypeStruct(master.shape, jnp.float32)
    return pl.pallas_call(
        functools.partial(outer_step_body, groups, chunks),
        grid=(1,),
        in_specs=[SMEM] * 3 + [whole(a) for a in (master, momentum, working, *received)],
        out_specs=[whole(master)] * 2,
        out_shape=[shape, shape],
        cost_estimate=LITTLE,
        compiler_params=SMALL,
        name="outer_step",
    )(*scalars, master, momentum, working, *received)


def product(tokens, pieces, offsets):
    total = None
    for piece, offset in zip(pieces, offsets):
        term = jnp.dot(
            tokens[:, offset : offset + piece.shape[0]], piece[...], preferred_element_type=jnp.float32
        )
        total = term if total is None else total + term
    return total


def early_body(offsets, tokens, *refs):
    refs[-1][...] = product(tokens, refs[:-1], offsets)


def early_keys(tokens, pieces, offsets):
    span = max(o + p.shape[0] for o, p in zip(offsets, pieces))
    rows, width = tokens.shape[0], pieces[0].shape[1]
    return pl.pallas_call(
        functools.partial(early_body, offsets),
        grid=(1,),
        in_specs=[pl.BlockSpec((rows, span), lambda *_: (0, 0))] + [whole(p) for p in pieces],
        out_specs=pl.BlockSpec((rows, width), lambda *_: (0, 0)),
        out_shape=jax.ShapeDtypeStruct((rows, width), jnp.float32),
        cost_estimate=LITTLE,
        compiler_params=SMALL,
        name="early_keys",
    )(tokens, *pieces)


def late_body(offsets, *refs):
    tokens, sums, pieces = refs[:PLANE], refs[PLANE : 2 * PLANE], refs[2 * PLANE : -3]
    own, from_core, from_y, from_both = [s[...] + product(t, pieces, offsets) for t, s in zip(tokens, sums)]
    keep, keep_y, to_core = refs[-3:]
    count = keep.shape[0]
    to_core[:count] = from_core
    to_core[count:] = from_both
    keep[...] = own
    keep_y[...] = from_y


def late_keys(tokens, sums, pieces, offsets):
    least, span = min(offsets), max(o + p.shape[0] for o, p in zip(offsets, pieces))
    rows, width = sums[0].shape
    if least % (span - least):
        least = 0
    taken = pl.BlockSpec((rows, span - least), lambda *_: (0, least // (span - least)))
    offsets = [o - least for o in offsets]
    one = jax.ShapeDtypeStruct((rows, width), jnp.float32)
    two = jax.ShapeDtypeStruct((2 * rows, width), jnp.float32)
    return pl.pallas_call(
        functools.partial(late_body, offsets),
        grid=(1,),
        in_specs=[taken] * PLANE + [whole(a) for a in (*sums, *pieces)],
        out_specs=[whole(one), whole(one), whole(two)],
        out_shape=[one, one, two],
        cost_estimate=LITTLE,
        compiler_params=SMALL,
        name="late_keys",
    )(*tokens, *sums, *pieces)


def over_core_body(keep_y, back, to_y):
    to_y[...] = (keep_y[...] + back[...]).astype(to_y.dtype)


def over_core(keep_y, back):
    rows, width = keep_y.shape
    return pl.pallas_call(
        over_core_body,
        grid=(1,),
        in_specs=[whole(keep_y), pl.BlockSpec((rows, width), lambda *_: (1, 0))],
        out_specs=whole(keep_y),
        out_shape=jax.ShapeDtypeStruct((rows, width), jnp.bfloat16),
        cost_estimate=LITTLE,
        compiler_params=SMALL,
        name="over_core",
    )(keep_y, back)


def over_y_body(keep, back, there, keys):
    keys[...] = (keep[...] + back[...] + there[...].astype(jnp.float32)).astype(keys.dtype)


def over_y(keep, back, there):
    rows, width = keep.shape
    return pl.pallas_call(
        over_y_body,
        grid=(1,),
        in_specs=[whole(keep), pl.BlockSpec((rows, width), lambda *_: (0, 0)), whole(there)],
        out_specs=whole(keep),
        out_shape=jax.ShapeDtypeStruct((rows, width), jnp.bfloat16),
        cost_estimate=LITTLE,
        compiler_params=SMALL,
        name="over_y",
    )(keep, back, there)


def shards(master, momentum, working, tokens, partners, mix_weights):
    groups = lax.axis_size("replica")
    size = lax.axis_size("fsdp")
    line = size // PLANE
    place = lax.axis_index("fsdp")
    master, momentum, working, tokens = master[0], momentum[0], working[0], tokens[0]
    rows = master.shape[0]
    chunks = CHUNKS if rows % (CHUNKS * 16) == 0 else 1
    step = rows // chunks
    scalars = (lax.axis_index("replica").astype(jnp.int32)[None], partners, mix_weights)

    received = []
    for i in range(chunks):
        delta = pseudo_gradient(master, working, i, step)
        if groups == 2:
            received.append([lax.ppermute(delta, "replica", [(0, 1), (1, 0)])])
        else:
            every = lax.all_gather(delta, "replica", axis=0)
            received.append([every[g] for g in range(groups)])

    if line == 4:
        order = [place ^ (k * PLANE + d) for k in (0, 1, 3, 2) for d in range(PLANE)]
    else:
        order = [((place % PLANE) ^ d) + k * PLANE for k in range(line) for d in range(PLANE)]
    order = jnp.stack(order).astype(jnp.int32)
    own, for_core, for_y, for_both = arrange_tokens(tokens, order, rows)
    from_y = lax.ppermute(for_y, "fsdp", plane_pairs(size, 2))
    at_core = lax.ppermute(for_both, "fsdp", plane_pairs(size, 1))
    from_core = lax.ppermute(for_core, "fsdp", plane_pairs(size, 1))
    from_both = lax.ppermute(at_core, "fsdp", plane_pairs(size, 2))
    inputs = [own, from_core, from_y, from_both]

    fresh = [
        next_working(scalars, groups, master, momentum, working, received[i], i, step) for i in range(chunks)
    ]
    if line == 4:
        z = place // PLANE
        middle = (z == 1) | (z == 2)
        far = [lax.ppermute(f, "fsdp", line_pairs(size, [3, 2, 1, 0])) for f in fresh]
        near = [lax.ppermute(f, "fsdp", line_pairs(size, [1, 0, 3, 2])) for f in fresh]
        last = [
            lax.ppermute(jnp.where(middle, g, f), "fsdp", line_pairs(size, [2, 0, 3, 1]))
            for f, g in zip(fresh, far)
        ]
        early, late = [*fresh, *near, *far], last
    else:
        lines = [[k * PLANE + p for k in range(line)] for p in range(PLANE)]
        every = [lax.all_gather(f, "fsdp", axis=0, axis_index_groups=lines) for f in fresh]
        blocks = [e[k] for k in range(line) for e in every]
        early, late = blocks[:-chunks], blocks[-chunks:]
    offsets = [i * step for i in range(line * chunks)]

    sums = [early_keys(t, early, offsets[:-chunks]) for t in inputs]
    keep, keep_y, to_core = late_keys(inputs, sums, late, offsets[-chunks:])
    back = lax.ppermute(to_core, "fsdp", plane_pairs(size, 1))
    there = lax.ppermute(over_core(keep_y, back), "fsdp", plane_pairs(size, 2))
    keys = over_y(keep, back, there)

    new_master, new_momentum = outer_step(scalars, groups, master, momentum, working, received)
    return new_master[None], new_momentum[None], keys[None]


def solution(mesh):
    return jax.shard_map(
        shards,
        mesh=mesh,
        in_specs=(
            P("replica", "fsdp", None),
            P("replica", "fsdp", None),
            P("replica", "fsdp", None),
            P("replica", "fsdp", None),
            P(),
            P(),
        ),
        out_specs=(
            P("replica", "fsdp", None),
            P("replica", "fsdp", None),
            P("replica", "fsdp", None),
        ),
        check_vma=False,
    )
```

time: 109 us -> 78.3 us (0.72)
  matrix products: 22 us -> 0 us
  other arithmetic: 13.8 us -> 0.07 us
  waiting for transfers between devices: 31.8 us -> 18.4 us
  Pallas kernels: 5.23 us -> 17.2 us
  starting transfers between devices: 31.5 us -> 37.4 us
  local copies, waits for them, and re-layouts: 2.5 us -> 4.02 us
    dot_general x32 -> x0, matrix products: 22 us -> none  [product(): return jnp.dot(tokens, weights, preferred_element_type=jnp.float32)]
    pallas_call x0 -> x12, Pallas kernels: none -> 14.3 us  [the longest x4 6.3 us: early_keys(): pl.pallas_call(functools.partial(early_body, offsets), grid=(1,), in_spec...]
    ppermute x1, waiting for transfers between devices: 13.7 us -> 4.06 us  [shards(): from_both = lax.ppermute(at_core, 'fsdp', plane_pairs(size, 2))]
    ppermute x2, waiting for transfers between devices: 7.65 us -> 0.01 us  [shards(): lax.ppermute(jnp.where(middle, g, f), 'fsdp', line_pairs(size, [2, 0, 3,...]
    div x1 -> x0, other arithmetic: 6.24 us -> none  [shards(): row_coef = row_coef / total]
    ppermute x8, starting transfers between devices: 22.6 us -> 27 us  [the longest x2 14.7 us: shards(): lax.ppermute(f, 'fsdp', line_pairs(size, [1, 0, 3, 2]))]
    unnamed x12 -> x22, local copies, waits for them, and re-layouts: 0.03 us -> 3.93 us
    convert_element_type x3 -> x0, other arithmetic: 3.88 us -> none  [the longest x1 2.21 us: others(): delta = (master[s] - working[s].astype(jnp.float32)).astype(jnp.bfloat16)]
  transfers between devices with their start and end apart: 14 -> 14, of which waited for: 4 -> 6; matrix products, arithmetic and copies ran while one was open for 30% -> 0% of each run, Pallas kernels for 5% -> 15%
where the time goes in v2:
time: 78.3 us; the launch traced here: 77.9 us
  starting transfers between devices  37.4 us (48%)
  waiting for transfers between devices  18.4 us (23%)
  Pallas kernels  17.2 us (22%)
  local copies, waits for them, and re-layouts  4.02 us (5%)
  between operations  0.83 us (1%)
    ppermute x2, starting transfers between devices, shards(): lax.ppermute(f, 'fsdp', line_pairs(size, [1, 0, 3, 2]))  14.7 us
    ppermute x2, starting transfers between devices, shards(): lax.ppermute(f, 'fsdp', line_pairs(size, [3, 2, 1, 0]))  8.04 us
    ppermute x2, starting transfers between devices, shards(): lax.ppermute(jnp.where(middle, g, f), 'fsdp', line_pairs(size, [2, 0, 3,...  7.95 us
    ppermute x2, waiting for transfers between devices, shards(): received.append([lax.ppermute(delta, 'replica', [(0, 1), (1, 0)])])  6.95 us
    pallas_call x4, Pallas kernels, early_keys(): pl.pallas_call(functools.partial(early_body, offsets), grid=(1,), in_spec...  6.3 us
    ppermute x1, waiting for transfers between devices, shards(): from_both = lax.ppermute(at_core, 'fsdp', plane_pairs(size, 2))  4.06 us
    unnamed x22, local copies, waits for them, and re-layouts  3.93 us
    pallas_call x1, Pallas kernels, arrange_tokens(): pl.pallas_call(arrange_body, grid_spec=pltpu.PrefetchScalarGridSpec(num_s...  2.82 us
  transfers between devices with their start and end apart: 14, of which 6 were waited for; matrix products, arithmetic and copies ran while one was open for 0% of the time, Pallas kernels for 15%

profile of v2, /device:TPU:0, one launch (start us, length us, event | category | flops | bytes accessed | tf_op | source)
XLA Modules:
  0.0 77.9 jit_solution(7734922442223706780)
XLA Ops:
  0.6 0.1 stack.67.order
  0.7 0.0 copy-start
  0.8 1.9 %copy-done = bf16[1,192,8192]{2,1,0:T(8,128)(2,1)S(1)} copy-done((bf16[1,192,8192]{2,1,0:T(8,128)(2,1)S(1)}, bf16[1,192,8192]{2,1,0:T(8,128)(2,1)}, u32[]{:S(2)}) %copy-start) | copy-done | bytes 3145752
  2.6 0.0 copy-start.1
  2.6 0.0 copy-start.2
  2.6 2.8 %arrange_tokens.1 = (bf16[192,2048]{1,0:T(8,128)(2,1)S(1)}, bf16[192,2048]{1,0:T(8,128)(2,1)}, bf16[192,2048]{1,0:T(8,128)(2,1)}, bf16[192,2048]{1,0:T(8,128)(2,1)}) custom-call(s32[16]{0:T(128)S(1)} %stack.67.order, bf16[192,8192]{1,0:T(8,128)(2,1)S(1)} %bitcast.24, bf16[192,8192]{1,0:T(8,128)(2,1)S(1)} %bitcast.25, bf16[192,8192]{1,0:T(8,128)(2,1)S(1)} %bitcast.26, ...), custom_call_target="tpu_custom_call" | custom-call | tf_op jit(solution)/shard_map/arrange_tokens/pallas_call | solution.py:42
  5.5 0.0 copy-start.4
  5.5 0.9 %copy-done.4 = bf16[192,2048]{1,0:T(8,128)(2,1)} copy-done((bf16[192,2048]{1,0:T(8,128)(2,1)}, bf16[192,2048]{1,0:T(8,128)(2,1)S(1)}, u32[]{:S(2)}) %copy-start.4) | copy-done | bytes 786456
  6.3 0.0 copy-start.3
  6.3 0.0 copy-start.9
  6.3 0.0 copy-start.10
  6.3 0.5 collective-permute-start.4
  6.8 0.0 copy-done.1
  6.8 0.0 copy-done.2
  6.9 2.6 %collective-permute-start = (bf16[256,512]{1,0:T(8,128)(2,1)S(1)}, bf16[256,512]{1,0:T(8,128)(2,1)S(1)}, u32[]{:S(2)}, u32[]{:S(2)}) collective-permute-start(bf16[256,512]{1,0:T(8,128)(2,1)S(1)} %pseudo_gradient.2), channel_id=1, source_target_pairs={{0,16},{16,0},{1,17},{17,1},{2,18},{18,2},{3,19},{19,3},{4,20},{20... | collective-permute-start | bytes 786440 | tf_op jit(solution)/shard_map/ppermute | solution.py:260
  9.4 0.8 pseudo_gradient.3
  10.2 0.0 collective-permute-start.1
  10.2 6.4 %collective-permute-done.refs_0_ = bf16[256,512]{1,0:T(8,128)(2,1)S(1)} collective-permute-done((bf16[256,512]{1,0:T(8,128)(2,1)S(1)}, bf16[256,512]{1,0:T(8,128)(2,1)S(1)}, u32[]{:S(2)}, u32[]{:S(2)}) %collective-permute-start) | collective-permute-done | bytes 262176 | tf_op jit(solution)/shard_map/ppermute | solution.py:260
  16.6 0.0 copy-start.7
  16.6 0.0 copy-done.3
  16.6 0.0 copy-done.9
  16.6 0.0 copy-done.10
  16.6 0.8 %next_working.2.refs_0_ = bf16[256,512]{1,0:T(8,128)(2,1)S(1)} custom-call(s32[1]{0:T(128)} %bitcast.own_group, s32[2,4]{1,0:T(2,128)S(1)} %copy-done.9, s32[2,5]{1,0:T(2,128)S(1)} %copy-done.10, f32[512,512]{1,0:T(8,128)S(1)} %bitcast.30, f32[512,512]{1,0:T(8,128)S(1)} %bitcast.38, bf16[512,512]{1,0:T(8,128)(2,1)S(1)} %bitcast.35, ...), custom_call_target="tpu_custom_call" | custom-call | tf_op jit(solution)/shard_map/next_working/pallas_call | solution.py:108
  17.4 4.1 %collective-permute-start.8 = (bf16[256,512]{1,0:T(8,128)(2,1)S(1)}, bf16[256,512]{1,0:T(8,128)(2,1)S(1)}, u32[]{:S(2)}, u32[]{:S(2)}) collective-permute-start(bf16[256,512]{1,0:T(8,128)(2,1)S(1)} %next_working.2.refs_0_), channel_id=1, source_target_pairs={{0,12},{1,13},{2,14},{3,15},{4,8},{5,9},{6,10},{7,11},{8,4},{9,5},... | collective-permute-start | bytes 786440 | tf_op jit(solution)/shard_map/ppermute | solution.py:283
  21.5 0.0 copy-done.7
  21.6 0.6 collective-permute-done.1.refs_1_.refs_0_
  22.1 1.2 %next_working.3.refs_1_ = bf16[256,512]{1,0:T(8,128)(2,1)S(1)} custom-call(s32[1]{0:T(128)} %bitcast.own_group, s32[2,4]{1,0:T(2,128)S(1)} %copy-done.9, s32[2,5]{1,0:T(2,128)S(1)} %copy-done.10, f32[512,512]{1,0:T(8,128)S(1)} %bitcast.31, f32[512,512]{1,0:T(8,128)S(1)} %bitcast.39, bf16[512,512]{1,0:T(8,128)(2,1)S(1)} %bitcast.36, ...), custom_call_target="tpu_custom_call" | custom-call | tf_op jit(solution)/shard_map/next_working/pallas_call | solution.py:108
  23.3 3.9 %collective-permute-start.9 = (bf16[256,512]{1,0:T(8,128)(2,1)S(1)}, bf16[256,512]{1,0:T(8,128)(2,1)}, u32[]{:S(2)}, u32[]{:S(2)}) collective-permute-start(bf16[256,512]{1,0:T(8,128)(2,1)S(1)} %next_working.3.refs_1_), channel_id=1, source_target_pairs={{0,12},{1,13},{2,14},{3,15},{4,8},{5,9},{6,10},{7,11},{8,4},{9,5},... | collective-permute-start | bytes 786440 | tf_op jit(solution)/shard_map/ppermute | solution.py:283
  27.2 0.0 collective-permute-start.2
  27.2 1.5 %collective-permute-start.3 = (bf16[192,2048]{1,0:T(8,128)(2,1)}, bf16[192,2048]{1,0:T(8,128)(2,1)}, u32[]{:S(2)}, u32[]{:S(2)}) collective-permute-start(bf16[192,2048]{1,0:T(8,128)(2,1)} %get-tuple-element.16), channel_id=1, source_target_pairs={{0,2},{1,3},{2,0},{3,1},{4,6},{5,7},{6,4},{7,5},{8,10},{9,11},{10,... | collective-permute-start | bytes 2359304 | tf_op jit(solution)/shard_map/ppermute | solution.py:271
  28.8 0.0 collective-permute-done.4
  28.8 0.5 collective-permute-start.5
  29.3 0.0 collective-permute-done.8.refs_4_
  29.3 10.0 %collective-permute-start.6 = (bf16[256,512]{1,0:T(8,128)(2,1)S(1)}, bf16[256,512]{1,0:T(8,128)(2,1)S(1)}, u32[]{:S(2)}, u32[]{:S(2)}) collective-permute-start(bf16[256,512]{1,0:T(8,128)(2,1)S(1)} %next_working.2.refs_0_), channel_id=1, source_target_pairs={{0,4},{1,5},{2,6},{3,7},{4,0},{5,1},{6,2},{7,3},{8,12},{9,13},{10,... | collective-permute-start | bytes 786440 | tf_op jit(solution)/shard_map/ppermute | solution.py:284
  39.3 0.0 collective-permute-done.9.refs_5_
  39.3 4.7 %collective-permute-start.7 = (bf16[256,512]{1,0:T(8,128)(2,1)S(1)}, bf16[256,512]{1,0:T(8,128)(2,1)S(1)}, u32[]{:S(2)}, u32[]{:S(2)}) collective-permute-start(bf16[256,512]{1,0:T(8,128)(2,1)S(1)} %next_working.3.refs_1_), channel_id=1, source_target_pairs={{0,4},{1,5},{2,6},{3,7},{4,0},{5,1},{6,2},{7,3},{8,12},{9,13},{10,... | collective-permute-start | bytes 786440 | tf_op jit(solution)/shard_map/ppermute | solution.py:284
  44.1 0.0 collective-permute-done.6.refs_2_
  44.1 4.7 %collective-permute-start.10 = (bf16[256,512]{1,0:T(8,128)(2,1)S(1)}, bf16[256,512]{1,0:T(8,128)(2,1)S(1)}, u32[]{:S(2)}, u32[]{:S(2)}) collective-permute-start(bf16[256,512]{1,0:T(8,128)(2,1)S(1)} %broadcast_select_fusion.1), channel_id=1, source_target_pairs={{0,8},{1,9},{2,10},{3,11},{4,0},{5,1},{6,2},{7,3},{8,12},{9,13},{1... | collective-permute-start | bytes 786440 | tf_op jit(solution)/shard_map/ppermute | solution.py:286
  48.8 2.4 %collective-permute-done.7.refs_3_ = bf16[256,512]{1,0:T(8,128)(2,1)S(1)} collective-permute-done((bf16[256,512]{1,0:T(8,128)(2,1)S(1)}, bf16[256,512]{1,0:T(8,128)(2,1)S(1)}, u32[]{:S(2)}, u32[]{:S(2)}) %collective-permute-start.7) | collective-permute-done | bytes 262176 | tf_op jit(solution)/shard_map/ppermute | solution.py:284
  51.2 3.2 %collective-permute-start.11 = (bf16[256,512]{1,0:T(8,128)(2,1)S(1)}, bf16[256,512]{1,0:T(8,128)(2,1)S(1)}, u32[]{:S(2)}, u32[]{:S(2)}) collective-permute-start(bf16[256,512]{1,0:T(8,128)(2,1)S(1)} %broadcast_select_fusion), channel_id=1, source_target_pairs={{0,8},{1,9},{2,10},{3,11},{4,0},{5,1},{6,2},{7,3},{8,12},{9,13},{1... | collective-permute-start | bytes 786440 | tf_op jit(solution)/shard_map/ppermute | solution.py:286
  54.4 0.0 copy-start.5
  54.4 1.1 %copy-done.5 = bf16[192,2048]{1,0:T(8,128)(2,1)S(1)} copy-done((bf16[192,2048]{1,0:T(8,128)(2,1)S(1)}, bf16[192,2048]{1,0:T(8,128)(2,1)}, u32[]{:S(2)}) %copy-start.5) | copy-done | bytes 786456
  55.5 1.4 %early_keys.4.refs_4_ = f32[192,512]{1,0:T(8,128)S(1)} custom-call(bf16[192,2048]{1,0:T(8,128)(2,1)S(1)} %copy-done.5, bf16[256,512]{1,0:T(8,128)(2,1)S(1)} %next_working.2.refs_0_, bf16[256,512]{1,0:T(8,128)(2,1)S(1)} %next_working.3.refs_1_, bf16[256,512]{1,0:T(8,128)(2,1)S(1)} %collective-permute-done.6.refs_2_, ...), custom_call_target="tpu_custom_call" | custom-call | tf_op jit(solution)/shard_map/early_keys/pallas_call | solution.py:165
  57.0 0.0 collective-permute-done.2.tokens.refs_1_
  57.0 1.6 %early_keys.5.refs_5_ = f32[192,512]{1,0:T(8,128)S(1)} custom-call(bf16[192,2048]{1,0:T(8,128)(2,1)} %collective-permute-done.2.tokens.refs_1_, bf16[256,512]{1,0:T(8,128)(2,1)S(1)} %next_working.2.refs_0_, bf16[256,512]{1,0:T(8,128)(2,1)S(1)} %next_working.3.refs_1_, bf16[256,512]{1,0:T(8,128)(2,1)S(1)} %collective-permute-done.6.refs_2_, ...), custom_call_target="tpu_custom_call" | custom-call | tf_op jit(solution)/shard_map/early_keys/pallas_call | solution.py:165
  58.6 0.0 copy-start.6
  58.6 0.0 collective-permute-done.3.tokens.refs_2_
  58.6 1.7 %early_keys.6.refs_6_ = f32[192,512]{1,0:T(8,128)S(1)} custom-call(bf16[192,2048]{1,0:T(8,128)(2,1)} %collective-permute-done.3.tokens.refs_2_, bf16[256,512]{1,0:T(8,128)(2,1)S(1)} %next_working.2.refs_0_, bf16[256,512]{1,0:T(8,128)(2,1)S(1)} %next_working.3.refs_1_, bf16[256,512]{1,0:T(8,128)(2,1)S(1)} %collective-permute-done.6.refs_2_, ...), custom_call_target="tpu_custom_call" | custom-call | tf_op jit(solution)/shard_map/early_keys/pallas_call | solution.py:165
  60.3 4.1 %collective-permute-done.5.tokens.refs_3_ = bf16[192,2048]{1,0:T(8,128)(2,1)} collective-permute-done((bf16[192,2048]{1,0:T(8,128)(2,1)}, bf16[192,2048]{1,0:T(8,128)(2,1)}, u32[]{:S(2)}, u32[]{:S(2)}) %collective-permute-start.5) | collective-permute-done | bytes 786464 | tf_op jit(solution)/shard_map/ppermute | solution.py:274
  64.4 1.6 %early_keys.7.refs_7_ = f32[192,512]{1,0:T(8,128)S(1)} custom-call(bf16[192,2048]{1,0:T(8,128)(2,1)} %collective-permute-done.5.tokens.refs_3_, bf16[256,512]{1,0:T(8,128)(2,1)S(1)} %next_working.2.refs_0_, bf16[256,512]{1,0:T(8,128)(2,1)S(1)} %next_working.3.refs_1_, bf16[256,512]{1,0:T(8,128)(2,1)S(1)} %collective-permute-done.6.refs_2_, ...), custom_call_target="tpu_custom_call" | custom-call | tf_op jit(solution)/shard_map/early_keys/pallas_call | solution.py:165
  66.0 0.0 copy-start.8
  66.0 0.0 collective-permute-done.10.refs_8_
  66.0 0.0 collective-permute-done.11.refs_9_
  66.0 0.0 copy-done.6
  66.0 1.7 %late_keys.1 = (f32[192,512]{1,0:T(8,128)S(1)}, f32[192,512]{1,0:T(8,128)S(1)}, f32[384,512]{1,0:T(8,128)S(1)}) custom-call(bf16[192,2048]{1,0:T(8,128)(2,1)S(1)} %copy-done.6, bf16[192,2048]{1,0:T(8,128)(2,1)} %collective-permute-done.2.tokens.refs_1_, bf16[192,2048]{1,0:T(8,128)(2,1)} %collective-permute-done.3.tokens.refs_2_, ...), custom_call_target="tpu_custom_call" | custom-call | tf_op jit(solution)/shard_map/late_keys/pallas_call | solution.py:197
  67.8 0.1 collective-permute-start.12
  67.8 2.3 %collective-permute-done.12.back = f32[384,512]{1,0:T(8,128)S(1)} collective-permute-done((f32[384,512]{1,0:T(8,128)S(1)}, f32[384,512]{1,0:T(8,128)S(1)}, u32[]{:S(2)}, u32[]{:S(2)}) %collective-permute-start.12) | collective-permute-done | bytes 786464 | tf_op jit(solution)/shard_map/ppermute | solution.py:299
  70.2 1.6 %collective-permute-start.13 = (bf16[192,512]{1,0:T(8,128)(2,1)S(1)}, bf16[192,512]{1,0:T(8,128)(2,1)S(1)}, u32[]{:S(2)}, u32[]{:S(2)}) collective-permute-start(bf16[192,512]{1,0:T(8,128)(2,1)S(1)} %over_core.1), channel_id=1, source_target_pairs={{0,2},{1,3},{2,0},{3,1},{4,6},{5,7},{6,4},{7,5},{8,10},{9,11},{10,... | collective-permute-start | bytes 589832 | tf_op jit(solution)/shard_map/ppermute | solution.py:300
  71.7 0.0 copy-done.8
  71.7 2.7 %outer_step.1 = (f32[512,512]{1,0:T(8,128)}, f32[512,512]{1,0:T(8,128)}) custom-call(s32[1]{0:T(128)} %bitcast.own_group, s32[2,4]{1,0:T(2,128)S(1)} %copy-done.9, s32[2,5]{1,0:T(2,128)S(1)} %copy-done.10, f32[512,512]{1,0:T(8,128)S(1)} %bitcast.32, f32[512,512]{1,0:T(8,128)S(1)} %bitcast.40, bf16[512,512]{1,0:T(8,128)(2,1)S(1)} %bitcast.37, ...), custom_call_target="tpu_custom_call" | custom-call | tf_op jit(solution)/shard_map/outer_step/pallas_call | solution.py:136
  74.5 2.7 %collective-permute-done.13.there = bf16[192,512]{1,0:T(8,128)(2,1)S(1)} collective-permute-done((bf16[192,512]{1,0:T(8,128)(2,1)S(1)}, bf16[192,512]{1,0:T(8,128)(2,1)S(1)}, u32[]{:S(2)}, u32[]{:S(2)}) %collective-permute-start.13) | collective-permute-done | bytes 196640 | tf_op jit(solution)/shard_map/ppermute | solution.py:300
  77.2 0.7 over_y.1
  (4 shorter events, 0.2 us)
Async XLA Ops:
  0.7 1.9 %copy-start = (bf16[1,192,8192]{2,1,0:T(8,128)(2,1)S(1)}, bf16[1,192,8192]{2,1,0:T(8,128)(2,1)}, u32[]{:S(2)}) copy-start(bf16[1,192,8192]{2,1,0:T(8,128)(2,1)} %param.9) | copy-start | bytes 9437188
  2.6 4.2 %copy-start.1 = (f32[1,512,512]{2,1,0:T(8,128)S(1)}, f32[1,512,512]{2,1,0:T(8,128)}, u32[]{:S(2)}) copy-start(f32[1,512,512]{2,1,0:T(8,128)} %param.6) | copy-start | bytes 3145732
  2.6 4.2 %copy-start.2 = (bf16[1,512,512]{2,1,0:T(8,128)(2,1)S(1)}, bf16[1,512,512]{2,1,0:T(8,128)(2,1)}, u32[]{:S(2)}) copy-start(bf16[1,512,512]{2,1,0:T(8,128)(2,1)} %param.8) | copy-start | bytes 1572868
  5.5 0.9 %copy-start.4 = (bf16[192,2048]{1,0:T(8,128)(2,1)}, bf16[192,2048]{1,0:T(8,128)(2,1)S(1)}, u32[]{:S(2)}) copy-start(bf16[192,2048]{1,0:T(8,128)(2,1)S(1)} %get-tuple-element.14.tokens.refs_0_) | copy-start | bytes 2359300
  6.3 10.3 %copy-start.3 = (f32[1,512,512]{2,1,0:T(8,128)S(1)}, f32[1,512,512]{2,1,0:T(8,128)}, u32[]{:S(2)}) copy-start(f32[1,512,512]{2,1,0:T(8,128)} %param.7) | copy-start | bytes 3145732
  6.3 10.3 %copy-start.9 = (s32[2,4]{1,0:T(2,128)S(1)}, s32[2,4]{1,0:T(2,128)}, u32[]{:S(2)}) copy-start(s32[2,4]{1,0:T(2,128)} %partners.5) | copy-start | bytes 100
  6.3 10.3 %copy-start.10 = (s32[2,5]{1,0:T(2,128)S(1)}, s32[2,5]{1,0:T(2,128)}, u32[]{:S(2)}) copy-start(s32[2,5]{1,0:T(2,128)} %mix_weights.5) | copy-start | bytes 124
  6.3 22.4 %collective-permute-start.4 = (bf16[192,2048]{1,0:T(8,128)(2,1)}, bf16[192,2048]{1,0:T(8,128)(2,1)}, u32[]{:S(2)}, u32[]{:S(2)}) collective-permute-start(bf16[192,2048]{1,0:T(8,128)(2,1)} %get-tuple-element.17), channel_id=1, source_target_pairs={{0,1},{1,0},{2,3},{3,2},{4,5},{5,4},{6,7},{7,6},{8,9},{9,8},{10,11... | collective-permute-start | bytes 2359304 | tf_op jit(solution)/shard_map/ppermute | solution.py:272
  6.9 9.7 %collective-permute-start = (bf16[256,512]{1,0:T(8,128)(2,1)S(1)}, bf16[256,512]{1,0:T(8,128)(2,1)S(1)}, u32[]{:S(2)}, u32[]{:S(2)}) collective-permute-start(bf16[256,512]{1,0:T(8,128)(2,1)S(1)} %pseudo_gradient.2), channel_id=1, source_target_pairs={{0,16},{16,0},{1,17},{17,1},{2,18},{18,2},{3,19},{19,3},{4,20},{20... | collective-permute-start | bytes 786440 | tf_op jit(solution)/shard_map/ppermute | solution.py:260
  10.2 11.9 %collective-permute-start.1 = (bf16[256,512]{1,0:T(8,128)(2,1)}, bf16[256,512]{1,0:T(8,128)(2,1)}, u32[]{:S(2)}, u32[]{:S(2)}) collective-permute-start(bf16[256,512]{1,0:T(8,128)(2,1)} %pseudo_gradient.3), channel_id=1, source_target_pairs={{0,16},{16,0},{1,17},{17,1},{2,18},{18,2},{3,19},{19,3},{4,20},{20... | collective-permute-start | bytes 786440 | tf_op jit(solution)/shard_map/ppermute | solution.py:260
  16.6 5.0 %copy-start.7 = (bf16[256,512]{1,0:T(8,128)(2,1)}, bf16[256,512]{1,0:T(8,128)(2,1)S(1)}, u32[]{:S(2)}) copy-start(bf16[256,512]{1,0:T(8,128)(2,1)S(1)} %collective-permute-done.refs_0_) | copy-start | bytes 786436
  17.4 11.9 %collective-permute-start.8 = (bf16[256,512]{1,0:T(8,128)(2,1)S(1)}, bf16[256,512]{1,0:T(8,128)(2,1)S(1)}, u32[]{:S(2)}, u32[]{:S(2)}) collective-permute-start(bf16[256,512]{1,0:T(8,128)(2,1)S(1)} %next_working.2.refs_0_), channel_id=1, source_target_pairs={{0,12},{1,13},{2,14},{3,15},{4,8},{5,9},{6,10},{7,11},{8,4},{9,5},... | collective-permute-start | bytes 786440 | tf_op jit(solution)/shard_map/ppermute | solution.py:283
  23.3 15.9 %collective-permute-start.9 = (bf16[256,512]{1,0:T(8,128)(2,1)S(1)}, bf16[256,512]{1,0:T(8,128)(2,1)}, u32[]{:S(2)}, u32[]{:S(2)}) collective-permute-start(bf16[256,512]{1,0:T(8,128)(2,1)S(1)} %next_working.3.refs_1_), channel_id=1, source_target_pairs={{0,12},{1,13},{2,14},{3,15},{4,8},{5,9},{6,10},{7,11},{8,4},{9,5},... | collective-permute-start | bytes 786440 | tf_op jit(solution)/shard_map/ppermute | solution.py:283
  27.2 29.8 %collective-permute-start.2 = (bf16[192,2048]{1,0:T(8,128)(2,1)}, bf16[192,2048]{1,0:T(8,128)(2,1)}, u32[]{:S(2)}, u32[]{:S(2)}) collective-permute-start(bf16[192,2048]{1,0:T(8,128)(2,1)} %get-tuple-element.15), channel_id=1, source_target_pairs={{0,1},{1,0},{2,3},{3,2},{4,5},{5,4},{6,7},{7,6},{8,9},{9,8},{10,11... | collective-permute-start | bytes 2359304 | tf_op jit(solution)/shard_map/ppermute | solution.py:273
  27.2 31.4 %collective-permute-start.3 = (bf16[192,2048]{1,0:T(8,128)(2,1)}, bf16[192,2048]{1,0:T(8,128)(2,1)}, u32[]{:S(2)}, u32[]{:S(2)}) collective-permute-start(bf16[192,2048]{1,0:T(8,128)(2,1)} %get-tuple-element.16), channel_id=1, source_target_pairs={{0,2},{1,3},{2,0},{3,1},{4,6},{5,7},{6,4},{7,5},{8,10},{9,11},{10,... | collective-permute-start | bytes 2359304 | tf_op jit(solution)/shard_map/ppermute | solution.py:271
  28.8 35.6 %collective-permute-start.5 = (bf16[192,2048]{1,0:T(8,128)(2,1)}, bf16[192,2048]{1,0:T(8,128)(2,1)}, u32[]{:S(2)}, u32[]{:S(2)}) collective-permute-start(bf16[192,2048]{1,0:T(8,128)(2,1)} %collective-permute-done.4), channel_id=1, source_target_pairs={{0,2},{1,3},{2,0},{3,1},{4,6},{5,7},{6,4},{7,5},{8,10},{9,11},{10,... | collective-permute-start | bytes 2359304 | tf_op jit(solution)/shard_map/ppermute | solution.py:274
  29.3 14.8 %collective-permute-start.6 = (bf16[256,512]{1,0:T(8,128)(2,1)S(1)}, bf16[256,512]{1,0:T(8,128)(2,1)S(1)}, u32[]{:S(2)}, u32[]{:S(2)}) collective-permute-start(bf16[256,512]{1,0:T(8,128)(2,1)S(1)} %next_working.2.refs_0_), channel_id=1, source_target_pairs={{0,4},{1,5},{2,6},{3,7},{4,0},{5,1},{6,2},{7,3},{8,12},{9,13},{10,... | collective-permute-start | bytes 786440 | tf_op jit(solution)/shard_map/ppermute | solution.py:284
  39.3 11.9 %collective-permute-start.7 = (bf16[256,512]{1,0:T(8,128)(2,1)S(1)}, bf16[256,512]{1,0:T(8,128)(2,1)S(1)}, u32[]{:S(2)}, u32[]{:S(2)}) collective-permute-start(bf16[256,512]{1,0:T(8,128)(2,1)S(1)} %next_working.3.refs_1_), channel_id=1, source_target_pairs={{0,4},{1,5},{2,6},{3,7},{4,0},{5,1},{6,2},{7,3},{8,12},{9,13},{10,... | collective-permute-start | bytes 786440 | tf_op jit(solution)/shard_map/ppermute | solution.py:284
  44.1 21.9 %collective-permute-start.10 = (bf16[256,512]{1,0:T(8,128)(2,1)S(1)}, bf16[256,512]{1,0:T(8,128)(2,1)S(1)}, u32[]{:S(2)}, u32[]{:S(2)}) collective-permute-start(bf16[256,512]{1,0:T(8,128)(2,1)S(1)} %broadcast_select_fusion.1), channel_id=1, source_target_pairs={{0,8},{1,9},{2,10},{3,11},{4,0},{5,1},{6,2},{7,3},{8,12},{9,13},{1... | collective-permute-start | bytes 786440 | tf_op jit(solution)/shard_map/ppermute | solution.py:286
  51.2 14.8 %collective-permute-start.11 = (bf16[256,512]{1,0:T(8,128)(2,1)S(1)}, bf16[256,512]{1,0:T(8,128)(2,1)S(1)}, u32[]{:S(2)}, u32[]{:S(2)}) collective-permute-start(bf16[256,512]{1,0:T(8,128)(2,1)S(1)} %broadcast_select_fusion), channel_id=1, source_target_pairs={{0,8},{1,9},{2,10},{3,11},{4,0},{5,1},{6,2},{7,3},{8,12},{9,13},{1... | collective-permute-start | bytes 786440 | tf_op jit(solution)/shard_map/ppermute | solution.py:286
  54.4 1.1 %copy-start.5 = (bf16[192,2048]{1,0:T(8,128)(2,1)S(1)}, bf16[192,2048]{1,0:T(8,128)(2,1)}, u32[]{:S(2)}) copy-start(bf16[192,2048]{1,0:T(8,128)(2,1)} %copy-done.4) | copy-start | bytes 2359300
  58.6 7.4 %copy-start.6 = (bf16[192,2048]{1,0:T(8,128)(2,1)S(1)}, bf16[192,2048]{1,0:T(8,128)(2,1)}, u32[]{:S(2)}) copy-start(bf16[192,2048]{1,0:T(8,128)(2,1)} %copy-done.4) | copy-start | bytes 2359300
  66.0 5.8 %copy-start.8 = (bf16[256,512]{1,0:T(8,128)(2,1)S(1)}, bf16[256,512]{1,0:T(8,128)(2,1)}, u32[]{:S(2)}) copy-start(bf16[256,512]{1,0:T(8,128)(2,1)} %copy-done.7) | copy-start | bytes 786436
  67.8 2.4 %collective-permute-start.12 = (f32[384,512]{1,0:T(8,128)S(1)}, f32[384,512]{1,0:T(8,128)S(1)}, u32[]{:S(2)}, u32[]{:S(2)}) collective-permute-start(f32[384,512]{1,0:T(8,128)S(1)} %get-tuple-element.19), channel_id=1, source_target_pairs={{0,1},{1,0},{2,3},{3,2},{4,5},{5,4},{6,7},{7,6},{8,9},{9,8},{10,11... | collective-permute-start | bytes 2359304 | tf_op jit(solution)/shard_map/ppermute | solution.py:299
  70.2 7.0 %collective-permute-start.13 = (bf16[192,512]{1,0:T(8,128)(2,1)S(1)}, bf16[192,512]{1,0:T(8,128)(2,1)S(1)}, u32[]{:S(2)}, u32[]{:S(2)}) collective-permute-start(bf16[192,512]{1,0:T(8,128)(2,1)S(1)} %over_core.1), channel_id=1, source_target_pairs={{0,2},{1,3},{2,0},{3,1},{4,6},{5,7},{6,4},{7,5},{8,10},{9,11},{10,... | collective-permute-start | bytes 589832 | tf_op jit(solution)/shard_map/ppermute | solution.py:300

commit v3 on v2

v3 whole, which is shorter than its diff:
```python
import functools

import jax
import jax.numpy as jnp
from jax import lax
from jax.experimental import pallas as pl
from jax.experimental.pallas import tpu as pltpu
from jax.sharding import PartitionSpec as P

outer_rate = 0.7
momentum_decay = 0.9
PLANE = 4
FIRST = 8
HBM = pl.BlockSpec(memory_space=pltpu.HBM)
SMEM = pl.BlockSpec(memory_space=pltpu.SMEM)
LARGE = pltpu.CompilerParams(vmem_limit_bytes=60 * 2**20)
SMALL = pltpu.CompilerParams(vmem_limit_bytes=16 * 2**20)


def cost(us):
    return pl.CostEstimate(flops=int(us * 1_153_000_000), bytes_accessed=0, transcendentals=0)


COST = dict(add_keys=1, pick=3)


def plane_pairs(size, bit):
    return [(i, i ^ bit) for i in range(size)]


def line_pairs(size, to):
    return [(i, to[i // PLANE] * PLANE + i % PLANE) for i in range(size)]


def whole(array):
    return pl.BlockSpec(array.shape, lambda *_: (0,) * array.ndim)


def arrange_body(width, distances, order, tokens, *refs):
    count = len(distances)
    outs, held, (arrived, left) = refs[:count], refs[count : 2 * count], refs[2 * count :]
    blocks = outs[0].shape[1] // width
    copies = []
    for i, distance in enumerate(distances):
        for k in range(blocks):
            start = pl.multiple_of(order[k * PLANE + distance] * width, width)
            copies.append(
                pltpu.make_async_copy(
                    tokens.at[:, pl.ds(start, width)],
                    held[i].at[:, pl.ds(k * width, width)],
                    arrived.at[i * blocks + k],
                )
            )
    for copy in copies:
        copy.start()
    away = [pltpu.make_async_copy(held[i], outs[i], left.at[i]) for i in range(count)]
    for i in range(count):
        for k in range(blocks):
            copies[i * blocks + k].wait()
        away[i].start()
    for copy in away:
        copy.wait()


def arrange_tokens(tokens, order, width, distances):
    blocks = order.shape[0] // PLANE
    shape = (tokens.shape[0], blocks * width)
    return pl.pallas_call(
        functools.partial(arrange_body, width, distances),
        grid=(1,),
        in_specs=[SMEM, HBM],
        out_specs=[HBM] * len(distances),
        out_shape=[jax.ShapeDtypeStruct(shape, tokens.dtype)] * len(distances),
        scratch_shapes=[pltpu.VMEM(shape, tokens.dtype)] * len(distances)
        + [pltpu.SemaphoreType.DMA((blocks * len(distances),)), pltpu.SemaphoreType.DMA((len(distances),))],
        cost_estimate=cost(0),
        compiler_params=LARGE,
        name="arrange_tokens",
    )(order, tokens)


def mixing_body(groups, own_group, partners, mix_weights, row):
    me = own_group[0]
    numerators = [mix_weights[me, j].astype(jnp.float32) for j in range(5)]
    total = sum(numerators)

    def coefficient(group):
        found = jnp.where(group == me, numerators[0], 0.0)
        for j in range(4):
            found = found + jnp.where(partners[me, j] == group, numerators[j + 1], 0.0)
        return jnp.full((1, row.shape[1]), found / total, jnp.float32)

    row[0:1] = coefficient(me)
    if groups == 2:
        row[1:2] = coefficient(1 - me)
    else:
        for g in range(groups):
            row[g + 1 : g + 2] = jnp.where(g == me, 0.0, coefficient(g))


def mixing_row(groups, *scalars):
    shape = (-(-(groups + 1) // 8) * 8, 128)
    row = pl.pallas_call(
        functools.partial(mixing_body, groups),
        grid=(1,),
        in_specs=[SMEM] * 3,
        out_specs=pl.BlockSpec(shape, lambda *_: (0, 0)),
        out_shape=jax.ShapeDtypeStruct(shape, jnp.float32),
        cost_estimate=cost(0),
        compiler_params=SMALL,
        name="mixing_row",
    )(*scalars)
    return row[:, 0]


def delta_body(starts, master, working, *refs):
    outs, (master_here, working_here, arrived) = refs[:-3], refs[-3:]
    copies = []
    for i, (start, out) in enumerate(zip(starts, outs)):
        part = pl.ds(start, out.shape[0])
        copies.append(
            [
                pltpu.make_async_copy(there.at[part], here.at[part], arrived.at[i, j])
                for j, (there, here) in enumerate([(master, master_here), (working, working_here)])
            ]
        )
    for copy in sum(copies, []):
        copy.start()
    for start, out, pair in zip(starts, outs, copies):
        part = slice(start, start + out.shape[0])
        for copy in pair:
            copy.wait()
        out[...] = (master_here[part] - working_here[part].astype(jnp.float32)).astype(out.dtype)


def pseudo_gradient(master, working, cuts):
    shapes = [(size, master.shape[1]) for _, size in cuts]
    return pl.pallas_call(
        functools.partial(delta_body, [start for start, _ in cuts]),
        grid=(1,),
        in_specs=[HBM, HBM],
        out_specs=[pl.BlockSpec(shape, lambda *_: (0, 0)) for shape in shapes],
        out_shape=[jax.ShapeDtypeStruct(shape, jnp.bfloat16) for shape in shapes],
        scratch_shapes=[
            pltpu.VMEM(master.shape, master.dtype),
            pltpu.VMEM(working.shape, working.dtype),
            pltpu.SemaphoreType.DMA((len(cuts), 2)),
        ],
        cost_estimate=cost(0),
        compiler_params=LARGE,
        name="pseudo_gradient",
    )(master, working)


def outer_step(row, master, momentum, working, received):
    mixed = row[0] * (master - working.astype(jnp.float32))
    for i, other in enumerate(received):
        mixed = mixed + row[i + 1] * other.astype(jnp.float32)
    new_momentum = momentum_decay * momentum + mixed
    new_master = master - outer_rate * (mixed + momentum_decay * new_momentum)
    return new_master, new_momentum


def after(value, *others):
    return lax.optimization_barrier((value, *others))[0]


def product(tokens, pieces, offsets):
    total = None
    for piece, offset in zip(pieces, offsets):
        term = jnp.dot(
            tokens[:, offset : offset + piece.shape[0]], piece[...], preferred_element_type=jnp.float32
        )
        total = term if total is None else total + term
    return total


def early_body(offsets, tokens, *refs):
    refs[-1][...] = product(tokens, refs[:-1], offsets)


def early_keys(tokens, pieces, offsets):
    span = max(o + p.shape[0] for o, p in zip(offsets, pieces))
    rows, width = tokens.shape[0], pieces[0].shape[1]
    return pl.pallas_call(
        functools.partial(early_body, offsets),
        grid=(1,),
        in_specs=[pl.BlockSpec((rows, span), lambda *_: (0, 0))] + [whole(p) for p in pieces],
        out_specs=pl.BlockSpec((rows, width), lambda *_: (0, 0)),
        out_shape=jax.ShapeDtypeStruct((rows, width), jnp.float32),
        cost_estimate=cost(0),
        compiler_params=SMALL,
        name="early_keys",
    )(tokens, *pieces)


def last_block(tokens, width):
    rows, span = tokens.shape
    return pl.BlockSpec((rows, width), lambda *_: (0, span // width - 1))


def add_body(offset, *refs):
    tokens, sums, piece, outs = refs[:PLANE], refs[PLANE : 2 * PLANE], refs[2 * PLANE], refs[-PLANE:]
    for t, s, o in zip(tokens, sums, outs):
        o[...] = s[...] + product(t, [piece], [offset])


def add_keys(tokens, sums, width, piece, offset):
    rows, columns = sums[0].shape
    return pl.pallas_call(
        functools.partial(add_body, offset),
        grid=(1,),
        in_specs=[last_block(t, width) for t in tokens] + [whole(a) for a in (*sums, piece)],
        out_specs=[whole(s) for s in sums],
        out_shape=[jax.ShapeDtypeStruct((rows, columns), jnp.float32)] * PLANE,
        cost_estimate=cost(COST["add_keys"]),
        compiler_params=SMALL,
        name="add_keys",
    )(*tokens, *sums, piece)


def pick_body(own_first, own, passed, *refs):
    @pl.when(own_first[0] == 1)
    def _():
        refs[-1][...] = own[...]

    @pl.when(own_first[0] == 0)
    def _():
        refs[-1][...] = passed[...]


def pick(own_first, own, passed):
    return pl.pallas_call(
        pick_body,
        grid=(1,),
        in_specs=[SMEM, whole(own), whole(passed)],
        out_specs=whole(own),
        out_shape=jax.ShapeDtypeStruct(own.shape, own.dtype),
        cost_estimate=cost(COST["pick"]),
        compiler_params=SMALL,
        name="pick",
    )(own_first, own, passed)


def late_body(offset, *refs):
    tokens, sums, piece, (keep, keep_y, to_core) = refs[:PLANE], refs[PLANE:-4], refs[-4], refs[-3:]
    own, from_core, from_y, from_both = [s[...] + product(t, [piece], [offset]) for t, s in zip(tokens, sums)]
    count = keep.shape[0]
    to_core[:count] = from_core
    to_core[count:] = from_both
    keep[...] = own
    keep_y[...] = from_y


def late_keys(tokens, sums, width, piece, offset):
    rows, columns = sums[0].shape
    one = jax.ShapeDtypeStruct((rows, columns), jnp.float32)
    two = jax.ShapeDtypeStruct((2 * rows, columns), jnp.float32)
    return pl.pallas_call(
        functools.partial(late_body, offset),
        grid=(1,),
        in_specs=[last_block(t, width) for t in tokens] + [whole(a) for a in (*sums, piece)],
        out_specs=[whole(one), whole(one), whole(two)],
        out_shape=[one, one, two],
        cost_estimate=cost(0),
        compiler_params=SMALL,
        name="late_keys",
    )(*tokens, *sums, piece)


def over_core_body(keep_y, back, to_y):
    to_y[...] = (keep_y[...] + back[...]).astype(to_y.dtype)


def over_core(keep_y, back):
    rows, width = keep_y.shape
    return pl.pallas_call(
        over_core_body,
        grid=(1,),
        in_specs=[whole(keep_y), pl.BlockSpec((rows, width), lambda *_: (1, 0))],
        out_specs=whole(keep_y),
        out_shape=jax.ShapeDtypeStruct((rows, width), jnp.bfloat16),
        cost_estimate=cost(0),
        compiler_params=SMALL,
        name="over_core",
    )(keep_y, back)


def over_y_body(keep, back, there, keys):
    keys[...] = (keep[...] + back[...] + there[...].astype(jnp.float32)).astype(keys.dtype)


def over_y(keep, back, there):
    rows, width = keep.shape
    return pl.pallas_call(
        over_y_body,
        grid=(1,),
        in_specs=[whole(keep), pl.BlockSpec((rows, width), lambda *_: (0, 0)), whole(there)],
        out_specs=whole(keep),
        out_shape=jax.ShapeDtypeStruct((rows, width), jnp.bfloat16),
        cost_estimate=cost(0),
        compiler_params=SMALL,
        name="over_y",
    )(keep, back, there)


def shards(master, momentum, working, tokens, partners, mix_weights):
    groups = lax.axis_size("replica")
    size = lax.axis_size("fsdp")
    line = size // PLANE
    place = lax.axis_index("fsdp")
    master, momentum, working, tokens = master[0], momentum[0], working[0], tokens[0]
    rows = master.shape[0]
    first = rows * FIRST // 16
    cuts = [(0, first), (first, rows - first)]
    parts = [slice(start, start + count) for start, count in cuts]

    deltas = pseudo_gradient(master, working, cuts)
    received = []
    for delta in deltas:
        if groups == 2:
            received.append([lax.ppermute(delta, "replica", [(0, 1), (1, 0)])])
        else:
            every = lax.all_gather(delta, "replica", axis=0)
            received.append([every[g] for g in range(groups)])
    row = mixing_row(groups, lax.axis_index("replica").astype(jnp.int32)[None], partners, mix_weights)

    if line == 4:
        order = [place ^ (k * PLANE + d) for k in (0, 1, 3, 2) for d in range(PLANE)]
    else:
        order = [((place % PLANE) ^ d) + k * PLANE for k in range(line) for d in range(PLANE)]
    order = after(jnp.stack(order).astype(jnp.int32), *deltas)
    for_y, for_both, for_core, own = arrange_tokens(tokens, order, rows, [2, 3, 1, 0])
    from_y = lax.ppermute(for_y, "fsdp", plane_pairs(size, 2))
    at_core = lax.ppermute(for_both, "fsdp", plane_pairs(size, 1))
    from_core = lax.ppermute(for_core, "fsdp", plane_pairs(size, 1))

    fresh = []
    for part, there in zip(parts, received):
        there = [after(t, *fresh) for t in there]
        new_master, _ = outer_step(row, master[part], momentum[part], working[part], there)
        fresh.append(new_master.astype(jnp.bfloat16))
    if line == 4:
        z = place // PLANE
        own_first = jnp.where((z == 1) | (z == 2), 0, 1).astype(jnp.int32)[None]
        far = [lax.ppermute(f, "fsdp", line_pairs(size, [3, 2, 1, 0])) for f in fresh]
        ready = [after(fresh[0], at_core, from_core), fresh[1]]
        near = [lax.ppermute(f, "fsdp", line_pairs(size, [1, 0, 3, 2])) for f in ready]
        passed = [far[0], far[1]]
        last = [
            lax.ppermute(pick(own_first, f, g), "fsdp", line_pairs(size, [2, 0, 3, 1]))
            for f, g in zip(fresh, passed)
        ]
        blocks = [fresh, near, far, last]
    else:
        lines = [[k * PLANE + p for k in range(line)] for p in range(PLANE)]
        every = [lax.all_gather(f, "fsdp", axis=0, axis_index_groups=lines) for f in fresh]
        blocks = [[e[k] for e in every] for k in range(line)]

    from_both = lax.ppermute(after(at_core, from_y, from_core), "fsdp", plane_pairs(size, 2))
    inputs = [own, from_core, from_y, from_both]

    early = [piece for block in blocks[:-1] for piece in block]
    offsets = [k * rows + start for k in range(line - 1) for start, _ in cuts]
    sums = [early_keys(t, early, offsets) for t in inputs]
    sums = add_keys(inputs, sums, rows, blocks[-1][0], cuts[0][0])
    keep, keep_y, to_core = late_keys(inputs, sums, rows, blocks[-1][1], cuts[1][0])
    back = lax.ppermute(to_core, "fsdp", plane_pairs(size, 1))
    there = lax.ppermute(over_core(keep_y, back), "fsdp", plane_pairs(size, 2))
    keys = over_y(keep, back, there)

    received = [after(jnp.concatenate(list(r)), keep) for r in zip(*received)]
    new_master, new_momentum = outer_step(row, master, momentum, working, received)
    return new_master[None], new_momentum[None], keys[None]


def solution(mesh):
    return jax.shard_map(
        shards,
        mesh=mesh,
        in_specs=(
            P("replica", "fsdp", None),
            P("replica", "fsdp", None),
            P("replica", "fsdp", None),
            P("replica", "fsdp", None),
            P(),
            P(),
        ),
        out_specs=(
            P("replica", "fsdp", None),
            P("replica", "fsdp", None),
            P("replica", "fsdp", None),
        ),
        check_vma=False,
    )
```

time: 78.3 us -> 65.7 us (0.84)
  other arithmetic: 0.07 us -> 8.87 us
  Pallas kernels: 17.2 us -> 10.1 us
  waiting for transfers between devices: 18.4 us -> 12 us
  starting transfers between devices: 37.4 us -> 32.4 us
  local copies, waits for them, and re-layouts: 4.02 us -> 1.19 us
    ppermute x2, starting transfers between devices: 14.7 us -> 0.01 us  [shards(): lax.ppermute(f, 'fsdp', line_pairs(size, [1, 0, 3, 2]))]
    ppermute x3, starting transfers between devices: 8.46 us -> 18.8 us  [the longest x2 17.3 us: shards(): lax.ppermute(pick(own_first, f, g), 'fsdp', line_pairs(size, [2, 0, 3, 1]))]
    ppermute x2, waiting for transfers between devices: 6.95 us -> 0.52 us  [shards(): received.append([lax.ppermute(delta, 'replica', [(0, 1), (1, 0)])])]
    convert_element_type x0 -> x2, other arithmetic: none -> 4.97 us  [shards(): fresh.append(new_master.astype(jnp.bfloat16))]
    pallas_call x4, Pallas kernels: 6.3 us -> 1.88 us  [early_keys(): pl.pallas_call(functools.partial(early_body, offsets), grid=(1,), in_spec...]
    unnamed x22 -> x12, local copies, waits for them, and re-layouts: 3.93 us -> 0.02 us
    ppermute x1, waiting for transfers between devices: 0.01 us -> 3.69 us  [shards(): from_y = lax.ppermute(for_y, 'fsdp', plane_pairs(size, 2))]
    broadcast_in_dim x0 -> x1, other arithmetic: none -> 2.92 us  [shards(): return (new_master[None], new_momentum[None], keys[None])]
  transfers between devices with their start and end apart: 14 -> 14, of which waited for: 6 -> 6; matrix products, arithmetic and copies ran while one was open for 0% -> 15% of each run, Pallas kernels for 15% -> 10%
where the time goes in v3:
time: 65.7 us; the launch traced here: 65.4 us
  starting transfers between devices  32.4 us (49%)
  waiting for transfers between devices  12 us (18%)
  Pallas kernels  10.1 us (15%)
  other arithmetic  8.87 us (14%)
  local copies, waits for them, and re-layouts  1.19 us (2%)
  between operations  0.82 us (1%)
    ppermute x2, starting transfers between devices, shards(): lax.ppermute(pick(own_first, f, g), 'fsdp', line_pairs(size, [2, 0, 3, 1]))  17.3 us
    ppermute x2, starting transfers between devices, shards(): lax.ppermute(f, 'fsdp', line_pairs(size, [3, 2, 1, 0]))  7.33 us
    convert_element_type x2, other arithmetic, shards(): fresh.append(new_master.astype(jnp.bfloat16))  4.97 us
    pallas_call x1, Pallas kernels, arrange_tokens(): pl.pallas_call(functools.partial(arrange_body, width, distances), grid=(1...  3.72 us
    ppermute x1, waiting for transfers between devices, shards(): from_y = lax.ppermute(for_y, 'fsdp', plane_pairs(size, 2))  3.69 us
    ppermute x2, starting transfers between devices, shards(): received.append([lax.ppermute(delta, 'replica', [(0, 1), (1, 0)])])  3.54 us
    ppermute x1, waiting for transfers between devices, shards(): there = lax.ppermute(over_core(keep_y, back), 'fsdp', plane_pairs(size, 2))  3.51 us
    broadcast_in_dim x1, other arithmetic, shards(): return (new_master[None], new_momentum[None], keys[None])  2.92 us
  transfers between devices with their start and end apart: 14, of which 6 were waited for; matrix products, arithmetic and copies ran while one was open for 15% of the time, Pallas kernels for 10%

profile of v3, /device:TPU:0, one launch (start us, length us, event | category | flops | bytes accessed | tf_op | source)
XLA Modules:
  0.0 65.4 jit_solution(16184015397252478256)
XLA Ops:
  0.6 0.0 copy-start.3
  0.6 0.0 copy-start.4
  0.7 0.0 copy-start.1
  0.7 0.0 copy-start.2
  0.7 2.3 %pseudo_gradient.1 = (bf16[256,512]{1,0:T(8,128)(2,1)}, bf16[256,512]{1,0:T(8,128)(2,1)}) custom-call(f32[512,512]{1,0:T(8,128)} %bitcast.72, bf16[512,512]{1,0:T(8,128)(2,1)} %bitcast.73), custom_call_target="tpu_custom_call" | custom-call | tf_op jit(solution)/shard_map/pseudo_gradient/pallas_call | solution.py:138
  3.0 3.0 %collective-permute-start = (bf16[256,512]{1,0:T(8,128)(2,1)}, bf16[256,512]{1,0:T(8,128)(2,1)S(1)}, u32[]{:S(2)}, u32[]{:S(2)}) collective-permute-start(bf16[256,512]{1,0:T(8,128)(2,1)} %get-tuple-element.21), channel_id=1, source_target_pairs={{0,16},{16,0},{1,17},{17,1},{2,18},{18,2},{3,19},{19,3},{4,20},{20... | collective-permute-start | bytes 786440 | tf_op jit(solution)/shard_map/ppermute | solution.py:322
  6.0 0.6 stack.67.order
  6.6 3.7 %arrange_tokens.1 = (bf16[192,2048]{1,0:T(8,128)(2,1)}, bf16[192,2048]{1,0:T(8,128)(2,1)}, bf16[192,2048]{1,0:T(8,128)(2,1)}, bf16[192,2048]{1,0:T(8,128)(2,1)}) custom-call(s32[16]{0:T(128)} %stack.67.order, bf16[192,8192]{1,0:T(8,128)(2,1)} %bitcast.74), custom_call_target="tpu_custom_call" | custom-call | tf_op jit(solution)/shard_map/arrange_tokens/pallas_call | solution.py:68
  10.3 0.1 collective-permute-start.2
  10.4 0.5 collective-permute-start.4
  10.9 1.5 %collective-permute-start.3 = (bf16[192,2048]{1,0:T(8,128)(2,1)}, bf16[192,2048]{1,0:T(8,128)(2,1)S(1)}, u32[]{:S(2)}, u32[]{:S(2)}) collective-permute-start(bf16[192,2048]{1,0:T(8,128)(2,1)} %get-tuple-element.26), channel_id=1, source_target_pairs={{0,2},{1,3},{2,0},{3,1},{4,6},{5,7},{6,4},{7,5},{8,10},{9,11},{10,... | collective-permute-start | bytes 2359304 | tf_op jit(solution)/shard_map/ppermute | solution.py:334
  12.4 0.5 collective-permute-start.1
  13.0 0.0 copy-done.1
  13.0 0.0 copy-done.2
  13.0 0.6 mixing_row.1
  13.6 0.5 fusion.15
  14.1 0.0 collective-permute-done
  14.1 0.0 copy-done.3
  14.1 0.0 copy-done.4
  14.1 2.4 %fusion.14.refs_0_.own = bf16[256,512]{1,0:T(8,128)(2,1)S(1)} fusion(f32[1,512,512]{2,1,0:T(8,128)} %param.7, bf16[256,512]{1,0:T(8,128)(2,1)S(1)} %collective-permute-done, f32[1,512,512]{2,1,0:T(8,128)S(1)} %copy-done.3, f32[]{:T(128)} %bitcast.4, bf16[1,512,512]{2,1,0:T(8,128)(2,1)S(1)} %copy-done.4, f32[]{:T(128)} %bitcast.2), kind=kLoop, calls=%fused_computation.22 | loop fusion | flops 1703936 | bytes 1835016 | tf_op jit(solution)/shard_map/convert_element_type | solution.py:342
  16.6 3.7 %collective-permute-start.8 = (bf16[256,512]{1,0:T(8,128)(2,1)S(1)}, bf16[256,512]{1,0:T(8,128)(2,1)S(1)}, u32[]{:S(2)}, u32[]{:S(2)}) collective-permute-start(bf16[256,512]{1,0:T(8,128)(2,1)S(1)} %fusion.14.refs_0_.own), channel_id=1, source_target_pairs={{0,12},{1,13},{2,14},{3,15},{4,8},{5,9},{6,10},{7,11},{8,4},{9,5},... | collective-permute-start | bytes 786440 | tf_op jit(solution)/shard_map/ppermute | solution.py:346
  20.2 0.5 collective-permute-done.1
  20.8 2.5 %fusion.9.refs_1_.own = bf16[256,512]{1,0:T(8,128)(2,1)S(1)} fusion(f32[1,512,512]{2,1,0:T(8,128)} %param.7, bf16[256,512]{1,0:T(8,128)(2,1)} %collective-permute-done.1, f32[1,512,512]{2,1,0:T(8,128)S(1)} %copy-done.3, bf16[1,512,512]{2,1,0:T(8,128)(2,1)S(1)} %copy-done.4, f32[]{:T(128)} %bitcast.4, f32[]{:T(128)} %bitcast.2), kind=kLoop, calls=%fused_computation.16 | loop fusion | flops 1703936 | bytes 1835016 | tf_op jit(solution)/shard_map/convert_element_type | solution.py:342
  23.3 3.7 %collective-permute-start.9 = (bf16[256,512]{1,0:T(8,128)(2,1)S(1)}, bf16[256,512]{1,0:T(8,128)(2,1)S(1)}, u32[]{:S(2)}, u32[]{:S(2)}) collective-permute-start(bf16[256,512]{1,0:T(8,128)(2,1)S(1)} %fusion.9.refs_1_.own), channel_id=1, source_target_pairs={{0,12},{1,13},{2,14},{3,15},{4,8},{5,9},{6,10},{7,11},{8,4},{9,5},... | collective-permute-start | bytes 786440 | tf_op jit(solution)/shard_map/ppermute | solution.py:346
  27.0 0.0 collective-permute-done.2.tokens.refs_1_
  27.0 0.0 collective-permute-start.7
  27.0 0.0 collective-permute-done.4
  27.0 3.7 %collective-permute-done.3.tokens.refs_2_ = bf16[192,2048]{1,0:T(8,128)(2,1)S(1)} collective-permute-done((bf16[192,2048]{1,0:T(8,128)(2,1)}, bf16[192,2048]{1,0:T(8,128)(2,1)S(1)}, u32[]{:S(2)}, u32[]{:S(2)}) %collective-permute-start.3) | collective-permute-done | bytes 786464 | tf_op jit(solution)/shard_map/ppermute | solution.py:334
  30.7 1.5 %collective-permute-start.5 = (bf16[192,2048]{1,0:T(8,128)(2,1)}, bf16[192,2048]{1,0:T(8,128)(2,1)S(1)}, u32[]{:S(2)}, u32[]{:S(2)}) collective-permute-start(bf16[192,2048]{1,0:T(8,128)(2,1)} %collective-permute-done.4), channel_id=1, source_target_pairs={{0,2},{1,3},{2,0},{3,1},{4,6},{5,7},{6,4},{7,5},{8,10},{9,11},{10,... | collective-permute-start | bytes 2359304 | tf_op jit(solution)/shard_map/ppermute | solution.py:360
  32.2 0.0 collective-permute-done.8.refs_4_.passed
  32.2 7.6 %collective-permute-start.10 = (bf16[256,512]{1,0:T(8,128)(2,1)S(1)}, bf16[256,512]{1,0:T(8,128)(2,1)S(1)}, u32[]{:S(2)}, u32[]{:S(2)}) collective-permute-start(bf16[256,512]{1,0:T(8,128)(2,1)S(1)} %pick.2), channel_id=1, source_target_pairs={{0,8},{1,9},{2,10},{3,11},{4,0},{5,1},{6,2},{7,3},{8,12},{9,13},{1... | collective-permute-start | bytes 786440 | tf_op jit(solution)/shard_map/ppermute | solution.py:351
  39.8 0.0 collective-permute-start.6
  39.8 0.0 collective-permute-done.9.refs_5_.passed
  39.8 0.0 copy-start
  39.8 9.7 %collective-permute-start.11 = (bf16[256,512]{1,0:T(8,128)(2,1)S(1)}, bf16[256,512]{1,0:T(8,128)(2,1)S(1)}, u32[]{:S(2)}, u32[]{:S(2)}) collective-permute-start(bf16[256,512]{1,0:T(8,128)(2,1)S(1)} %pick.3), channel_id=1, source_target_pairs={{0,8},{1,9},{2,10},{3,11},{4,0},{5,1},{6,2},{7,3},{8,12},{9,13},{1... | collective-permute-start | bytes 786440 | tf_op jit(solution)/shard_map/ppermute | solution.py:351
  49.5 0.0 collective-permute-done.7.refs_3_
  49.5 1.4 %collective-permute-done.6.refs_2_ = bf16[256,512]{1,0:T(8,128)(2,1)S(1)} collective-permute-done((bf16[256,512]{1,0:T(8,128)(2,1)S(1)}, bf16[256,512]{1,0:T(8,128)(2,1)S(1)}, u32[]{:S(2)}, u32[]{:S(2)}) %collective-permute-start.6) | collective-permute-done | bytes 262176 | tf_op jit(solution)/shard_map/ppermute | solution.py:348
  51.0 0.5 early_keys.6.refs_6_
  51.4 0.5 early_keys.5.refs_5_
  51.9 0.0 copy-done
  51.9 0.5 early_keys.4.refs_4_
  52.4 0.0 collective-permute-done.5.tokens.refs_3_
  52.4 0.5 early_keys.7.refs_7_
  52.9 0.0 collective-permute-done.10.refs_8_
  52.9 0.4 add_keys.1
  53.3 1.6 %collective-permute-done.11.refs_8_ = bf16[256,512]{1,0:T(8,128)(2,1)S(1)} collective-permute-done((bf16[256,512]{1,0:T(8,128)(2,1)S(1)}, bf16[256,512]{1,0:T(8,128)(2,1)S(1)}, u32[]{:S(2)}, u32[]{:S(2)}) %collective-permute-start.11) | collective-permute-done | bytes 262176 | tf_op jit(solution)/shard_map/ppermute | solution.py:351
  54.9 0.0 copy-start.5
  54.9 0.4 late_keys.1
  55.2 0.1 collective-permute-start.12
  55.3 1.0 %pad_maximum_fusion = bf16[512,512]{1,0:T(8,128)(2,1)S(1)} fusion(bf16[256,512]{1,0:T(8,128)(2,1)} %collective-permute-done.1, bf16[256,512]{1,0:T(8,128)(2,1)S(1)} %collective-permute-done), kind=kLoop, calls=%fused_computation.4 | loop fusion | flops 1048576 | bytes 1048576 | tf_op jit(solution)/shard_map/concatenate | solution.py:372
  56.3 1.3 %collective-permute-done.12.back = f32[384,512]{1,0:T(8,128)S(1)} collective-permute-done((f32[384,512]{1,0:T(8,128)S(1)}, f32[384,512]{1,0:T(8,128)S(1)}, u32[]{:S(2)}, u32[]{:S(2)}) %collective-permute-start.12) | collective-permute-done | bytes 786464 | tf_op jit(solution)/shard_map/ppermute | solution.py:368
  57.6 0.1 over_core.1
  57.7 0.6 collective-permute-start.13
  58.2 0.0 copy-done.5
  58.2 2.9 %fusion = (f32[1,512,512]{2,1,0:T(8,128)}, f32[1,512,512]{2,1,0:T(8,128)}) fusion(f32[1,512,512]{2,1,0:T(8,128)S(1)} %copy-done.5, bf16[512,512]{1,0:T(8,128)(2,1)S(1)} %pad_maximum_fusion, f32[]{:T(128)} %bitcast.4, f32[]{:T(128)} %bitcast.2, bf16[1,512,512]{2,1,0:T(8,128)(2,1)S(1)} %copy-done.4, f32[1,512,512]{2,1,0:T(8,128)S(1)} %copy-done.3), kind=kLoop, calls=%fused_computation.3 | loop fusion | flops 3145728 | bytes 5242888 | tf_op jit(solution)/shard_map/broadcast_in_dim | solution.py:374
  61.2 3.5 %collective-permute-done.13.there = bf16[192,512]{1,0:T(8,128)(2,1)S(1)} collective-permute-done((bf16[192,512]{1,0:T(8,128)(2,1)S(1)}, bf16[192,512]{1,0:T(8,128)(2,1)S(1)}, u32[]{:S(2)}, u32[]{:S(2)}) %collective-permute-start.13) | collective-permute-done | bytes 196640 | tf_op jit(solution)/shard_map/ppermute | solution.py:369
  64.7 0.7 %over_y.1 = bf16[192,512]{1,0:T(8,128)(2,1)} custom-call(f32[192,512]{1,0:T(8,128)S(1)} %get-tuple-element.35.keep, f32[384,512]{1,0:T(8,128)S(1)} %collective-permute-done.12.back, bf16[192,512]{1,0:T(8,128)(2,1)S(1)} %collective-permute-done.13.there), custom_call_target="tpu_custom_call" | custom-call | tf_op jit(solution)/shard_map/over_y/pallas_call | solution.py:295
  (2 shorter events, 0.0 us)
Async XLA Ops:
  0.6 13.5 %copy-start.3 = (f32[1,512,512]{2,1,0:T(8,128)S(1)}, f32[1,512,512]{2,1,0:T(8,128)}, u32[]{:S(2)}) copy-start(f32[1,512,512]{2,1,0:T(8,128)} %param.6) | copy-start | bytes 3145732
  0.6 13.5 %copy-start.4 = (bf16[1,512,512]{2,1,0:T(8,128)(2,1)S(1)}, bf16[1,512,512]{2,1,0:T(8,128)(2,1)}, u32[]{:S(2)}) copy-start(bf16[1,512,512]{2,1,0:T(8,128)(2,1)} %param.8) | copy-start | bytes 1572868
  0.7 12.3 %copy-start.1 = (s32[2,4]{1,0:T(2,128)S(1)}, s32[2,4]{1,0:T(2,128)}, u32[]{:S(2)}) copy-start(s32[2,4]{1,0:T(2,128)} %partners.1) | copy-start | bytes 100
  0.7 12.3 %copy-start.2 = (s32[2,5]{1,0:T(2,128)S(1)}, s32[2,5]{1,0:T(2,128)}, u32[]{:S(2)}) copy-start(s32[2,5]{1,0:T(2,128)} %mix_weights.1) | copy-start | bytes 124
  3.0 11.1 %collective-permute-start = (bf16[256,512]{1,0:T(8,128)(2,1)}, bf16[256,512]{1,0:T(8,128)(2,1)S(1)}, u32[]{:S(2)}, u32[]{:S(2)}) collective-permute-start(bf16[256,512]{1,0:T(8,128)(2,1)} %get-tuple-element.21), channel_id=1, source_target_pairs={{0,16},{16,0},{1,17},{17,1},{2,18},{18,2},{3,19},{19,3},{4,20},{20... | collective-permute-start | bytes 786440 | tf_op jit(solution)/shard_map/ppermute | solution.py:322
  10.3 16.6 %collective-permute-start.2 = (bf16[192,2048]{1,0:T(8,128)(2,1)}, bf16[192,2048]{1,0:T(8,128)(2,1)S(1)}, u32[]{:S(2)}, u32[]{:S(2)}) collective-permute-start(bf16[192,2048]{1,0:T(8,128)(2,1)} %get-tuple-element.25), channel_id=1, source_target_pairs={{0,1},{1,0},{2,3},{3,2},{4,5},{5,4},{6,7},{7,6},{8,9},{9,8},{10,11... | collective-permute-start | bytes 2359304 | tf_op jit(solution)/shard_map/ppermute | solution.py:336
  10.4 16.5 %collective-permute-start.4 = (bf16[192,2048]{1,0:T(8,128)(2,1)}, bf16[192,2048]{1,0:T(8,128)(2,1)}, u32[]{:S(2)}, u32[]{:S(2)}) collective-permute-start(bf16[192,2048]{1,0:T(8,128)(2,1)} %get-tuple-element.27), channel_id=1, source_target_pairs={{0,1},{1,0},{2,3},{3,2},{4,5},{5,4},{6,7},{7,6},{8,9},{9,8},{10,11... | collective-permute-start | bytes 2359304 | tf_op jit(solution)/shard_map/ppermute | solution.py:335
  10.9 19.7 %collective-permute-start.3 = (bf16[192,2048]{1,0:T(8,128)(2,1)}, bf16[192,2048]{1,0:T(8,128)(2,1)S(1)}, u32[]{:S(2)}, u32[]{:S(2)}) collective-permute-start(bf16[192,2048]{1,0:T(8,128)(2,1)} %get-tuple-element.26), channel_id=1, source_target_pairs={{0,2},{1,3},{2,0},{3,1},{4,6},{5,7},{6,4},{7,5},{8,10},{9,11},{10,... | collective-permute-start | bytes 2359304 | tf_op jit(solution)/shard_map/ppermute | solution.py:334
  12.4 8.3 %collective-permute-start.1 = (bf16[256,512]{1,0:T(8,128)(2,1)}, bf16[256,512]{1,0:T(8,128)(2,1)}, u32[]{:S(2)}, u32[]{:S(2)}) collective-permute-start(bf16[256,512]{1,0:T(8,128)(2,1)} %get-tuple-element.22), channel_id=1, source_target_pairs={{0,16},{16,0},{1,17},{17,1},{2,18},{18,2},{3,19},{19,3},{4,20},{20... | collective-permute-start | bytes 786440 | tf_op jit(solution)/shard_map/ppermute | solution.py:322
  16.6 15.6 %collective-permute-start.8 = (bf16[256,512]{1,0:T(8,128)(2,1)S(1)}, bf16[256,512]{1,0:T(8,128)(2,1)S(1)}, u32[]{:S(2)}, u32[]{:S(2)}) collective-permute-start(bf16[256,512]{1,0:T(8,128)(2,1)S(1)} %fusion.14.refs_0_.own), channel_id=1, source_target_pairs={{0,12},{1,13},{2,14},{3,15},{4,8},{5,9},{6,10},{7,11},{8,4},{9,5},... | collective-permute-start | bytes 786440 | tf_op jit(solution)/shard_map/ppermute | solution.py:346
  23.3 16.5 %collective-permute-start.9 = (bf16[256,512]{1,0:T(8,128)(2,1)S(1)}, bf16[256,512]{1,0:T(8,128)(2,1)S(1)}, u32[]{:S(2)}, u32[]{:S(2)}) collective-permute-start(bf16[256,512]{1,0:T(8,128)(2,1)S(1)} %fusion.9.refs_1_.own), channel_id=1, source_target_pairs={{0,12},{1,13},{2,14},{3,15},{4,8},{5,9},{6,10},{7,11},{8,4},{9,5},... | collective-permute-start | bytes 786440 | tf_op jit(solution)/shard_map/ppermute | solution.py:346
  27.0 22.6 %collective-permute-start.7 = (bf16[256,512]{1,0:T(8,128)(2,1)S(1)}, bf16[256,512]{1,0:T(8,128)(2,1)S(1)}, u32[]{:S(2)}, u32[]{:S(2)}) collective-permute-start(bf16[256,512]{1,0:T(8,128)(2,1)S(1)} %fusion.9.refs_1_.own), channel_id=1, source_target_pairs={{0,4},{1,5},{2,6},{3,7},{4,0},{5,1},{6,2},{7,3},{8,12},{9,13},{10,... | collective-permute-start | bytes 786440 | tf_op jit(solution)/shard_map/ppermute | solution.py:348
  30.7 21.8 %collective-permute-start.5 = (bf16[192,2048]{1,0:T(8,128)(2,1)}, bf16[192,2048]{1,0:T(8,128)(2,1)S(1)}, u32[]{:S(2)}, u32[]{:S(2)}) collective-permute-start(bf16[192,2048]{1,0:T(8,128)(2,1)} %collective-permute-done.4), channel_id=1, source_target_pairs={{0,2},{1,3},{2,0},{3,1},{4,6},{5,7},{6,4},{7,5},{8,10},{9,11},{10,... | collective-permute-start | bytes 2359304 | tf_op jit(solution)/shard_map/ppermute | solution.py:360
  32.2 20.7 %collective-permute-start.10 = (bf16[256,512]{1,0:T(8,128)(2,1)S(1)}, bf16[256,512]{1,0:T(8,128)(2,1)S(1)}, u32[]{:S(2)}, u32[]{:S(2)}) collective-permute-start(bf16[256,512]{1,0:T(8,128)(2,1)S(1)} %pick.2), channel_id=1, source_target_pairs={{0,8},{1,9},{2,10},{3,11},{4,0},{5,1},{6,2},{7,3},{8,12},{9,13},{1... | collective-permute-start | bytes 786440 | tf_op jit(solution)/shard_map/ppermute | solution.py:351
  39.8 11.2 %collective-permute-start.6 = (bf16[256,512]{1,0:T(8,128)(2,1)S(1)}, bf16[256,512]{1,0:T(8,128)(2,1)S(1)}, u32[]{:S(2)}, u32[]{:S(2)}) collective-permute-start(bf16[256,512]{1,0:T(8,128)(2,1)S(1)} %fusion.14.refs_0_.own), channel_id=1, source_target_pairs={{0,4},{1,5},{2,6},{3,7},{4,0},{5,1},{6,2},{7,3},{8,12},{9,13},{10,... | collective-permute-start | bytes 786440 | tf_op jit(solution)/shard_map/ppermute | solution.py:348
  39.8 12.1 %copy-start = (bf16[192,2048]{1,0:T(8,128)(2,1)S(1)}, bf16[192,2048]{1,0:T(8,128)(2,1)}, u32[]{:S(2)}) copy-start(bf16[192,2048]{1,0:T(8,128)(2,1)} %get-tuple-element.24.tokens.refs_0_) | copy-start | bytes 2359300
  39.8 15.0 %collective-permute-start.11 = (bf16[256,512]{1,0:T(8,128)(2,1)S(1)}, bf16[256,512]{1,0:T(8,128)(2,1)S(1)}, u32[]{:S(2)}, u32[]{:S(2)}) collective-permute-start(bf16[256,512]{1,0:T(8,128)(2,1)S(1)} %pick.3), channel_id=1, source_target_pairs={{0,8},{1,9},{2,10},{3,11},{4,0},{5,1},{6,2},{7,3},{8,12},{9,13},{1... | collective-permute-start | bytes 786440 | tf_op jit(solution)/shard_map/ppermute | solution.py:351
  54.9 3.4 %copy-start.5 = (f32[1,512,512]{2,1,0:T(8,128)S(1)}, f32[1,512,512]{2,1,0:T(8,128)}, u32[]{:S(2)}) copy-start(f32[1,512,512]{2,1,0:T(8,128)} %param.7) | copy-start | bytes 3145732
  55.2 2.4 %collective-permute-start.12 = (f32[384,512]{1,0:T(8,128)S(1)}, f32[384,512]{1,0:T(8,128)S(1)}, u32[]{:S(2)}, u32[]{:S(2)}) collective-permute-start(f32[384,512]{1,0:T(8,128)S(1)} %get-tuple-element.37), channel_id=1, source_target_pairs={{0,1},{1,0},{2,3},{3,2},{4,5},{5,4},{6,7},{7,6},{8,9},{9,8},{10,11... | collective-permute-start | bytes 2359304 | tf_op jit(solution)/shard_map/ppermute | solution.py:368
  57.7 7.0 %collective-permute-start.13 = (bf16[192,512]{1,0:T(8,128)(2,1)S(1)}, bf16[192,512]{1,0:T(8,128)(2,1)S(1)}, u32[]{:S(2)}, u32[]{:S(2)}) collective-permute-start(bf16[192,512]{1,0:T(8,128)(2,1)S(1)} %over_core.1), channel_id=1, source_target_pairs={{0,2},{1,3},{2,0},{3,1},{4,6},{5,7},{6,4},{7,5},{8,10},{9,11},{10,... | collective-permute-start | bytes 589832 | tf_op jit(solution)/shard_map/ppermute | solution.py:369

commit v4 on v3

v4 whole, which is shorter than its diff:
```python
import functools

import jax
import jax.numpy as jnp
from jax import lax
from jax.experimental import pallas as pl
from jax.experimental.pallas import tpu as pltpu
from jax.sharding import PartitionSpec as P

outer_rate = 0.7
momentum_decay = 0.9
PLANE = 4
FIRST = 8
HBM = pl.BlockSpec(memory_space=pltpu.HBM)
SMEM = pl.BlockSpec(memory_space=pltpu.SMEM)
FIRST_LIMIT = pltpu.CompilerParams(vmem_limit_bytes=int(60 * 2**20))
ARRANGE_LIMIT = pltpu.CompilerParams(vmem_limit_bytes=int(60 * 2**20))
SMALL = pltpu.CompilerParams(vmem_limit_bytes=16 * 2**20)


def cost(us):
    return pl.CostEstimate(flops=int(us * 1_153_000_000), bytes_accessed=0, transcendentals=0)


COST = dict(add_keys=1, pick=4.5, next_working=4)


def plane_pairs(size, bit):
    return [(i, i ^ bit) for i in range(size)]


def line_pairs(size, to):
    return [(i, to[i // PLANE] * PLANE + i % PLANE) for i in range(size)]


def whole(array):
    return pl.BlockSpec(array.shape, lambda *_: (0,) * array.ndim)


def block_of(line, place, k, distance):
    if line == 4:
        return place ^ ([0, 1, 3, 2][k] * PLANE + distance)
    return ((place % PLANE) ^ distance) + k * PLANE


def arrange_body(width, distances, place, tokens, *refs):
    count = len(distances)
    outs, held, (arrived, left) = refs[:count], refs[count : 2 * count], refs[2 * count :]
    line = outs[0].shape[1] // width
    copies = []
    for i, distance in enumerate(distances):
        for k in range(line):
            start = pl.multiple_of(block_of(line, place[0], k, distance) * width, width)
            copies.append(
                pltpu.make_async_copy(
                    tokens.at[:, pl.ds(start, width)],
                    held[i].at[:, pl.ds(k * width, width)],
                    arrived.at[i * line + k],
                )
            )
    for copy in copies:
        copy.start()
    away = [pltpu.make_async_copy(held[i], outs[i], left.at[i]) for i in range(count)]
    for i in range(count):
        for k in range(line):
            copies[i * line + k].wait()
        away[i].start()
    for copy in away:
        copy.wait()


def arrange_tokens(place, tokens, line, width, distances):
    shape = (tokens.shape[0], line * width)
    return pl.pallas_call(
        functools.partial(arrange_body, width, distances),
        grid=(1,),
        in_specs=[SMEM, HBM],
        out_specs=[HBM] * len(distances),
        out_shape=[jax.ShapeDtypeStruct(shape, tokens.dtype)] * len(distances),
        scratch_shapes=[pltpu.VMEM(shape, tokens.dtype)] * len(distances)
        + [pltpu.SemaphoreType.DMA((line * len(distances),)), pltpu.SemaphoreType.DMA((len(distances),))],
        cost_estimate=cost(0),
        compiler_params=ARRANGE_LIMIT,
        name="arrange_tokens",
    )(place, tokens)


def read_mixing(own_group, partners, mix_weights):
    me = own_group[0]
    numerators = [mix_weights[me, j].astype(jnp.float32) for j in range(5)]
    total = sum(numerators)

    def coefficient(group):
        found = jnp.where(group == me, numerators[0], 0.0)
        for j in range(4):
            found = found + jnp.where(partners[me, j] == group, numerators[j + 1], 0.0)
        return found / total

    return me, coefficient


def others_mixed(groups, me, coefficient, received):
    if groups == 2:
        return coefficient(1 - me) * received[0][...].astype(jnp.float32)
    mixed = jnp.zeros(received[0].shape, jnp.float32)
    for g in range(groups):
        mixed = mixed + jnp.where(g == me, 0.0, coefficient(g)) * received[g][...].astype(jnp.float32)
    return mixed


def first_body(starts, own_group, partners, mix_weights, master, momentum, working, *refs):
    outs, (master_here, momentum_here, working_here, arrived) = refs[:-4], refs[-4:]
    deltas, bases = outs[: len(starts)], outs[len(starts) :]
    parts = [pl.ds(start, delta.shape[0]) for start, delta in zip(starts, deltas)]
    copies = [
        [
            pltpu.make_async_copy(there.at[part], here.at[part], arrived.at[i, j])
            for i, part in enumerate(parts)
        ]
        for j, (there, here) in enumerate([(master, master_here), (working, working_here), (momentum, momentum_here)])
    ]
    for i in range(len(parts)):
        copies[0][i].start()
        copies[1][i].start()
    for i in range(len(parts)):
        copies[2][i].start()
    me, coefficient = read_mixing(own_group, partners, mix_weights)
    own = coefficient(me)
    for i, part in enumerate(parts):
        copies[0][i].wait()
        copies[1][i].wait()
        delta = master_here[part] - working_here[part].astype(jnp.float32)
        deltas[i][...] = delta.astype(jnp.bfloat16)
    for i, part in enumerate(parts):
        copies[2][i].wait()
        mixed = own * (master_here[part] - working_here[part].astype(jnp.float32))
        new_momentum = momentum_decay * momentum_here[part] + mixed
        bases[i][...] = master_here[part] - outer_rate * (mixed + momentum_decay * new_momentum)


def first_step(scalars, master, momentum, working, cuts):
    shapes = [(size, master.shape[1]) for _, size in cuts]
    outs = pl.pallas_call(
        functools.partial(first_body, [start for start, _ in cuts]),
        grid=(1,),
        in_specs=[SMEM] * 3 + [HBM] * 3,
        out_specs=[pl.BlockSpec(shape, lambda *_: (0, 0)) for shape in shapes] * 2,
        out_shape=[jax.ShapeDtypeStruct(shape, jnp.bfloat16) for shape in shapes]
        + [jax.ShapeDtypeStruct(shape, jnp.float32) for shape in shapes],
        scratch_shapes=[
            pltpu.VMEM(master.shape, master.dtype),
            pltpu.VMEM(momentum.shape, momentum.dtype),
            pltpu.VMEM(working.shape, working.dtype),
            pltpu.SemaphoreType.DMA((len(cuts), 3)),
        ],
        cost_estimate=cost(0),
        compiler_params=FIRST_LIMIT,
        name="first_step",
    )(*scalars, master, momentum, working)
    return outs[: len(cuts)], outs[len(cuts) :]


def working_body(groups, own_group, partners, mix_weights, base, *refs):
    me, coefficient = read_mixing(own_group, partners, mix_weights)
    mixed = others_mixed(groups, me, coefficient, refs)
    refs[-1][...] = (base[...] - outer_rate * (1 + momentum_decay) * mixed).astype(jnp.bfloat16)


def next_working(scalars, groups, base, received):
    return pl.pallas_call(
        functools.partial(working_body, groups),
        grid=(1,),
        in_specs=[SMEM] * 3 + [whole(a) for a in (base, *received)],
        out_specs=whole(base),
        out_shape=jax.ShapeDtypeStruct(base.shape, jnp.bfloat16),
        cost_estimate=cost(COST["next_working"]),
        compiler_params=SMALL,
        name="next_working",
    )(*scalars, base, *received)


def outer_step_body(groups, starts, own_group, partners, mix_weights, master, momentum, working, *refs):
    received, (new_master, new_momentum) = refs[:-2], refs[-2:]
    each = len(received) // len(starts)
    me, coefficient = read_mixing(own_group, partners, mix_weights)
    own = coefficient(me)
    for i, start in enumerate(starts):
        others = received[i * each : (i + 1) * each]
        part = slice(start, start + others[0].shape[0])
        mixed = own * (master[part] - working[part].astype(jnp.float32))
        mixed = mixed + others_mixed(groups, me, coefficient, others)
        momentum_now = momentum_decay * momentum[part] + mixed
        new_momentum[part] = momentum_now
        new_master[part] = master[part] - outer_rate * (mixed + momentum_decay * momentum_now)


def outer_step(scalars, groups, master, momentum, working, cuts, received):
    shape = jax.ShapeDtypeStruct(master.shape, jnp.float32)
    return pl.pallas_call(
        functools.partial(outer_step_body, groups, [start for start, _ in cuts]),
        grid=(1,),
        in_specs=[SMEM] * 3 + [whole(a) for a in (master, momentum, working, *received)],
        out_specs=[whole(master)] * 2,
        out_shape=[shape, shape],
        cost_estimate=cost(0),
        compiler_params=SMALL,
        name="outer_step",
    )(*scalars, master, momentum, working, *received)


def after(value, *others):
    return lax.optimization_barrier((value, *others))[0]


def product(tokens, pieces, offsets):
    total = None
    for piece, offset in zip(pieces, offsets):
        term = jnp.dot(
            tokens[:, offset : offset + piece.shape[0]], piece[...], preferred_element_type=jnp.float32
        )
        total = term if total is None else total + term
    return total


def early_body(offsets, tokens, *refs):
    refs[-1][...] = product(tokens, refs[:-1], offsets)


def early_keys(tokens, pieces, offsets):
    span = max(o + p.shape[0] for o, p in zip(offsets, pieces))
    rows, width = tokens.shape[0], pieces[0].shape[1]
    return pl.pallas_call(
        functools.partial(early_body, offsets),
        grid=(1,),
        in_specs=[pl.BlockSpec((rows, span), lambda *_: (0, 0))] + [whole(p) for p in pieces],
        out_specs=pl.BlockSpec((rows, width), lambda *_: (0, 0)),
        out_shape=jax.ShapeDtypeStruct((rows, width), jnp.float32),
        cost_estimate=cost(0),
        compiler_params=SMALL,
        name="early_keys",
    )(tokens, *pieces)


def last_block(tokens, width):
    rows, span = tokens.shape
    return pl.BlockSpec((rows, width), lambda *_: (0, span // width - 1))


def add_body(offset, *refs):
    tokens, sums, piece, outs = refs[:PLANE], refs[PLANE : 2 * PLANE], refs[2 * PLANE], refs[-PLANE:]
    for t, s, o in zip(tokens, sums, outs):
        o[...] = s[...] + product(t, [piece], [offset])


def add_keys(tokens, sums, width, piece, offset):
    rows, columns = sums[0].shape
    return pl.pallas_call(
        functools.partial(add_body, offset),
        grid=(1,),
        in_specs=[last_block(t, width) for t in tokens] + [whole(a) for a in (*sums, piece)],
        out_specs=[whole(s) for s in sums],
        out_shape=[jax.ShapeDtypeStruct((rows, columns), jnp.float32)] * PLANE,
        cost_estimate=cost(COST["add_keys"]),
        compiler_params=SMALL,
        name="add_keys",
    )(*tokens, *sums, piece)


def pick_body(own_first, own, passed, *refs):
    @pl.when(own_first[0] == 1)
    def _():
        refs[-1][...] = own[...]

    @pl.when(own_first[0] == 0)
    def _():
        refs[-1][...] = passed[...]


def pick(own_first, own, passed):
    return pl.pallas_call(
        pick_body,
        grid=(1,),
        in_specs=[SMEM, whole(own), whole(passed)],
        out_specs=whole(own),
        out_shape=jax.ShapeDtypeStruct(own.shape, own.dtype),
        cost_estimate=cost(COST["pick"]),
        compiler_params=SMALL,
        name="pick",
    )(own_first, own, passed)


def late_body(offset, *refs):
    tokens, sums, piece, outs = refs[:PLANE], refs[PLANE:-5], refs[-5], refs[-4:]
    for t, s, out in zip(tokens, sums, outs):
        out[...] = s[...] + product(t, [piece], [offset])


def late_keys(tokens, sums, width, piece, offset):
    rows, columns = sums[0].shape
    return pl.pallas_call(
        functools.partial(late_body, offset),
        grid=(1,),
        in_specs=[last_block(t, width) for t in tokens] + [whole(a) for a in (*sums, piece)],
        out_specs=[whole(s) for s in sums],
        out_shape=[jax.ShapeDtypeStruct((rows, columns), jnp.float32)] * PLANE,
        cost_estimate=cost(0),
        compiler_params=SMALL,
        name="late_keys",
    )(*tokens, *sums, piece)


def over_core_body(keep_y, back, to_y):
    to_y[...] = (keep_y[...] + back[...]).astype(to_y.dtype)


def over_core(keep_y, back):
    rows, width = keep_y.shape
    return pl.pallas_call(
        over_core_body,
        grid=(1,),
        in_specs=[whole(keep_y), whole(back)],
        out_specs=whole(keep_y),
        out_shape=jax.ShapeDtypeStruct((rows, width), jnp.bfloat16),
        cost_estimate=cost(0),
        compiler_params=SMALL,
        name="over_core",
    )(keep_y, back)


def over_y_body(keep, back, there, keys):
    keys[...] = (keep[...] + back[...] + there[...].astype(jnp.float32)).astype(keys.dtype)


def over_y(keep, back, there):
    rows, width = keep.shape
    return pl.pallas_call(
        over_y_body,
        grid=(1,),
        in_specs=[whole(keep), whole(back), whole(there)],
        out_specs=whole(keep),
        out_shape=jax.ShapeDtypeStruct((rows, width), jnp.bfloat16),
        cost_estimate=cost(0),
        compiler_params=SMALL,
        name="over_y",
    )(keep, back, there)


def shards(master, momentum, working, tokens, partners, mix_weights):
    groups = lax.axis_size("replica")
    size = lax.axis_size("fsdp")
    line = size // PLANE
    place = lax.axis_index("fsdp").astype(jnp.int32)[None]
    scalars = (lax.axis_index("replica").astype(jnp.int32)[None], partners, mix_weights)
    master, momentum, working, tokens = master[0], momentum[0], working[0], tokens[0]
    rows = master.shape[0]
    first = rows * FIRST // 16
    cuts = [(0, first), (first, rows - first)]

    deltas, bases = first_step(scalars, master, momentum, working, cuts)
    received = []
    for delta in deltas:
        if groups == 2:
            received.append([lax.ppermute(delta, "replica", [(0, 1), (1, 0)])])
        else:
            every = lax.all_gather(delta, "replica", axis=0)
            received.append([every[g] for g in range(groups)])

    for_y, for_both, for_core, own = arrange_tokens(after(place, *deltas), tokens, line, rows, [2, 3, 1, 0])
    from_y = lax.ppermute(for_y, "fsdp", plane_pairs(size, 2))
    at_core = lax.ppermute(for_both, "fsdp", plane_pairs(size, 1))
    from_core = lax.ppermute(for_core, "fsdp", plane_pairs(size, 1))

    fresh = []
    for base, there in zip(bases, received):
        fresh.append(next_working(scalars, groups, base, [after(t, *fresh) for t in there]))
    if line == 4:
        z = place // PLANE
        own_first = jnp.where((z == 1) | (z == 2), 0, 1).astype(jnp.int32)
        far = [lax.ppermute(f, "fsdp", line_pairs(size, [3, 2, 1, 0])) for f in fresh]
        ready = [after(fresh[0], at_core, from_core), fresh[1]]
        near = [lax.ppermute(f, "fsdp", line_pairs(size, [1, 0, 3, 2])) for f in ready]
        passed = [far[0], far[1]]
        last = [
            lax.ppermute(pick(own_first, f, g), "fsdp", line_pairs(size, [2, 0, 3, 1]))
            for f, g in zip(fresh, passed)
        ]
        blocks = [fresh, near, far, last]
    else:
        lines = [[k * PLANE + p for k in range(line)] for p in range(PLANE)]
        every = [lax.all_gather(f, "fsdp", axis=0, axis_index_groups=lines) for f in fresh]
        blocks = [[e[k] for e in every] for k in range(line)]
    from_both = lax.ppermute(after(at_core, from_y, from_core), "fsdp", plane_pairs(size, 2))
    inputs = [own, from_core, from_y, from_both]

    early = [piece for block in blocks[:-1] for piece in block]
    offsets = [k * rows + start for k in range(line - 1) for start, _ in cuts]
    sums = [early_keys(t, early, offsets) for t in inputs]
    sums = add_keys(inputs, sums, rows, blocks[-1][0], cuts[0][0])
    own, for_core, keep_y, for_both = late_keys(inputs, sums, rows, blocks[-1][1], cuts[1][0])
    to_y = over_core(keep_y, lax.ppermute(for_both, "fsdp", plane_pairs(size, 1)))
    back = lax.ppermute(for_core, "fsdp", plane_pairs(size, 1))
    keys = over_y(own, back, lax.ppermute(to_y, "fsdp", plane_pairs(size, 2)))

    received = [after(r, to_y) for chunk in received for r in chunk]
    new_master, new_momentum = outer_step(scalars, groups, master, momentum, working, cuts, received)
    return new_master[None], new_momentum[None], keys[None]


def solution(mesh):
    return jax.shard_map(
        shards,
        mesh=mesh,
        in_specs=(
            P("replica", "fsdp", None),
            P("replica", "fsdp", None),
            P("replica", "fsdp", None),
            P("replica", "fsdp", None),
            P(),
            P(),
        ),
        out_specs=(
            P("replica", "fsdp", None),
            P("replica", "fsdp", None),
            P("replica", "fsdp", None),
        ),
        check_vma=False,
    )
```

time: 65.7 us -> 62.3 us (0.948)
  other arithmetic: 8.87 us -> 0 us
  Pallas kernels: 10.1 us -> 14.2 us
  waiting for transfers between devices: 12 us -> 14.1 us
  local copies, waits for them, and re-layouts: 1.19 us -> 0.04 us
    convert_element_type x2 -> x0, other arithmetic: 4.97 us -> none  [shards(): fresh.append(new_master.astype(jnp.bfloat16))]
    pallas_call x4 -> x6, Pallas kernels: 3.7 us -> 8.41 us  [the longest x1 3.63 us: first_step(): pl.pallas_call(functools.partial(first_body, [start for start, _ in cuts]...]
    ppermute x1, waiting for transfers between devices: 3.69 us -> 6.93 us  [shards(): from_y = lax.ppermute(for_y, 'fsdp', plane_pairs(size, 2))]
    broadcast_in_dim x1 -> x0, other arithmetic: 2.92 us -> none  [shards(): return (new_master[None], new_momentum[None], keys[None])]
    ppermute x2, starting transfers between devices: 17.3 us -> 15.3 us  [shards(): lax.ppermute(pick(own_first, f, g), 'fsdp', line_pairs(size, [2, 0, 3, 1]))]
    ppermute x2 -> x3, starting transfers between devices: 0.65 us -> 2.37 us  [the longest x1 1.8 us: shards(): keys = over_y(own, back, lax.ppermute(to_y, 'fsdp', plane_pairs(size, 2)))]
    ppermute x2, waiting for transfers between devices: 0.52 us -> 1.61 us  [shards(): received.append([lax.ppermute(delta, 'replica', [(0, 1), (1, 0)])])]
    concatenate x1 -> x0, other arithmetic: 0.99 us -> none  [shards(): received = [after(jnp.concatenate(list(r)), keep) for r in zip(*received)]]
  transfers between devices with their start and end apart: 14 -> 15, of which waited for: 6 -> 6; matrix products, arithmetic and copies ran while one was open for 15% -> 0% of each run, Pallas kernels for 10% -> 15%
where the time goes in v4:
time: 62.3 us; the launch traced here: 62.1 us
  starting transfers between devices  33 us (53%)
  Pallas kernels  14.2 us (23%)
  waiting for transfers between devices  14.1 us (23%)
  between operations  0.85 us (1%)
    ppermute x2, starting transfers between devices, shards(): lax.ppermute(pick(own_first, f, g), 'fsdp', line_pairs(size, [2, 0, 3, 1]))  15.3 us
    ppermute x2, starting transfers between devices, shards(): lax.ppermute(f, 'fsdp', line_pairs(size, [3, 2, 1, 0]))  7.94 us
    ppermute x1, waiting for transfers between devices, shards(): from_y = lax.ppermute(for_y, 'fsdp', plane_pairs(size, 2))  6.93 us
    pallas_call x1, Pallas kernels, first_step(): pl.pallas_call(functools.partial(first_body, [start for start, _ in cuts]...  3.63 us
    pallas_call x1, Pallas kernels, arrange_tokens(): pl.pallas_call(functools.partial(arrange_body, width, distances), grid=(1...  3.1 us
    ppermute x2, starting transfers between devices, shards(): received.append([lax.ppermute(delta, 'replica', [(0, 1), (1, 0)])])  3.08 us
    ppermute x1, waiting for transfers between devices, shards(): keys = over_y(own, back, lax.ppermute(to_y, 'fsdp', plane_pairs(size, 2)))  2.65 us
    pallas_call x1, Pallas kernels, outer_step(): pl.pallas_call(functools.partial(outer_step_body, groups, [start for star...  2.55 us
  transfers between devices with their start and end apart: 15, of which 6 were waited for; matrix products, arithmetic and copies ran while one was open for 0% of the time, Pallas kernels for 15%

profile of v4, /device:TPU:0, one launch (start us, length us, event | category | flops | bytes accessed | tf_op | source)
XLA Modules:
  0.0 62.1 jit_solution(2011430765124856014)
XLA Ops:
  0.6 0.0 copy-start.4
  0.6 0.0 copy-start.5
  0.7 3.6 %first_step.1 = (bf16[256,512]{1,0:T(8,128)(2,1)}, bf16[256,512]{1,0:T(8,128)(2,1)}, f32[256,512]{1,0:T(8,128)}, f32[256,512]{1,0:T(8,128)}) custom-call(s32[1]{0:T(128)} %bitcast.own_group, s32[2,4]{1,0:T(2,128)} %partners.7, s32[2,5]{1,0:T(2,128)} %mix_weights.7, f32[512,512]{1,0:T(8,128)} %bitcast.9, f32[512,512]{1,0:T(8,128)} %bitcast.11, ...), custom_call_target="tpu_custom_call" | custom-call | tf_op jit(solution)/shard_map/first_step/pallas_call | solution.py:143
  4.3 0.0 copy-start.7
  4.3 3.0 %collective-permute-start = (bf16[256,512]{1,0:T(8,128)(2,1)}, bf16[256,512]{1,0:T(8,128)(2,1)S(1)}, u32[]{:S(2)}, u32[]{:S(2)}) collective-permute-start(bf16[256,512]{1,0:T(8,128)(2,1)} %get-tuple-element.27), channel_id=1, source_target_pairs={{0,16},{16,0},{1,17},{17,1},{2,18},{18,2},{3,19},{19,3},{4,20},{20... | collective-permute-start | bytes 786440 | tf_op jit(solution)/shard_map/ppermute | solution.py:363
  7.3 0.1 collective-permute-start.5
  7.4 3.1 %arrange_tokens.1 = (bf16[192,2048]{1,0:T(8,128)(2,1)}, bf16[192,2048]{1,0:T(8,128)(2,1)}, bf16[192,2048]{1,0:T(8,128)(2,1)}, bf16[192,2048]{1,0:T(8,128)(2,1)}) custom-call(s32[1]{0:T(128)} %bitcast.4.place, bf16[192,8192]{1,0:T(8,128)(2,1)} %bitcast.15), custom_call_target="tpu_custom_call" | custom-call | tf_op jit(solution)/shard_map/arrange_tokens/pallas_call | solution.py:74
  10.5 0.1 collective-permute-start.1
  10.6 0.5 collective-permute-start.3
  11.1 2.0 %collective-permute-start.2 = (bf16[192,2048]{1,0:T(8,128)(2,1)}, bf16[192,2048]{1,0:T(8,128)(2,1)S(1)}, u32[]{:S(2)}, u32[]{:S(2)}) collective-permute-start(bf16[192,2048]{1,0:T(8,128)(2,1)} %get-tuple-element.32), channel_id=1, source_target_pairs={{0,2},{1,3},{2,0},{3,1},{4,6},{5,7},{6,4},{7,5},{8,10},{9,11},{10,... | collective-permute-start | bytes 2359304 | tf_op jit(solution)/shard_map/ppermute | solution.py:369
  13.0 1.6 %collective-permute-done.refs_0_ = bf16[256,512]{1,0:T(8,128)(2,1)S(1)} collective-permute-done((bf16[256,512]{1,0:T(8,128)(2,1)}, bf16[256,512]{1,0:T(8,128)(2,1)S(1)}, u32[]{:S(2)}, u32[]{:S(2)}) %collective-permute-start) | collective-permute-done | bytes 262176 | tf_op jit(solution)/shard_map/ppermute | solution.py:363
  14.7 0.0 copy-done.4
  14.7 0.0 copy-done.5
  14.7 0.0 copy-done.7
  14.7 0.0 copy-start.6
  14.7 0.7 %next_working.2.refs_0_.own = bf16[256,512]{1,0:T(8,128)(2,1)S(1)} custom-call(s32[1]{0:T(128)} %bitcast.own_group, s32[2,4]{1,0:T(2,128)S(1)} %copy-done.4, s32[2,5]{1,0:T(2,128)S(1)} %copy-done.5, f32[256,512]{1,0:T(8,128)S(1)} %copy-done.7, bf16[256,512]{1,0:T(8,128)(2,1)S(1)} %collective-permute-done.refs_0_), custom_call_target="tpu_custom_call" | custom-call | flops 4611999744 | tf_op jit(solution)/shard_map/next_working/pallas_call | solution.py:170
  15.4 4.2 %collective-permute-start.8 = (bf16[256,512]{1,0:T(8,128)(2,1)S(1)}, bf16[256,512]{1,0:T(8,128)(2,1)S(1)}, u32[]{:S(2)}, u32[]{:S(2)}) collective-permute-start(bf16[256,512]{1,0:T(8,128)(2,1)S(1)} %next_working.2.refs_0_.own), channel_id=1, source_target_pairs={{0,12},{1,13},{2,14},{3,15},{4,8},{5,9},{6,10},{7,11},{8,4},{9,5},... | collective-permute-start | bytes 786440 | tf_op jit(solution)/shard_map/ppermute | solution.py:379
  19.6 0.0 collective-permute-done.5.refs_0_.refs_1_
  19.7 0.0 copy-done.6
  19.7 0.7 %next_working.3.refs_1_.own = bf16[256,512]{1,0:T(8,128)(2,1)S(1)} custom-call(s32[1]{0:T(128)} %bitcast.own_group, s32[2,4]{1,0:T(2,128)S(1)} %copy-done.4, s32[2,5]{1,0:T(2,128)S(1)} %copy-done.5, f32[256,512]{1,0:T(8,128)S(1)} %copy-done.6, bf16[256,512]{1,0:T(8,128)(2,1)S(1)} %collective-permute-done.5.refs_0_.refs_1_), custom_call_target="tpu_custom_call" | custom-call | flops 4611999744 | tf_op jit(solution)/shard_map/next_working/pallas_call | solution.py:170
  20.4 3.7 %collective-permute-start.9 = (bf16[256,512]{1,0:T(8,128)(2,1)S(1)}, bf16[256,512]{1,0:T(8,128)(2,1)S(1)}, u32[]{:S(2)}, u32[]{:S(2)}) collective-permute-start(bf16[256,512]{1,0:T(8,128)(2,1)S(1)} %next_working.3.refs_1_.own), channel_id=1, source_target_pairs={{0,12},{1,13},{2,14},{3,15},{4,8},{5,9},{6,10},{7,11},{8,4},{9,5},... | collective-permute-start | bytes 786440 | tf_op jit(solution)/shard_map/ppermute | solution.py:379
  24.1 0.0 collective-permute-done.1.tokens.refs_1_
  24.1 0.0 collective-permute-start.7
  24.1 0.0 collective-permute-done.3
  24.1 6.9 %collective-permute-done.2.tokens.refs_2_ = bf16[192,2048]{1,0:T(8,128)(2,1)S(1)} collective-permute-done((bf16[192,2048]{1,0:T(8,128)(2,1)}, bf16[192,2048]{1,0:T(8,128)(2,1)S(1)}, u32[]{:S(2)}, u32[]{:S(2)}) %collective-permute-start.2) | collective-permute-done | bytes 786464 | tf_op jit(solution)/shard_map/ppermute | solution.py:369
  31.0 1.7 %collective-permute-start.4 = (bf16[192,2048]{1,0:T(8,128)(2,1)S(1)}, bf16[192,2048]{1,0:T(8,128)(2,1)S(1)}, u32[]{:S(2)}, u32[]{:S(2)}) collective-permute-start(bf16[192,2048]{1,0:T(8,128)(2,1)S(1)} %collective-permute-done.3), channel_id=1, source_target_pairs={{0,2},{1,3},{2,0},{3,1},{4,6},{5,7},{6,4},{7,5},{8,10},{9,11},{10,... | collective-permute-start | bytes 2359304 | tf_op jit(solution)/shard_map/ppermute | solution.py:392
  32.8 0.0 collective-permute-done.8.refs_4_.passed
  32.8 5.2 %collective-permute-start.10 = (bf16[256,512]{1,0:T(8,128)(2,1)S(1)}, bf16[256,512]{1,0:T(8,128)(2,1)S(1)}, u32[]{:S(2)}, u32[]{:S(2)}) collective-permute-start(bf16[256,512]{1,0:T(8,128)(2,1)S(1)} %pick.2), channel_id=1, source_target_pairs={{0,8},{1,9},{2,10},{3,11},{4,0},{5,1},{6,2},{7,3},{8,12},{9,13},{1... | collective-permute-start | bytes 786440 | tf_op jit(solution)/shard_map/ppermute | solution.py:384
  38.0 0.0 collective-permute-start.6
  38.0 0.0 collective-permute-done.9.refs_5_.passed
  38.1 0.0 copy-start
  38.1 10.0 %collective-permute-start.11 = (bf16[256,512]{1,0:T(8,128)(2,1)S(1)}, bf16[256,512]{1,0:T(8,128)(2,1)S(1)}, u32[]{:S(2)}, u32[]{:S(2)}) collective-permute-start(bf16[256,512]{1,0:T(8,128)(2,1)S(1)} %pick.3), channel_id=1, source_target_pairs={{0,8},{1,9},{2,10},{3,11},{4,0},{5,1},{6,2},{7,3},{8,12},{9,13},{1... | collective-permute-start | bytes 786440 | tf_op jit(solution)/shard_map/ppermute | solution.py:384
  48.1 0.0 collective-permute-done.7.refs_3_
  48.1 0.8 %collective-permute-done.6.refs_2_ = bf16[256,512]{1,0:T(8,128)(2,1)S(1)} collective-permute-done((bf16[256,512]{1,0:T(8,128)(2,1)S(1)}, bf16[256,512]{1,0:T(8,128)(2,1)S(1)}, u32[]{:S(2)}, u32[]{:S(2)}) %collective-permute-start.6) | collective-permute-done | bytes 262176 | tf_op jit(solution)/shard_map/ppermute | solution.py:381
  48.9 0.5 early_keys.6.refs_6_
  49.4 0.5 early_keys.5.refs_5_
  49.9 0.0 copy-done
  49.9 0.5 early_keys.4.refs_4_
  50.4 0.0 collective-permute-done.4.tokens.refs_3_
  50.4 0.5 early_keys.7.refs_7_
  50.9 0.0 collective-permute-done.10.refs_8_
  50.9 0.4 add_keys.1
  51.3 0.0 copy-start.1
  51.3 0.0 copy-start.2
  51.3 0.0 copy-start.3
  51.3 0.8 %collective-permute-done.11.refs_8_ = bf16[256,512]{1,0:T(8,128)(2,1)S(1)} collective-permute-done((bf16[256,512]{1,0:T(8,128)(2,1)S(1)}, bf16[256,512]{1,0:T(8,128)(2,1)S(1)}, u32[]{:S(2)}, u32[]{:S(2)}) %collective-permute-start.11) | collective-permute-done | bytes 262176 | tf_op jit(solution)/shard_map/ppermute | solution.py:384
  52.1 0.4 late_keys.1
  52.5 0.1 collective-permute-start.12
  52.6 0.5 collective-permute-start.13
  53.1 1.2 %collective-permute-done.12.back = f32[192,512]{1,0:T(8,128)S(1)} collective-permute-done((f32[192,512]{1,0:T(8,128)S(1)}, f32[192,512]{1,0:T(8,128)S(1)}, u32[]{:S(2)}, u32[]{:S(2)}) %collective-permute-start.12) | collective-permute-done | bytes 393248 | tf_op jit(solution)/shard_map/ppermute | solution.py:400
  54.3 1.8 %collective-permute-start.14 = (bf16[192,512]{1,0:T(8,128)(2,1)S(1)}, bf16[192,512]{1,0:T(8,128)(2,1)S(1)}, u32[]{:S(2)}, u32[]{:S(2)}) collective-permute-start(bf16[192,512]{1,0:T(8,128)(2,1)S(1)} %over_core.1), channel_id=1, source_target_pairs={{0,2},{1,3},{2,0},{3,1},{4,6},{5,7},{6,4},{7,5},{8,10},{9,11},{10,... | collective-permute-start | bytes 589832 | tf_op jit(solution)/shard_map/ppermute | solution.py:402
  56.1 0.0 copy-done.1
  56.2 0.0 copy-done.2
  56.2 0.0 copy-done.3
  56.2 2.5 %outer_step.1 = (f32[512,512]{1,0:T(8,128)}, f32[512,512]{1,0:T(8,128)}) custom-call(s32[1]{0:T(128)} %bitcast.own_group, s32[2,4]{1,0:T(2,128)S(1)} %copy-done.4, s32[2,5]{1,0:T(2,128)S(1)} %copy-done.5, f32[512,512]{1,0:T(8,128)S(1)} %bitcast.10, f32[512,512]{1,0:T(8,128)S(1)} %bitcast.12, bf16[512,512]{1,0:T(8,128)(2,1)S(1)} %bitcast.14, ...), custom_call_target="tpu_custom_call" | custom-call | tf_op jit(solution)/shard_map/outer_step/pallas_call | solution.py:199
  58.7 0.0 collective-permute-done.13.back
  58.7 2.6 %collective-permute-done.14.there = bf16[192,512]{1,0:T(8,128)(2,1)S(1)} collective-permute-done((bf16[192,512]{1,0:T(8,128)(2,1)S(1)}, bf16[192,512]{1,0:T(8,128)(2,1)S(1)}, u32[]{:S(2)}, u32[]{:S(2)}) %collective-permute-start.14) | collective-permute-done | bytes 196640 | tf_op jit(solution)/shard_map/ppermute | solution.py:402
  61.4 0.7 %over_y.1 = bf16[192,512]{1,0:T(8,128)(2,1)} custom-call(f32[192,512]{1,0:T(8,128)S(1)} %get-tuple-element.49.keep, f32[192,512]{1,0:T(8,128)S(1)} %collective-permute-done.13.back, bf16[192,512]{1,0:T(8,128)(2,1)S(1)} %collective-permute-done.14.there), custom_call_target="tpu_custom_call" | custom-call | tf_op jit(solution)/shard_map/over_y/pallas_call | solution.py:336
  (3 shorter events, 0.1 us)
Async XLA Ops:
  0.6 14.0 %copy-start.4 = (s32[2,4]{1,0:T(2,128)S(1)}, s32[2,4]{1,0:T(2,128)}, u32[]{:S(2)}) copy-start(s32[2,4]{1,0:T(2,128)} %partners.7) | copy-start | bytes 100
  0.6 14.0 %copy-start.5 = (s32[2,5]{1,0:T(2,128)S(1)}, s32[2,5]{1,0:T(2,128)}, u32[]{:S(2)}) copy-start(s32[2,5]{1,0:T(2,128)} %mix_weights.7) | copy-start | bytes 124
  4.3 10.4 %copy-start.7 = (f32[256,512]{1,0:T(8,128)S(1)}, f32[256,512]{1,0:T(8,128)}, u32[]{:S(2)}) copy-start(f32[256,512]{1,0:T(8,128)} %get-tuple-element.35.base) | copy-start | bytes 1572868
  4.3 10.3 %collective-permute-start = (bf16[256,512]{1,0:T(8,128)(2,1)}, bf16[256,512]{1,0:T(8,128)(2,1)S(1)}, u32[]{:S(2)}, u32[]{:S(2)}) collective-permute-start(bf16[256,512]{1,0:T(8,128)(2,1)} %get-tuple-element.27), channel_id=1, source_target_pairs={{0,16},{16,0},{1,17},{17,1},{2,18},{18,2},{3,19},{19,3},{4,20},{20... | collective-permute-start | bytes 786440 | tf_op jit(solution)/shard_map/ppermute | solution.py:363
  7.3 12.3 %collective-permute-start.5 = (bf16[256,512]{1,0:T(8,128)(2,1)}, bf16[256,512]{1,0:T(8,128)(2,1)S(1)}, u32[]{:S(2)}, u32[]{:S(2)}) collective-permute-start(bf16[256,512]{1,0:T(8,128)(2,1)} %get-tuple-element.28), channel_id=1, source_target_pairs={{0,16},{16,0},{1,17},{17,1},{2,18},{18,2},{3,19},{19,3},{4,20},{20... | collective-permute-start | bytes 786440 | tf_op jit(solution)/shard_map/ppermute | solution.py:363
  10.5 13.6 %collective-permute-start.1 = (bf16[192,2048]{1,0:T(8,128)(2,1)}, bf16[192,2048]{1,0:T(8,128)(2,1)S(1)}, u32[]{:S(2)}, u32[]{:S(2)}) collective-permute-start(bf16[192,2048]{1,0:T(8,128)(2,1)} %get-tuple-element.31), channel_id=1, source_target_pairs={{0,1},{1,0},{2,3},{3,2},{4,5},{5,4},{6,7},{7,6},{8,9},{9,8},{10,11... | collective-permute-start | bytes 2359304 | tf_op jit(solution)/shard_map/ppermute | solution.py:371
  10.6 13.5 %collective-permute-start.3 = (bf16[192,2048]{1,0:T(8,128)(2,1)}, bf16[192,2048]{1,0:T(8,128)(2,1)S(1)}, u32[]{:S(2)}, u32[]{:S(2)}) collective-permute-start(bf16[192,2048]{1,0:T(8,128)(2,1)} %get-tuple-element.33), channel_id=1, source_target_pairs={{0,1},{1,0},{2,3},{3,2},{4,5},{5,4},{6,7},{7,6},{8,9},{9,8},{10,11... | collective-permute-start | bytes 2359304 | tf_op jit(solution)/shard_map/ppermute | solution.py:370
  11.1 20.0 %collective-permute-start.2 = (bf16[192,2048]{1,0:T(8,128)(2,1)}, bf16[192,2048]{1,0:T(8,128)(2,1)S(1)}, u32[]{:S(2)}, u32[]{:S(2)}) collective-permute-start(bf16[192,2048]{1,0:T(8,128)(2,1)} %get-tuple-element.32), channel_id=1, source_target_pairs={{0,2},{1,3},{2,0},{3,1},{4,6},{5,7},{6,4},{7,5},{8,10},{9,11},{10,... | collective-permute-start | bytes 2359304 | tf_op jit(solution)/shard_map/ppermute | solution.py:369
  14.7 5.0 %copy-start.6 = (f32[256,512]{1,0:T(8,128)S(1)}, f32[256,512]{1,0:T(8,128)}, u32[]{:S(2)}) copy-start(f32[256,512]{1,0:T(8,128)} %get-tuple-element.36.base) | copy-start | bytes 1572868
  15.4 17.4 %collective-permute-start.8 = (bf16[256,512]{1,0:T(8,128)(2,1)S(1)}, bf16[256,512]{1,0:T(8,128)(2,1)S(1)}, u32[]{:S(2)}, u32[]{:S(2)}) collective-permute-start(bf16[256,512]{1,0:T(8,128)(2,1)S(1)} %next_working.2.refs_0_.own), channel_id=1, source_target_pairs={{0,12},{1,13},{2,14},{3,15},{4,8},{5,9},{6,10},{7,11},{8,4},{9,5},... | collective-permute-start | bytes 786440 | tf_op jit(solution)/shard_map/ppermute | solution.py:379
  20.4 17.7 %collective-permute-start.9 = (bf16[256,512]{1,0:T(8,128)(2,1)S(1)}, bf16[256,512]{1,0:T(8,128)(2,1)S(1)}, u32[]{:S(2)}, u32[]{:S(2)}) collective-permute-start(bf16[256,512]{1,0:T(8,128)(2,1)S(1)} %next_working.3.refs_1_.own), channel_id=1, source_target_pairs={{0,12},{1,13},{2,14},{3,15},{4,8},{5,9},{6,10},{7,11},{8,4},{9,5},... | collective-permute-start | bytes 786440 | tf_op jit(solution)/shard_map/ppermute | solution.py:379
  24.1 24.0 %collective-permute-start.7 = (bf16[256,512]{1,0:T(8,128)(2,1)S(1)}, bf16[256,512]{1,0:T(8,128)(2,1)S(1)}, u32[]{:S(2)}, u32[]{:S(2)}) collective-permute-start(bf16[256,512]{1,0:T(8,128)(2,1)S(1)} %next_working.3.refs_1_.own), channel_id=1, source_target_pairs={{0,4},{1,5},{2,6},{3,7},{4,0},{5,1},{6,2},{7,3},{8,12},{9,13},{10,... | collective-permute-start | bytes 786440 | tf_op jit(solution)/shard_map/ppermute | solution.py:381
  31.0 19.4 %collective-permute-start.4 = (bf16[192,2048]{1,0:T(8,128)(2,1)S(1)}, bf16[192,2048]{1,0:T(8,128)(2,1)S(1)}, u32[]{:S(2)}, u32[]{:S(2)}) collective-permute-start(bf16[192,2048]{1,0:T(8,128)(2,1)S(1)} %collective-permute-done.3), channel_id=1, source_target_pairs={{0,2},{1,3},{2,0},{3,1},{4,6},{5,7},{6,4},{7,5},{8,10},{9,11},{10,... | collective-permute-start | bytes 2359304 | tf_op jit(solution)/shard_map/ppermute | solution.py:392
  32.8 18.1 %collective-permute-start.10 = (bf16[256,512]{1,0:T(8,128)(2,1)S(1)}, bf16[256,512]{1,0:T(8,128)(2,1)S(1)}, u32[]{:S(2)}, u32[]{:S(2)}) collective-permute-start(bf16[256,512]{1,0:T(8,128)(2,1)S(1)} %pick.2), channel_id=1, source_target_pairs={{0,8},{1,9},{2,10},{3,11},{4,0},{5,1},{6,2},{7,3},{8,12},{9,13},{1... | collective-permute-start | bytes 786440 | tf_op jit(solution)/shard_map/ppermute | solution.py:384
  38.0 10.9 %collective-permute-start.6 = (bf16[256,512]{1,0:T(8,128)(2,1)S(1)}, bf16[256,512]{1,0:T(8,128)(2,1)S(1)}, u32[]{:S(2)}, u32[]{:S(2)}) collective-permute-start(bf16[256,512]{1,0:T(8,128)(2,1)S(1)} %next_working.2.refs_0_.own), channel_id=1, source_target_pairs={{0,4},{1,5},{2,6},{3,7},{4,0},{5,1},{6,2},{7,3},{8,12},{9,13},{10,... | collective-permute-start | bytes 786440 | tf_op jit(solution)/shard_map/ppermute | solution.py:381
  38.1 11.8 %copy-start = (bf16[192,2048]{1,0:T(8,128)(2,1)S(1)}, bf16[192,2048]{1,0:T(8,128)(2,1)}, u32[]{:S(2)}) copy-start(bf16[192,2048]{1,0:T(8,128)(2,1)} %get-tuple-element.30.tokens.refs_0_) | copy-start | bytes 2359300
  38.1 14.0 %collective-permute-start.11 = (bf16[256,512]{1,0:T(8,128)(2,1)S(1)}, bf16[256,512]{1,0:T(8,128)(2,1)S(1)}, u32[]{:S(2)}, u32[]{:S(2)}) collective-permute-start(bf16[256,512]{1,0:T(8,128)(2,1)S(1)} %pick.3), channel_id=1, source_target_pairs={{0,8},{1,9},{2,10},{3,11},{4,0},{5,1},{6,2},{7,3},{8,12},{9,13},{1... | collective-permute-start | bytes 786440 | tf_op jit(solution)/shard_map/ppermute | solution.py:384
  51.3 4.9 %copy-start.1 = (f32[1,512,512]{2,1,0:T(8,128)S(1)}, f32[1,512,512]{2,1,0:T(8,128)}, u32[]{:S(2)}) copy-start(f32[1,512,512]{2,1,0:T(8,128)} %param.6) | copy-start | bytes 3145732
  51.3 4.9 %copy-start.2 = (f32[1,512,512]{2,1,0:T(8,128)S(1)}, f32[1,512,512]{2,1,0:T(8,128)}, u32[]{:S(2)}) copy-start(f32[1,512,512]{2,1,0:T(8,128)} %param.7) | copy-start | bytes 3145732
  51.3 4.9 %copy-start.3 = (bf16[1,512,512]{2,1,0:T(8,128)(2,1)S(1)}, bf16[1,512,512]{2,1,0:T(8,128)(2,1)}, u32[]{:S(2)}) copy-start(bf16[1,512,512]{2,1,0:T(8,128)(2,1)} %param.8) | copy-start | bytes 1572868
  52.5 1.8 %collective-permute-start.12 = (f32[192,512]{1,0:T(8,128)S(1)}, f32[192,512]{1,0:T(8,128)S(1)}, u32[]{:S(2)}, u32[]{:S(2)}) collective-permute-start(f32[192,512]{1,0:T(8,128)S(1)} %get-tuple-element.44), channel_id=1, source_target_pairs={{0,1},{1,0},{2,3},{3,2},{4,5},{5,4},{6,7},{7,6},{8,9},{9,8},{10,11... | collective-permute-start | bytes 1179656 | tf_op jit(solution)/shard_map/ppermute | solution.py:400
  52.6 6.1 %collective-permute-start.13 = (f32[192,512]{1,0:T(8,128)S(1)}, f32[192,512]{1,0:T(8,128)S(1)}, u32[]{:S(2)}, u32[]{:S(2)}) collective-permute-start(f32[192,512]{1,0:T(8,128)S(1)} %get-tuple-element.50), channel_id=1, source_target_pairs={{0,1},{1,0},{2,3},{3,2},{4,5},{5,4},{6,7},{7,6},{8,9},{9,8},{10,11... | collective-permute-start | bytes 1179656 | tf_op jit(solution)/shard_map/ppermute | solution.py:401
  54.3 7.0 %collective-permute-start.14 = (bf16[192,512]{1,0:T(8,128)(2,1)S(1)}, bf16[192,512]{1,0:T(8,128)(2,1)S(1)}, u32[]{:S(2)}, u32[]{:S(2)}) collective-permute-start(bf16[192,512]{1,0:T(8,128)(2,1)S(1)} %over_core.1), channel_id=1, source_target_pairs={{0,2},{1,3},{2,0},{3,1},{4,6},{5,7},{6,4},{7,5},{8,10},{9,11},{10,... | collective-permute-start | bytes 589832 | tf_op jit(solution)/shard_map/ppermute | solution.py:402

commit v5 on v4

--- a/solution.py
+++ b/solution.py
@@ -13,8 +13,8 @@
 FIRST = 8
 HBM = pl.BlockSpec(memory_space=pltpu.HBM)
 SMEM = pl.BlockSpec(memory_space=pltpu.SMEM)
-FIRST_LIMIT = pltpu.CompilerParams(vmem_limit_bytes=int(60 * 2**20))
-ARRANGE_LIMIT = pltpu.CompilerParams(vmem_limit_bytes=int(60 * 2**20))
+FIRST_LIMIT = pltpu.CompilerParams(vmem_limit_bytes=60 * 2**20)
+ARRANGE_LIMIT = pltpu.CompilerParams(vmem_limit_bytes=60 * 2**20)
 SMALL = pltpu.CompilerParams(vmem_limit_bytes=16 * 2**20)
 
 
@@ -109,37 +109,31 @@
 
 
 def first_body(starts, own_group, partners, mix_weights, master, momentum, working, *refs):
-    outs, (master_here, momentum_here, working_here, arrived) = refs[:-4], refs[-4:]
+    outs, here, arrived = refs[:-4], refs[-4:-1], refs[-1]
     deltas, bases = outs[: len(starts)], outs[len(starts) :]
-    parts = [pl.ds(start, delta.shape[0]) for start, delta in zip(starts, deltas)]
     copies = [
-        [
-            pltpu.make_async_copy(there.at[part], here.at[part], arrived.at[i, j])
-            for i, part in enumerate(parts)
-        ]
-        for j, (there, here) in enumerate([(master, master_here), (working, working_here), (momentum, momentum_here)])
+        pltpu.make_async_copy(there, place, arrived.at[i])
+        for i, (there, place) in enumerate(zip((master, working, momentum), here))
     ]
-    for i in range(len(parts)):
-        copies[0][i].start()
-        copies[1][i].start()
-    for i in range(len(parts)):
-        copies[2][i].start()
+    for copy in copies:
+        copy.start()
     me, coefficient = read_mixing(own_group, partners, mix_weights)
     own = coefficient(me)
-    for i, part in enumerate(parts):
-        copies[0][i].wait()
-        copies[1][i].wait()
-        delta = master_here[part] - working_here[part].astype(jnp.float32)
-        deltas[i][...] = delta.astype(jnp.bfloat16)
-    for i, part in enumerate(parts):
-        copies[2][i].wait()
-        mixed = own * (master_here[part] - working_here[part].astype(jnp.float32))
-        new_momentum = momentum_decay * momentum_here[part] + mixed
-        bases[i][...] = master_here[part] - outer_rate * (mixed + momentum_decay * new_momentum)
+    copies[0].wait()
+    copies[1].wait()
+    parts = [slice(start, start + delta.shape[1]) for start, delta in zip(starts, deltas)]
+    for part, out in zip(parts, deltas):
+        out[...] = (here[0][:, part] - here[1][:, part].astype(jnp.float32)).astype(jnp.bfloat16)
+    copies[2].wait()
+    for part, out in zip(parts, bases):
+        now = here[0][:, part]
+        mixed = own * (now - here[1][:, part].astype(jnp.float32))
+        new_momentum = momentum_decay * here[2][:, part] + mixed
+        out[...] = now - outer_rate * (mixed + momentum_decay * new_momentum)
 
 
 def first_step(scalars, master, momentum, working, cuts):
-    shapes = [(size, master.shape[1]) for _, size in cuts]
+    shapes = [(master.shape[0], size) for _, size in cuts]
     outs = pl.pallas_call(
         functools.partial(first_body, [start for start, _ in cuts]),
         grid=(1,),
@@ -147,12 +141,8 @@
         out_specs=[pl.BlockSpec(shape, lambda *_: (0, 0)) for shape in shapes] * 2,
         out_shape=[jax.ShapeDtypeStruct(shape, jnp.bfloat16) for shape in shapes]
         + [jax.ShapeDtypeStruct(shape, jnp.float32) for shape in shapes],
-        scratch_shapes=[
-            pltpu.VMEM(master.shape, master.dtype),
-            pltpu.VMEM(momentum.shape, momentum.dtype),
-            pltpu.VMEM(working.shape, working.dtype),
-            pltpu.SemaphoreType.DMA((len(cuts), 3)),
-        ],
+        scratch_shapes=[pltpu.VMEM(a.shape, a.dtype) for a in (master, working, momentum)]
+        + [pltpu.SemaphoreType.DMA((3,))],
         cost_estimate=cost(0),
         compiler_params=FIRST_LIMIT,
         name="first_step",
@@ -186,12 +176,12 @@
     own = coefficient(me)
     for i, start in enumerate(starts):
         others = received[i * each : (i + 1) * each]
-        part = slice(start, start + others[0].shape[0])
-        mixed = own * (master[part] - working[part].astype(jnp.float32))
+        part = slice(start, start + others[0].shape[1])
+        mixed = own * (master[:, part] - working[:, part].astype(jnp.float32))
         mixed = mixed + others_mixed(groups, me, coefficient, others)
-        momentum_now = momentum_decay * momentum[part] + mixed
-        new_momentum[part] = momentum_now
-        new_master[part] = master[part] - outer_rate * (mixed + momentum_decay * momentum_now)
+        momentum_now = momentum_decay * momentum[:, part] + mixed
+        new_momentum[:, part] = momentum_now
+        new_master[:, part] = master[:, part] - outer_rate * (mixed + momentum_decay * momentum_now)
 
 
 def outer_step(scalars, groups, master, momentum, working, cuts, received):
@@ -222,8 +212,8 @@
     return total
 
 
-def early_body(offsets, tokens, *refs):
-    refs[-1][...] = product(tokens, refs[:-1], offsets)
+def early_body(offsets, *refs):
+    refs[-1][...] = product(refs[0], refs[1:-1], offsets)
 
 
 def early_keys(tokens, pieces, offsets):
@@ -241,39 +231,75 @@
     )(tokens, *pieces)
 
 
+def own_block(line, k, rows, width):
+    return pl.BlockSpec((rows, width), lambda i, place: (0, block_of(line, place[0], k, 0)))
+
+
+def own_early_body(count, each, offsets, place, *refs):
+    total = None
+    for k in range(count):
+        part = slice(k * each, (k + 1) * each)
+        term = product(refs[k], refs[count:-1][part], offsets)
+        total = term if total is None else total + term
+    refs[-1][...] = total
+
+
+def own_early_keys(place, line, tokens, blocks, width, offsets):
+    count, pieces = len(blocks), [piece for block in blocks for piece in block]
+    rows, columns = tokens.shape[0], pieces[0].shape[1]
+    return pl.pallas_call(
+        functools.partial(own_early_body, count, len(offsets), offsets),
+        grid_spec=pltpu.PrefetchScalarGridSpec(
+            num_scalar_prefetch=1,
+            grid=(1,),
+            in_specs=[own_block(line, k, rows, width) for k in range(count)] + [whole(p) for p in pieces],
+            out_specs=pl.BlockSpec((rows, columns), lambda *_: (0, 0)),
+        ),
+        out_shape=jax.ShapeDtypeStruct((rows, columns), jnp.float32),
+        cost_estimate=cost(0),
+        compiler_params=SMALL,
+        name="own_early_keys",
+    )(place, *([tokens] * count), *pieces)
+
+
 def last_block(tokens, width):
     rows, span = tokens.shape
     return pl.BlockSpec((rows, width), lambda *_: (0, span // width - 1))
 
 
-def add_body(offset, *refs):
+def late_body(offset, place, *refs):
     tokens, sums, piece, outs = refs[:PLANE], refs[PLANE : 2 * PLANE], refs[2 * PLANE], refs[-PLANE:]
     for t, s, o in zip(tokens, sums, outs):
         o[...] = s[...] + product(t, [piece], [offset])
 
 
-def add_keys(tokens, sums, width, piece, offset):
+def late_keys(place, line, tokens, sums, width, piece, offset, declared):
     rows, columns = sums[0].shape
     return pl.pallas_call(
-        functools.partial(add_body, offset),
-        grid=(1,),
-        in_specs=[last_block(t, width) for t in tokens] + [whole(a) for a in (*sums, piece)],
-        out_specs=[whole(s) for s in sums],
+        functools.partial(late_body, offset),
+        grid_spec=pltpu.PrefetchScalarGridSpec(
+            num_scalar_prefetch=1,
+            grid=(1,),
+            in_specs=[own_block(line, line - 1, rows, width)]
+            + [last_block(t, width) for t in tokens[1:]]
+            + [whole(a) for a in (*sums, piece)],
+            out_specs=[whole(s) for s in sums],
+        ),
         out_shape=[jax.ShapeDtypeStruct((rows, columns), jnp.float32)] * PLANE,
-        cost_estimate=cost(COST["add_keys"]),
-        compiler_params=SMALL,
-        name="add_keys",
-    )(*tokens, *sums, piece)
-
-
-def pick_body(own_first, own, passed, *refs):
+        cost_estimate=cost(declared),
+        compiler_params=SMALL,
+        name="late_keys",
+    )(place, *tokens, *sums, piece)
+
+
+def pick_body(own_first, own, passed, out):
     @pl.when(own_first[0] == 1)
     def _():
-        refs[-1][...] = own[...]
+        out[...] = own[...]
 
     @pl.when(own_first[0] == 0)
     def _():
-        refs[-1][...] = passed[...]
+        out[...] = passed[...]
 
 
 def pick(own_first, own, passed):
@@ -289,26 +315,6 @@
     )(own_first, own, passed)
 
 
-def late_body(offset, *refs):
-    tokens, sums, piece, outs = refs[:PLANE], refs[PLANE:-5], refs[-5], refs[-4:]
-    for t, s, out in zip(tokens, sums, outs):
-        out[...] = s[...] + product(t, [piece], [offset])
-
-
-def late_keys(tokens, sums, width, piece, offset):
-    rows, columns = sums[0].shape
-    return pl.pallas_call(
-        functools.partial(late_body, offset),
-        grid=(1,),
-        in_specs=[last_block(t, width) for t in tokens] + [whole(a) for a in (*sums, piece)],
-        out_specs=[whole(s) for s in sums],
-        out_shape=[jax.ShapeDtypeStruct((rows, columns), jnp.float32)] * PLANE,
-        cost_estimate=cost(0),
-        compiler_params=SMALL,
-        name="late_keys",
-    )(*tokens, *sums, piece)
-
-
 def over_core_body(keep_y, back, to_y):
     to_y[...] = (keep_y[...] + back[...]).astype(to_y.dtype)
 
@@ -327,22 +333,26 @@
     )(keep_y, back)
 
 
-def over_y_body(keep, back, there, keys):
-    keys[...] = (keep[...] + back[...] + there[...].astype(jnp.float32)).astype(keys.dtype)
-
-
-def over_y(keep, back, there):
-    rows, width = keep.shape
+def over_y_body(*refs):
+    keys, start = refs[-1], 0
+    for keep, back, there in zip(refs[0:-1:3], refs[1:-1:3], refs[2:-1:3]):
+        part = slice(start, start + keep.shape[1])
+        keys[:, part] = (keep[...] + back[...] + there[...].astype(jnp.float32)).astype(keys.dtype)
+        start = part.stop
+
+
+def over_y(columns, *terms):
+    shape = (terms[0].shape[0], columns)
     return pl.pallas_call(
         over_y_body,
         grid=(1,),
-        in_specs=[whole(keep), whole(back), whole(there)],
-        out_specs=whole(keep),
-        out_shape=jax.ShapeDtypeStruct((rows, width), jnp.bfloat16),
+        in_specs=[whole(t) for t in terms],
+        out_specs=pl.BlockSpec(shape, lambda *_: (0, 0)),
+        out_shape=jax.ShapeDtypeStruct(shape, jnp.bfloat16),
         cost_estimate=cost(0),
         compiler_params=SMALL,
         name="over_y",
-    )(keep, back, there)
+    )(*terms)
 
 
 def shards(master, momentum, working, tokens, partners, mix_weights):
@@ -352,23 +362,24 @@
     place = lax.axis_index("fsdp").astype(jnp.int32)[None]
     scalars = (lax.axis_index("replica").astype(jnp.int32)[None], partners, mix_weights)
     master, momentum, working, tokens = master[0], momentum[0], working[0], tokens[0]
-    rows = master.shape[0]
-    first = rows * FIRST // 16
-    cuts = [(0, first), (first, rows - first)]
+    rows, columns = master.shape
+    first = columns * FIRST // 16
+    cuts = [(0, first), (first, columns - first)]
 
     deltas, bases = first_step(scalars, master, momentum, working, cuts)
-    received = []
-    for delta in deltas:
+    def exchange(delta):
         if groups == 2:
-            received.append([lax.ppermute(delta, "replica", [(0, 1), (1, 0)])])
-        else:
-            every = lax.all_gather(delta, "replica", axis=0)
-            received.append([every[g] for g in range(groups)])
-
-    for_y, for_both, for_core, own = arrange_tokens(after(place, *deltas), tokens, line, rows, [2, 3, 1, 0])
+            return [lax.ppermute(delta, "replica", [(0, 1), (1, 0)])]
+        every = lax.all_gather(delta, "replica", axis=0)
+        return [every[g] for g in range(groups)]
+
+    received = [exchange(deltas[0])]
+
+    for_y, for_both, for_core = arrange_tokens(after(place, *deltas), tokens, line, rows, [2, 3, 1])
     from_y = lax.ppermute(for_y, "fsdp", plane_pairs(size, 2))
-    at_core = lax.ppermute(for_both, "fsdp", plane_pairs(size, 1))
     from_core = lax.ppermute(for_core, "fsdp", plane_pairs(size, 1))
+
+    received.append([t for t in exchange(deltas[1])])
 
     fresh = []
     for base, there in zip(bases, received):
@@ -377,7 +388,7 @@
         z = place // PLANE
         own_first = jnp.where((z == 1) | (z == 2), 0, 1).astype(jnp.int32)
         far = [lax.ppermute(f, "fsdp", line_pairs(size, [3, 2, 1, 0])) for f in fresh]
-        ready = [after(fresh[0], at_core, from_core), fresh[1]]
+        ready = [after(fresh[0], from_core), fresh[1]]
         near = [lax.ppermute(f, "fsdp", line_pairs(size, [1, 0, 3, 2])) for f in ready]
         passed = [far[0], far[1]]
         last = [
@@ -389,17 +400,21 @@
         lines = [[k * PLANE + p for k in range(line)] for p in range(PLANE)]
         every = [lax.all_gather(f, "fsdp", axis=0, axis_index_groups=lines) for f in fresh]
         blocks = [[e[k] for e in every] for k in range(line)]
-    from_both = lax.ppermute(after(at_core, from_y, from_core), "fsdp", plane_pairs(size, 2))
-    inputs = [own, from_core, from_y, from_both]
-
-    early = [piece for block in blocks[:-1] for piece in block]
-    offsets = [k * rows + start for k in range(line - 1) for start, _ in cuts]
-    sums = [early_keys(t, early, offsets) for t in inputs]
-    sums = add_keys(inputs, sums, rows, blocks[-1][0], cuts[0][0])
-    own, for_core, keep_y, for_both = late_keys(inputs, sums, rows, blocks[-1][1], cuts[1][0])
-    to_y = over_core(keep_y, lax.ppermute(for_both, "fsdp", plane_pairs(size, 1)))
-    back = lax.ppermute(for_core, "fsdp", plane_pairs(size, 1))
-    keys = over_y(own, back, lax.ppermute(to_y, "fsdp", plane_pairs(size, 2)))
+    from_both = lax.ppermute(after(for_both, from_y), "fsdp", plane_pairs(size, 3))
+    inputs = [tokens, from_core, from_y, from_both]
+
+    terms = []
+    for half, declared in enumerate((COST["add_keys"], 0)):
+        early = [[block[half]] for block in blocks[:-1]]
+        sums = [own_early_keys(place, line, tokens, early, rows, [0])]
+        sums += [early_keys(t, [e for [e] in early], [k * rows for k in range(line - 1)]) for t in inputs[1:]]
+        own, for_core, keep_y, for_both = late_keys(
+            place, line, inputs, sums, rows, blocks[-1][half], 0, declared
+        )
+        to_y = over_core(keep_y, lax.ppermute(for_both, "fsdp", plane_pairs(size, 1)))
+        back = lax.ppermute(for_core, "fsdp", plane_pairs(size, 1))
+        terms += [own, back, lax.ppermute(to_y, "fsdp", plane_pairs(size, 2))]
+    keys = over_y(columns, *terms)
 
     received = [after(r, to_y) for chunk in received for r in chunk]
     new_master, new_momentum = outer_step(scalars, groups, master, momentum, working, cuts, received)

time: 62.3 us -> 61.6 us (0.989)
  waiting for transfers between devices: 14.1 us -> 10.7 us
  starting transfers between devices: 33 us -> 35 us
    ppermute x2, starting transfers between devices: 15.3 us -> 18.6 us  [shards(): lax.ppermute(pick(own_first, f, g), 'fsdp', line_pairs(size, [2, 0, 3, 1]))]
    ppermute x1, waiting for transfers between devices: 6.93 us -> 5.34 us  [shards(): from_y = lax.ppermute(for_y, 'fsdp', plane_pairs(size, 2))]
    ppermute x5, starting transfers between devices: 7.12 us -> 5.7 us  [the longest x2 3.08 us: exchange(): return [lax.ppermute(delta, 'replica', [(0, 1), (1, 0)])]]
    ppermute x1 -> x2, waiting for transfers between devices: 1.21 us -> 0.01 us  [shards(): lax.ppermute(for_both, 'fsdp', plane_pairs(size, 1))]
    ppermute x2, waiting for transfers between devices: 0.81 us -> 0.01 us  [shards(): lax.ppermute(f, 'fsdp', line_pairs(size, [1, 0, 3, 2]))]
    pallas_call x3 -> x5, Pallas kernels: 1.49 us -> 2.16 us  [the longest x2 0.76 us: late_keys(): pl.pallas_call(functools.partial(late_body, offset), grid_spec=pltpu.Pref...]
    pallas_call x4 -> x6, Pallas kernels: 1.88 us -> 1.93 us  [early_keys(): pl.pallas_call(functools.partial(early_body, offsets), grid=(1,), in_spec...]
  transfers between devices with their start and end apart: 15 -> 17, of which waited for: 6 -> 5; matrix products, arithmetic and copies ran while one was open for 0% -> 0% of each run, Pallas kernels for 15% -> 17%
where the time goes in v5:
time: 61.6 us; the launch traced here: 61.4 us
  starting transfers between devices  35 us (57%)
  Pallas kernels  14.8 us (24%)
  waiting for transfers between devices  10.7 us (17%)
  between operations  0.89 us (1%)
    ppermute x2, starting transfers between devices, shards(): lax.ppermute(pick(own_first, f, g), 'fsdp', line_pairs(size, [2, 0, 3, 1]))  18.6 us
    ppermute x2, starting transfers between devices, shards(): lax.ppermute(f, 'fsdp', line_pairs(size, [3, 2, 1, 0]))  7.94 us
    ppermute x1, waiting for transfers between devices, shards(): from_y = lax.ppermute(for_y, 'fsdp', plane_pairs(size, 2))  5.34 us
    pallas_call x1, Pallas kernels, first_step(): pl.pallas_call(functools.partial(first_body, [start for start, _ in cuts]...  3.75 us
    ppermute x2, starting transfers between devices, exchange(): return [lax.ppermute(delta, 'replica', [(0, 1), (1, 0)])]  3.08 us
    pallas_call x1, Pallas kernels, arrange_tokens(): pl.pallas_call(functools.partial(arrange_body, width, distances), grid=(1...  2.77 us
    ppermute x2, starting transfers between devices, shards(): terms += [own, back, lax.ppermute(to_y, 'fsdp', plane_pairs(size, 2))]  2.62 us
    pallas_call x1, Pallas kernels, outer_step(): pl.pallas_call(functools.partial(outer_step_body, groups, [start for star...  2.58 us
  transfers between devices with their start and end apart: 17, of which 5 were waited for; matrix products, arithmetic and copies ran while one was open for 0% of the time, Pallas kernels for 17%

profile of v5, /device:TPU:0, one launch (start us, length us, event | category | flops | bytes accessed | tf_op | source)
XLA Modules:
  0.0 61.4 jit_solution(14817903640514355469)
XLA Ops:
  0.6 0.0 copy-start.4
  0.6 0.0 copy-start.5
  0.7 3.8 %first_step.1 = (bf16[512,256]{1,0:T(8,128)(2,1)}, bf16[512,256]{1,0:T(8,128)(2,1)}, f32[512,256]{1,0:T(8,128)}, f32[512,256]{1,0:T(8,128)}) custom-call(s32[1]{0:T(128)} %bitcast.own_group, s32[2,4]{1,0:T(2,128)} %partners.7, s32[2,5]{1,0:T(2,128)} %mix_weights.7, f32[512,512]{1,0:T(8,128)} %bitcast.18, f32[512,512]{1,0:T(8,128)} %bitcast.20, ...), custom_call_target="tpu_custom_call" | custom-call | tf_op jit(solution)/shard_map/first_step/pallas_call | solution.py:137
  4.4 0.0 copy-start.7
  4.4 3.0 %collective-permute-start = (bf16[512,256]{1,0:T(8,128)(2,1)}, bf16[512,256]{1,0:T(8,128)(2,1)S(1)}, u32[]{:S(2)}, u32[]{:S(2)}) collective-permute-start(bf16[512,256]{1,0:T(8,128)(2,1)} %get-tuple-element.26), channel_id=1, source_target_pairs={{0,16},{16,0},{1,17},{17,1},{2,18},{18,2},{3,19},{19,3},{4,20},{20... | collective-permute-start | bytes 786440 | tf_op jit(solution)/shard_map/ppermute | solution.py:372
  7.4 0.1 collective-permute-start.4
  7.5 2.8 %arrange_tokens.1 = (bf16[192,2048]{1,0:T(8,128)(2,1)}, bf16[192,2048]{1,0:T(8,128)(2,1)}, bf16[192,2048]{1,0:T(8,128)(2,1)}) custom-call(s32[1]{0:T(128)} %bitcast.4.place, bf16[192,8192]{1,0:T(8,128)(2,1)} %bitcast.9), custom_call_target="tpu_custom_call" | custom-call | tf_op jit(solution)/shard_map/arrange_tokens/pallas_call | solution.py:74
  10.3 2.0 %collective-permute-start.2 = (bf16[192,2048]{1,0:T(8,128)(2,1)}, bf16[192,2048]{1,0:T(8,128)(2,1)S(1)}, u32[]{:S(2)}, u32[]{:S(2)}) collective-permute-start(bf16[192,2048]{1,0:T(8,128)(2,1)} %get-tuple-element.30), channel_id=1, source_target_pairs={{0,2},{1,3},{2,0},{3,1},{4,6},{5,7},{6,4},{7,5},{8,10},{9,11},{10,... | collective-permute-start | bytes 2359304 | tf_op jit(solution)/shard_map/ppermute | solution.py:379
  12.3 0.0 collective-permute-start.1
  12.3 2.4 %collective-permute-done.refs_0_ = bf16[512,256]{1,0:T(8,128)(2,1)S(1)} collective-permute-done((bf16[512,256]{1,0:T(8,128)(2,1)}, bf16[512,256]{1,0:T(8,128)(2,1)S(1)}, u32[]{:S(2)}, u32[]{:S(2)}) %collective-permute-start) | collective-permute-done | bytes 262176 | tf_op jit(solution)/shard_map/ppermute | solution.py:372
  14.8 0.0 copy-done.4
  14.8 0.0 copy-done.5
  14.8 0.0 copy-done.7
  14.8 0.0 copy-start.6
  14.8 0.7 %next_working.2.refs_3_.refs_1_.own = bf16[512,256]{1,0:T(8,128)(2,1)S(1)} custom-call(s32[1]{0:T(128)} %bitcast.own_group, s32[2,4]{1,0:T(2,128)S(1)} %copy-done.4, s32[2,5]{1,0:T(2,128)S(1)} %copy-done.5, f32[512,256]{1,0:T(8,128)S(1)} %copy-done.7, bf16[512,256]{1,0:T(8,128)(2,1)S(1)} %collective-permute-done.refs_0_), custom_call_target="tpu_custom_call" | custom-call | flops 4611999744 | tf_op jit(solution)/shard_map/next_working/pallas_call | solution.py:160
  15.5 4.2 %collective-permute-start.10 = (bf16[512,256]{1,0:T(8,128)(2,1)S(1)}, bf16[512,256]{1,0:T(8,128)(2,1)S(1)}, u32[]{:S(2)}, u32[]{:S(2)}) collective-permute-start(bf16[512,256]{1,0:T(8,128)(2,1)S(1)} %next_working.2.refs_3_.refs_1_.own), channel_id=1, source_target_pairs={{0,12},{1,13},{2,14},{3,15},{4,8},{5,9},{6,10},{7,11},{8,4},{9,5},... | collective-permute-start | bytes 786440 | tf_op jit(solution)/shard_map/ppermute | solution.py:390
  19.8 0.0 collective-permute-done.4.refs_0_.refs_1_
  19.8 0.0 copy-done.6
  19.8 0.7 %next_working.3.refs_3_.refs_1_.own = bf16[512,256]{1,0:T(8,128)(2,1)S(1)} custom-call(s32[1]{0:T(128)} %bitcast.own_group, s32[2,4]{1,0:T(2,128)S(1)} %copy-done.4, s32[2,5]{1,0:T(2,128)S(1)} %copy-done.5, f32[512,256]{1,0:T(8,128)S(1)} %copy-done.6, bf16[512,256]{1,0:T(8,128)(2,1)S(1)} %collective-permute-done.4.refs_0_.refs_1_), custom_call_target="tpu_custom_call" | custom-call | flops 4611999744 | tf_op jit(solution)/shard_map/next_working/pallas_call | solution.py:160
  20.5 3.7 %collective-permute-start.6 = (bf16[512,256]{1,0:T(8,128)(2,1)S(1)}, bf16[512,256]{1,0:T(8,128)(2,1)S(1)}, u32[]{:S(2)}, u32[]{:S(2)}) collective-permute-start(bf16[512,256]{1,0:T(8,128)(2,1)S(1)} %next_working.3.refs_3_.refs_1_.own), channel_id=1, source_target_pairs={{0,12},{1,13},{2,14},{3,15},{4,8},{5,9},{6,10},{7,11},{8,4},{9,5},... | collective-permute-start | bytes 786440 | tf_op jit(solution)/shard_map/ppermute | solution.py:390
  24.2 0.0 collective-permute-start.5
  24.2 5.3 %collective-permute-done.2.refs_0_.refs_2_ = bf16[192,2048]{1,0:T(8,128)(2,1)S(1)} collective-permute-done((bf16[192,2048]{1,0:T(8,128)(2,1)}, bf16[192,2048]{1,0:T(8,128)(2,1)S(1)}, u32[]{:S(2)}, u32[]{:S(2)}) %collective-permute-start.2) | collective-permute-done | bytes 786464 | tf_op jit(solution)/shard_map/ppermute | solution.py:379
  29.6 0.0 copy-done.8
  29.6 0.0 collective-permute-start.3
  29.6 0.0 collective-permute-done.10.refs_5_.refs_3_.passed
  29.6 0.0 copy-start
  29.6 9.0 %collective-permute-start.11 = (bf16[512,256]{1,0:T(8,128)(2,1)S(1)}, bf16[512,256]{1,0:T(8,128)(2,1)S(1)}, u32[]{:S(2)}, u32[]{:S(2)}) collective-permute-start(bf16[512,256]{1,0:T(8,128)(2,1)S(1)} %pick.3), channel_id=1, source_target_pairs={{0,8},{1,9},{2,10},{3,11},{4,0},{5,1},{6,2},{7,3},{8,12},{9,13},{1... | collective-permute-start | bytes 786440 | tf_op jit(solution)/shard_map/ppermute | solution.py:395
  38.7 0.0 collective-permute-done.1.refs_0_.refs_1_
  38.7 0.0 collective-permute-start.9
  38.7 0.0 collective-permute-done.6.refs_5_.refs_3_.passed
  38.7 9.6 %collective-permute-start.7 = (bf16[512,256]{1,0:T(8,128)(2,1)S(1)}, bf16[512,256]{1,0:T(8,128)(2,1)S(1)}, u32[]{:S(2)}, u32[]{:S(2)}) collective-permute-start(bf16[512,256]{1,0:T(8,128)(2,1)S(1)} %pick.2), channel_id=1, source_target_pairs={{0,8},{1,9},{2,10},{3,11},{4,0},{5,1},{6,2},{7,3},{8,12},{9,13},{1... | collective-permute-start | bytes 786440 | tf_op jit(solution)/shard_map/ppermute | solution.py:395
  48.3 0.0 collective-permute-done.5.refs_4_.refs_2_
  48.3 0.3 own_early_keys.2.refs_4_
  48.6 0.3 early_keys.7.refs_6_
  49.0 0.3 early_keys.6.refs_5_
  49.3 0.0 collective-permute-done.9.refs_4_.refs_2_
  49.3 0.3 early_keys.10.refs_6_
  49.6 0.3 early_keys.9.refs_5_
  50.0 0.3 own_early_keys.3.refs_4_
  50.3 0.0 collective-permute-done.3.refs_0_.refs_3_
  50.3 0.3 early_keys.11.refs_7_
  50.6 0.0 collective-permute-done.11.refs_8_
  50.6 0.4 late_keys.3
  51.0 0.1 collective-permute-start.13
  51.1 0.3 early_keys.8.refs_7_
  51.4 0.0 copy-start.1
  51.4 0.0 copy-start.2
  51.5 0.0 copy-start.3
  51.5 0.8 %collective-permute-done.7.refs_8_ = bf16[512,256]{1,0:T(8,128)(2,1)S(1)} collective-permute-done((bf16[512,256]{1,0:T(8,128)(2,1)S(1)}, bf16[512,256]{1,0:T(8,128)(2,1)S(1)}, u32[]{:S(2)}, u32[]{:S(2)}) %collective-permute-start.7) | collective-permute-done | bytes 262176 | tf_op jit(solution)/shard_map/ppermute | solution.py:395
  52.3 0.4 late_keys.2
  52.6 0.1 collective-permute-start.8
  52.7 0.5 collective-permute-start.12
  53.2 0.1 collective-permute-start.15
  53.3 0.0 collective-permute-done.13.back
  53.3 1.8 %collective-permute-start.14 = (bf16[192,256]{1,0:T(8,128)(2,1)S(1)}, bf16[192,256]{1,0:T(8,128)(2,1)S(1)}, u32[]{:S(2)}, u32[]{:S(2)}) collective-permute-start(bf16[192,256]{1,0:T(8,128)(2,1)S(1)} %over_core.3), channel_id=1, source_target_pairs={{0,2},{1,3},{2,0},{3,1},{4,6},{5,7},{6,4},{7,5},{8,10},{9,11},{10,... | collective-permute-start | bytes 294920 | tf_op jit(solution)/shard_map/ppermute | solution.py:416
  55.1 0.0 collective-permute-done.8.back
  55.2 0.8 %collective-permute-start.16 = (bf16[192,256]{1,0:T(8,128)(2,1)S(1)}, bf16[192,256]{1,0:T(8,128)(2,1)S(1)}, u32[]{:S(2)}, u32[]{:S(2)}) collective-permute-start(bf16[192,256]{1,0:T(8,128)(2,1)S(1)} %over_core.2), channel_id=1, source_target_pairs={{0,2},{1,3},{2,0},{3,1},{4,6},{5,7},{6,4},{7,5},{8,10},{9,11},{10,... | collective-permute-start | bytes 294920 | tf_op jit(solution)/shard_map/ppermute | solution.py:416
  56.0 0.0 copy-done.2
  56.0 2.6 %outer_step.1 = (f32[512,512]{1,0:T(8,128)}, f32[512,512]{1,0:T(8,128)}) custom-call(s32[1]{0:T(128)} %bitcast.own_group, s32[2,4]{1,0:T(2,128)S(1)} %copy-done.4, s32[2,5]{1,0:T(2,128)S(1)} %copy-done.5, f32[512,512]{1,0:T(8,128)S(1)} %bitcast.19, f32[512,512]{1,0:T(8,128)S(1)} %bitcast.21, bf16[512,512]{1,0:T(8,128)(2,1)S(1)} %bitcast.23, ...), custom_call_target="tpu_custom_call" | custom-call | tf_op jit(solution)/shard_map/outer_step/pallas_call | solution.py:189
  58.6 0.0 collective-permute-done.12.refs_1_
  58.6 0.0 collective-permute-done.15.refs_4_
  58.6 0.4 collective-permute-done.14.refs_2_
  59.0 1.7 %collective-permute-done.16.refs_5_ = bf16[192,256]{1,0:T(8,128)(2,1)S(1)} collective-permute-done((bf16[192,256]{1,0:T(8,128)(2,1)S(1)}, bf16[192,256]{1,0:T(8,128)(2,1)S(1)}, u32[]{:S(2)}, u32[]{:S(2)}) %collective-permute-start.16) | collective-permute-done | bytes 98336 | tf_op jit(solution)/shard_map/ppermute | solution.py:416
  60.6 0.8 %over_y.1 = bf16[192,512]{1,0:T(8,128)(2,1)} custom-call(f32[192,256]{1,0:T(8,128)S(1)} %get-tuple-element.43.refs_0_, f32[192,256]{1,0:T(8,128)S(1)} %collective-permute-done.12.refs_1_, bf16[192,256]{1,0:T(8,128)(2,1)S(1)} %collective-permute-done.14.refs_2_, f32[192,256]{1,0:T(8,128)S(1)} %get-tuple-element.47.refs_3_, ...), custom_call_target="tpu_custom_call" | custom-call | tf_op jit(solution)/shard_map/over_y/pallas_call | solution.py:346
  (8 shorter events, 0.1 us)
Async XLA Ops:
  0.6 14.1 %copy-start.4 = (s32[2,4]{1,0:T(2,128)S(1)}, s32[2,4]{1,0:T(2,128)}, u32[]{:S(2)}) copy-start(s32[2,4]{1,0:T(2,128)} %partners.7) | copy-start | bytes 100
  0.6 14.1 %copy-start.5 = (s32[2,5]{1,0:T(2,128)S(1)}, s32[2,5]{1,0:T(2,128)}, u32[]{:S(2)}) copy-start(s32[2,5]{1,0:T(2,128)} %mix_weights.7) | copy-start | bytes 124
  4.4 10.4 %copy-start.7 = (f32[512,256]{1,0:T(8,128)S(1)}, f32[512,256]{1,0:T(8,128)}, u32[]{:S(2)}) copy-start(f32[512,256]{1,0:T(8,128)} %get-tuple-element.34.base) | copy-start | bytes 1572868
  4.4 10.3 %collective-permute-start = (bf16[512,256]{1,0:T(8,128)(2,1)}, bf16[512,256]{1,0:T(8,128)(2,1)S(1)}, u32[]{:S(2)}, u32[]{:S(2)}) collective-permute-start(bf16[512,256]{1,0:T(8,128)(2,1)} %get-tuple-element.26), channel_id=1, source_target_pairs={{0,16},{16,0},{1,17},{17,1},{2,18},{18,2},{3,19},{19,3},{4,20},{20... | collective-permute-start | bytes 786440 | tf_op jit(solution)/shard_map/ppermute | solution.py:372
  7.4 12.3 %collective-permute-start.4 = (bf16[512,256]{1,0:T(8,128)(2,1)}, bf16[512,256]{1,0:T(8,128)(2,1)S(1)}, u32[]{:S(2)}, u32[]{:S(2)}) collective-permute-start(bf16[512,256]{1,0:T(8,128)(2,1)} %get-tuple-element.27), channel_id=1, source_target_pairs={{0,16},{16,0},{1,17},{17,1},{2,18},{18,2},{3,19},{19,3},{4,20},{20... | collective-permute-start | bytes 786440 | tf_op jit(solution)/shard_map/ppermute | solution.py:372
  10.3 19.3 %collective-permute-start.2 = (bf16[192,2048]{1,0:T(8,128)(2,1)}, bf16[192,2048]{1,0:T(8,128)(2,1)S(1)}, u32[]{:S(2)}, u32[]{:S(2)}) collective-permute-start(bf16[192,2048]{1,0:T(8,128)(2,1)} %get-tuple-element.30), channel_id=1, source_target_pairs={{0,2},{1,3},{2,0},{3,1},{4,6},{5,7},{6,4},{7,5},{8,10},{9,11},{10,... | collective-permute-start | bytes 2359304 | tf_op jit(solution)/shard_map/ppermute | solution.py:379
  12.3 26.3 %collective-permute-start.1 = (bf16[192,2048]{1,0:T(8,128)(2,1)}, bf16[192,2048]{1,0:T(8,128)(2,1)S(1)}, u32[]{:S(2)}, u32[]{:S(2)}) collective-permute-start(bf16[192,2048]{1,0:T(8,128)(2,1)} %get-tuple-element.29), channel_id=1, source_target_pairs={{0,1},{1,0},{2,3},{3,2},{4,5},{5,4},{6,7},{7,6},{8,9},{9,8},{10,11... | collective-permute-start | bytes 2359304 | tf_op jit(solution)/shard_map/ppermute | solution.py:380
  14.8 5.0 %copy-start.6 = (f32[512,256]{1,0:T(8,128)S(1)}, f32[512,256]{1,0:T(8,128)}, u32[]{:S(2)}) copy-start(f32[512,256]{1,0:T(8,128)} %get-tuple-element.33.base) | copy-start | bytes 1572868
  15.5 14.0 %collective-permute-start.10 = (bf16[512,256]{1,0:T(8,128)(2,1)S(1)}, bf16[512,256]{1,0:T(8,128)(2,1)S(1)}, u32[]{:S(2)}, u32[]{:S(2)}) collective-permute-start(bf16[512,256]{1,0:T(8,128)(2,1)S(1)} %next_working.2.refs_3_.refs_1_.own), channel_id=1, source_target_pairs={{0,12},{1,13},{2,14},{3,15},{4,8},{5,9},{6,10},{7,11},{8,4},{9,5},... | collective-permute-start | bytes 786440 | tf_op jit(solution)/shard_map/ppermute | solution.py:390
  19.8 9.8 %copy-start.8 = (bf16[192,2048]{1,0:T(8,128)(2,1)S(1)}, bf16[192,2048]{1,0:T(8,128)(2,1)}, u32[]{:S(2)}) copy-start(bf16[192,2048]{1,0:T(8,128)(2,1)} %get-tuple-element.32) | copy-start | bytes 2359300
  20.5 18.1 %collective-permute-start.6 = (bf16[512,256]{1,0:T(8,128)(2,1)S(1)}, bf16[512,256]{1,0:T(8,128)(2,1)S(1)}, u32[]{:S(2)}, u32[]{:S(2)}) collective-permute-start(bf16[512,256]{1,0:T(8,128)(2,1)S(1)} %next_working.3.refs_3_.refs_1_.own), channel_id=1, source_target_pairs={{0,12},{1,13},{2,14},{3,15},{4,8},{5,9},{6,10},{7,11},{8,4},{9,5},... | collective-permute-start | bytes 786440 | tf_op jit(solution)/shard_map/ppermute | solution.py:390
  24.2 24.1 %collective-permute-start.5 = (bf16[512,256]{1,0:T(8,128)(2,1)S(1)}, bf16[512,256]{1,0:T(8,128)(2,1)S(1)}, u32[]{:S(2)}, u32[]{:S(2)}) collective-permute-start(bf16[512,256]{1,0:T(8,128)(2,1)S(1)} %next_working.3.refs_3_.refs_1_.own), channel_id=1, source_target_pairs={{0,4},{1,5},{2,6},{3,7},{4,0},{5,1},{6,2},{7,3},{8,12},{9,13},{10,... | collective-permute-start | bytes 786440 | tf_op jit(solution)/shard_map/ppermute | solution.py:392
  29.6 20.7 %collective-permute-start.3 = (bf16[192,2048]{1,0:T(8,128)(2,1)S(1)}, bf16[192,2048]{1,0:T(8,128)(2,1)S(1)}, u32[]{:S(2)}, u32[]{:S(2)}) collective-permute-start(bf16[192,2048]{1,0:T(8,128)(2,1)S(1)} %copy-done.8), channel_id=1, source_target_pairs={{0,3},{1,2},{2,1},{3,0},{4,7},{5,6},{6,5},{7,4},{8,11},{9,10},{10,... | collective-permute-start | bytes 2359304 | tf_op jit(solution)/shard_map/ppermute | solution.py:403
  29.6 18.7 %copy-start = (bf16[1,192,8192]{2,1,0:T(8,128)(2,1)S(1)}, bf16[1,192,8192]{2,1,0:T(8,128)(2,1)}, u32[]{:S(2)}) copy-start(bf16[1,192,8192]{2,1,0:T(8,128)(2,1)} %param.9) | copy-start | bytes 9437188
  29.6 21.0 %collective-permute-start.11 = (bf16[512,256]{1,0:T(8,128)(2,1)S(1)}, bf16[512,256]{1,0:T(8,128)(2,1)S(1)}, u32[]{:S(2)}, u32[]{:S(2)}) collective-permute-start(bf16[512,256]{1,0:T(8,128)(2,1)S(1)} %pick.3), channel_id=1, source_target_pairs={{0,8},{1,9},{2,10},{3,11},{4,0},{5,1},{6,2},{7,3},{8,12},{9,13},{1... | collective-permute-start | bytes 786440 | tf_op jit(solution)/shard_map/ppermute | solution.py:395
  38.7 10.6 %collective-permute-start.9 = (bf16[512,256]{1,0:T(8,128)(2,1)S(1)}, bf16[512,256]{1,0:T(8,128)(2,1)S(1)}, u32[]{:S(2)}, u32[]{:S(2)}) collective-permute-start(bf16[512,256]{1,0:T(8,128)(2,1)S(1)} %next_working.2.refs_3_.refs_1_.own), channel_id=1, source_target_pairs={{0,4},{1,5},{2,6},{3,7},{4,0},{5,1},{6,2},{7,3},{8,12},{9,13},{10,... | collective-permute-start | bytes 786440 | tf_op jit(solution)/shard_map/ppermute | solution.py:392
  38.7 13.6 %collective-permute-start.7 = (bf16[512,256]{1,0:T(8,128)(2,1)S(1)}, bf16[512,256]{1,0:T(8,128)(2,1)S(1)}, u32[]{:S(2)}, u32[]{:S(2)}) collective-permute-start(bf16[512,256]{1,0:T(8,128)(2,1)S(1)} %pick.2), channel_id=1, source_target_pairs={{0,8},{1,9},{2,10},{3,11},{4,0},{5,1},{6,2},{7,3},{8,12},{9,13},{1... | collective-permute-start | bytes 786440 | tf_op jit(solution)/shard_map/ppermute | solution.py:395
  51.0 2.3 %collective-permute-start.13 = (f32[192,256]{1,0:T(8,128)S(1)}, f32[192,256]{1,0:T(8,128)S(1)}, u32[]{:S(2)}, u32[]{:S(2)}) collective-permute-start(f32[192,256]{1,0:T(8,128)S(1)} %get-tuple-element.46), channel_id=1, source_target_pairs={{0,1},{1,0},{2,3},{3,2},{4,5},{5,4},{6,7},{7,6},{8,9},{9,8},{10,11... | collective-permute-start | bytes 589832 | tf_op jit(solution)/shard_map/ppermute | solution.py:414
  51.4 4.6 %copy-start.1 = (f32[1,512,512]{2,1,0:T(8,128)S(1)}, f32[1,512,512]{2,1,0:T(8,128)}, u32[]{:S(2)}) copy-start(f32[1,512,512]{2,1,0:T(8,128)} %param.6) | copy-start | bytes 3145732
  51.4 4.5 %copy-start.2 = (f32[1,512,512]{2,1,0:T(8,128)S(1)}, f32[1,512,512]{2,1,0:T(8,128)}, u32[]{:S(2)}) copy-start(f32[1,512,512]{2,1,0:T(8,128)} %param.7) | copy-start | bytes 3145732
  51.5 4.5 %copy-start.3 = (bf16[1,512,512]{2,1,0:T(8,128)(2,1)S(1)}, bf16[1,512,512]{2,1,0:T(8,128)(2,1)}, u32[]{:S(2)}) copy-start(bf16[1,512,512]{2,1,0:T(8,128)(2,1)} %param.8) | copy-start | bytes 1572868
  52.6 2.5 %collective-permute-start.8 = (f32[192,256]{1,0:T(8,128)S(1)}, f32[192,256]{1,0:T(8,128)S(1)}, u32[]{:S(2)}, u32[]{:S(2)}) collective-permute-start(f32[192,256]{1,0:T(8,128)S(1)} %get-tuple-element.37), channel_id=1, source_target_pairs={{0,1},{1,0},{2,3},{3,2},{4,5},{5,4},{6,7},{7,6},{8,9},{9,8},{10,11... | collective-permute-start | bytes 589832 | tf_op jit(solution)/shard_map/ppermute | solution.py:414
  52.7 5.8 %collective-permute-start.12 = (f32[192,256]{1,0:T(8,128)S(1)}, f32[192,256]{1,0:T(8,128)S(1)}, u32[]{:S(2)}, u32[]{:S(2)}) collective-permute-start(f32[192,256]{1,0:T(8,128)S(1)} %get-tuple-element.44), channel_id=1, source_target_pairs={{0,1},{1,0},{2,3},{3,2},{4,5},{5,4},{6,7},{7,6},{8,9},{9,8},{10,11... | collective-permute-start | bytes 589832 | tf_op jit(solution)/shard_map/ppermute | solution.py:415
  53.2 5.3 %collective-permute-start.15 = (f32[192,256]{1,0:T(8,128)S(1)}, f32[192,256]{1,0:T(8,128)S(1)}, u32[]{:S(2)}, u32[]{:S(2)}) collective-permute-start(f32[192,256]{1,0:T(8,128)S(1)} %get-tuple-element.48), channel_id=1, source_target_pairs={{0,1},{1,0},{2,3},{3,2},{4,5},{5,4},{6,7},{7,6},{8,9},{9,8},{10,11... | collective-permute-start | bytes 589832 | tf_op jit(solution)/shard_map/ppermute | solution.py:415
  53.3 5.7 %collective-permute-start.14 = (bf16[192,256]{1,0:T(8,128)(2,1)S(1)}, bf16[192,256]{1,0:T(8,128)(2,1)S(1)}, u32[]{:S(2)}, u32[]{:S(2)}) collective-permute-start(bf16[192,256]{1,0:T(8,128)(2,1)S(1)} %over_core.3), channel_id=1, source_target_pairs={{0,2},{1,3},{2,0},{3,1},{4,6},{5,7},{6,4},{7,5},{8,10},{9,11},{10,... | collective-permute-start | bytes 294920 | tf_op jit(solution)/shard_map/ppermute | solution.py:416
  55.2 5.5 %collective-permute-start.16 = (bf16[192,256]{1,0:T(8,128)(2,1)S(1)}, bf16[192,256]{1,0:T(8,128)(2,1)S(1)}, u32[]{:S(2)}, u32[]{:S(2)}) collective-permute-start(bf16[192,256]{1,0:T(8,128)(2,1)S(1)} %over_core.2), channel_id=1, source_target_pairs={{0,2},{1,3},{2,0},{3,1},{4,6},{5,7},{6,4},{7,5},{8,10},{9,11},{10,... | collective-permute-start | bytes 294920 | tf_op jit(solution)/shard_map/ppermute | solution.py:416
